TPU v7x, 32 devices: a whole 2x2x4 slice. The times are simulated.
32 devices in a mesh: ctx: 8 (over z, y), fsdp: 4 (over x, core).
Axes of the slice: x: 2, y: 2, z: 4, core: 2. Of those that a mesh axis runs over, the one named last changes fastest.
Arguments:
- tokens: bfloat16 [4, 1024, 768], P('fsdp', 'ctx'), may hold values from -6 to 6
- memory: bfloat16 [4, 5120, 768], P('fsdp', 'ctx'), may hold values from -6 to 6
- piece_order: int32 [16], replicated, may hold values from 0 to 15, as said below
- bucket_table: int32 [2047], replicated, may hold values from 0 to 31, as said below
- passage_lengths: int32 [4, 20], P('fsdp'), may hold values from 32 to 256, as said below
- self_gain: bfloat16 [768], P('fsdp'), may hold values from 0.5 to 1.5
- cross_gain: bfloat16 [768], P('fsdp'), may hold values from 0.5 to 1.5
- hidden_gain: bfloat16 [768], P('fsdp'), may hold values from 0.5 to 1.5
- position_bias: bfloat16 [32, 12], P('fsdp'), may hold values from -3 to 3
- self_query: bfloat16 [768, 768], P('fsdp'), may hold values from -0.09375 to 0.09375
- self_attention_key: bfloat16 [768, 768], P('fsdp'), may hold values from -0.09375 to 0.09375
- self_value: bfloat16 [768, 768], P('fsdp'), may hold values from -0.21875 to 0.21875
- self_output: bfloat16 [768, 768], P('fsdp'), may hold values from -2 to 2
- cross_query: bfloat16 [768, 768], P('fsdp'), may hold values from -0.09375 to 0.09375
- cross_key: bfloat16 [768, 768], P('fsdp'), may hold values from -0.09375 to 0.09375
- cross_value: bfloat16 [768, 768], P('fsdp'), may hold values from -0.21875 to 0.21875
- cross_output: bfloat16 [768, 768], P('fsdp'), may hold values from -2 to 2
- hidden_in: bfloat16 [768, 3072], P('fsdp'), may hold values from -0.21875 to 0.21875
- hidden_out: bfloat16 [3072, 768], P('fsdp'), may hold values from -0.15625 to 0.15625
- grad_output: bfloat16 [4, 1024, 768], P('fsdp', 'ctx'), may hold values from -6 to 6
Outputs:
- layer_output: bfloat16 [4, 1024, 768], P('fsdp', 'ctx')
- grad_tokens: bfloat16 [4, 1024, 768], P('fsdp', 'ctx')
- grad_memory: bfloat16 [4, 5120, 768], P('fsdp', 'ctx')
- grad_self_gain: float32 [768], P('fsdp')
- grad_cross_gain: float32 [768], P('fsdp')
- grad_hidden_gain: float32 [768], P('fsdp')
- grad_position_bias: float32 [32, 12], P('fsdp')
- grad_self_query: float32 [768, 768], P('fsdp')
- grad_self_key: float32 [768, 768], P('fsdp')
- grad_self_value: float32 [768, 768], P('fsdp')
- grad_self_output: float32 [768, 768], P('fsdp')
- grad_cross_query: float32 [768, 768], P('fsdp')
- grad_cross_key: float32 [768, 768], P('fsdp')
- grad_cross_value: float32 [768, 768], P('fsdp')
- grad_cross_output: float32 [768, 768], P('fsdp')
- grad_hidden_in: float32 [768, 3072], P('fsdp')
- grad_hidden_out: float32 [3072, 768], P('fsdp')
Inputs may be any that keep to these rules, and one draw needn't show every extreme that they name: `piece_order`: slots 2i and 2i + 1 hold two pieces whose numbers add up to 15; every piece appears once. `bucket_table`: entry 1023 + r is the bucket of r = key place minus query place; buckets below 16 serve r <= 0, the others r > 0, and on either side the bucket never falls as the distance grows. `passage_lengths`: in every sequence one passage fills all 256 slots.
All inputs are finite; a program needn't handle non-finite values.
Results may differ from a plain program's by a relative error of at most 0.03.
Values may be sent and summed in bfloat16 or wider, within the bound.
A program may use at most 320 MiB of HBM per device.

v0:
```python
import jax
import jax.numpy as jnp
from jax import lax
from jax.sharding import PartitionSpec as P

D = 768
HEADS = 12
HEAD_DIM = 64
BUCKETS = 32
PIECE = 64
BLOCK = 256
KBLK = 512
PSG = 20
PLEN = 256


EPSILON = 1e-06
NEGATIVE = -1e30


def norm_scale(values, gain_vector):
    return (
        values
        * lax.rsqrt(jnp.mean(values * values, axis=-1, keepdims=True) + EPSILON)
        * gain_vector
    )


def smooth_gate(values):
    return jax.nn.gelu(values, approximate=True)


def project(operand, matrix):
    return jnp.dot(operand, matrix, preferred_element_type=jnp.float32)


def project_back(operand, matrix):
    return jnp.einsum("sra,ba->srb", operand, matrix, preferred_element_type=jnp.float32)


def weight_grad(inputs, upstream):
    return jnp.einsum("sra,srb->ab", inputs, upstream, preferred_element_type=jnp.float32)


def to_heads(matrix):
    return matrix.reshape(matrix.shape[0], matrix.shape[1], HEADS, HEAD_DIM)


def heads_first(matrix):
    return jnp.transpose(to_heads(matrix), (0, 2, 1, 3))


def from_heads(tensor):
    return jnp.transpose(tensor, (0, 2, 1, 3)).reshape(
        tensor.shape[0], tensor.shape[2], HEADS * HEAD_DIM
    )


def block_scores(queries, keys_all, values_all, extras, offset):
    key_block = lax.dynamic_slice_in_dim(keys_all, offset, KBLK, 1)
    value_block = lax.dynamic_slice_in_dim(values_all, offset, KBLK, 1)
    added_bias, visible, bucket_indicator = extras(offset)
    scores = (
        jnp.einsum("sqhd,skhd->shqk", queries, key_block, preferred_element_type=jnp.float32)
        + added_bias
    )
    block_maximum = jnp.max(jnp.where(visible, scores, NEGATIVE), axis=-1)
    weights = jnp.exp(jnp.where(visible, scores - block_maximum[..., None], NEGATIVE))
    return (key_block, value_block, bucket_indicator, block_maximum, weights)


def attend_forward(queries, keys_all, values_all, extras):
    block_count = keys_all.shape[1] // KBLK

    def single_block_tile(carried, block_index):
        key_block, value_block, bucket_indicator, block_maximum, weights = block_scores(
            queries, keys_all, values_all, extras, block_index * KBLK
        )
        numerator = jnp.einsum(
            "shqk,skhd->shqd",
            weights.astype(jnp.bfloat16),
            value_block,
            preferred_element_type=jnp.float32,
        )
        return (carried, (block_maximum, jnp.sum(weights, axis=-1), numerator))

    ignored, stacked = lax.scan(
        single_block_tile, jnp.zeros((), jnp.float32), jnp.arange(block_count, dtype=jnp.int32)
    )
    block_maximum, block_sum, numerator = stacked
    row_maximum = jnp.max(block_maximum, axis=0)
    rescale = jnp.exp(block_maximum - row_maximum)
    row_total = jnp.sum(rescale * block_sum, axis=0)
    output = jnp.sum(rescale[..., None] * numerator, axis=0) / row_total[..., None]
    return (output, row_maximum, row_total)


def attend_backward(
    queries, keys_all, values_all, extras, grad_out, output, row_maximum, row_total
):
    block_count = keys_all.shape[1] // KBLK
    grad_wide = grad_out.astype(jnp.float32)
    row_dot = jnp.sum(grad_wide * output, axis=-1)
    scaled = grad_wide / row_total[..., None]
    sum_weight = -row_dot / row_total
    initial = (
        jnp.zeros(queries.shape, jnp.float32),
        jnp.zeros(keys_all.shape, jnp.float32),
        jnp.zeros(values_all.shape, jnp.float32),
        jnp.zeros((BUCKETS, HEADS), jnp.float32),
    )

    def single_block_tile(carried, block_index):
        grad_query, grad_keys, grad_values, grad_bias = carried
        offset = block_index * KBLK
        key_block, value_block, bucket_indicator, block_maximum, weights = block_scores(
            queries, keys_all, values_all, extras, offset
        )
        rescale = jnp.exp(block_maximum - row_maximum)
        grad_numerator = (scaled * rescale[..., None]).astype(jnp.bfloat16)
        grad_weights = (
            jnp.einsum(
                "shqd,skhd->shqk", grad_numerator, value_block, preferred_element_type=jnp.float32
            )
            + (sum_weight * rescale)[..., None]
        )
        grad_scores = weights * grad_weights
        gradient_bfloat_cast = grad_scores.astype(jnp.bfloat16)
        grad_query = grad_query + jnp.einsum(
            "shqk,skhd->sqhd", gradient_bfloat_cast, key_block, preferred_element_type=jnp.float32
        )
        key_part = jnp.einsum(
            "shqk,sqhd->skhd", gradient_bfloat_cast, queries, preferred_element_type=jnp.float32
        )
        value_part = jnp.einsum(
            "shqk,shqd->skhd",
            weights.astype(jnp.bfloat16),
            grad_numerator,
            preferred_element_type=jnp.float32,
        )
        grad_keys = lax.dynamic_update_slice_in_dim(grad_keys, key_part, offset, 1)
        grad_values = lax.dynamic_update_slice_in_dim(grad_values, value_part, offset, 1)
        if bucket_indicator is not None:
            remainder_portion = (grad_scores - gradient_bfloat_cast.astype(jnp.float32)).astype(
                jnp.bfloat16
            )
            grad_bias = (
                grad_bias
                + jnp.einsum(
                    "uljf,pjf->pl",
                    gradient_bfloat_cast,
                    bucket_indicator,
                    preferred_element_type=jnp.float32,
                )
                + jnp.einsum(
                    "uljf,pjf->pl",
                    remainder_portion,
                    bucket_indicator,
                    preferred_element_type=jnp.float32,
                )
            )
        return ((grad_query, grad_keys, grad_values, grad_bias), None)

    result, ignored = lax.scan(single_block_tile, initial, jnp.arange(block_count, dtype=jnp.int32))
    return result


def shards(
    tokens,
    memory,
    piece_order,
    bucket_table,
    passage_lengths,
    self_gain,
    cross_gain,
    hidden_gain,
    position_bias,
    self_query,
    self_attention_key,
    self_value,
    self_output,
    cross_query,
    cross_key,
    cross_value,
    cross_output,
    hidden_in,
    hidden_out,
    grad_output,
):
    (
        gain_one,
        gain_two,
        gain_three,
        position_bias_lookup,
        query_full,
        key_full,
        value_full,
        output_full,
        cross_query_full,
        cross_key_full,
        cross_value_full,
        cross_output_full,
        inner_full,
        outer_full,
    ) = (
        lax.all_gather(self_gain, "fsdp", axis=0, tiled=True),
        lax.all_gather(cross_gain, "fsdp", axis=0, tiled=True),
        lax.all_gather(hidden_gain, "fsdp", axis=0, tiled=True),
        lax.all_gather(position_bias, "fsdp", axis=0, tiled=True),
        lax.all_gather(self_query, "fsdp", axis=0, tiled=True),
        lax.all_gather(self_attention_key, "fsdp", axis=0, tiled=True),
        lax.all_gather(self_value, "fsdp", axis=0, tiled=True),
        lax.all_gather(self_output, "fsdp", axis=0, tiled=True),
        lax.all_gather(cross_query, "fsdp", axis=0, tiled=True),
        lax.all_gather(cross_key, "fsdp", axis=0, tiled=True),
        lax.all_gather(cross_value, "fsdp", axis=0, tiled=True),
        lax.all_gather(cross_output, "fsdp", axis=0, tiled=True),
        lax.all_gather(hidden_in, "fsdp", axis=0, tiled=True),
        lax.all_gather(hidden_out, "fsdp", axis=0, tiled=True),
    )
    gain_one = gain_one.astype(jnp.float32)
    gain_two = gain_two.astype(jnp.float32)
    gain_three = gain_three.astype(jnp.float32)
    sequence_count = tokens.shape[0]
    local_rows = tokens.shape[1]
    sequence_length = (bucket_table.shape[0] + 1) // 2
    memory_length = PSG * PLEN
    piece_offsets = jnp.arange(PIECE, dtype=jnp.int32)
    local_pieces = lax.dynamic_slice_in_dim(
        piece_order, lax.axis_index("ctx") * (local_rows // PIECE), local_rows // PIECE
    )
    query_position = (local_pieces[:, None] * PIECE + piece_offsets[None, :]).reshape(local_rows)
    key_position = (piece_order[:, None] * PIECE + piece_offsets[None, :]).reshape(sequence_length)
    bucket_numbers = jnp.arange(BUCKETS, dtype=jnp.int32)

    def self_extras(offset):
        key_block_position = lax.dynamic_slice_in_dim(key_position, offset, KBLK)
        relative_bucket_index = jnp.take(
            bucket_table,
            key_block_position[None, :] - query_position[:, None] + sequence_length - 1,
        )
        bucket_indicator = (
            relative_bucket_index[None, :, :] == bucket_numbers[:, None, None]
        ).astype(jnp.bfloat16)
        added_bias = jnp.einsum(
            "lvj,lf->fvj",
            bucket_indicator,
            position_bias_lookup,
            preferred_element_type=jnp.float32,
        )
        visible = key_block_position[None, :] // BLOCK <= query_position[:, None] // BLOCK
        return (added_bias, visible, bucket_indicator)

    slot_numbers = jnp.arange(PLEN, dtype=jnp.int32)
    memory_valid = (passage_lengths[:, :, None] > slot_numbers[None, None, :]).reshape(
        sequence_count, memory_length
    )

    def cross_extras(offset):
        visible = lax.dynamic_slice_in_dim(memory_valid, offset, KBLK, 1)[:, None, None, :]
        return (0.0, visible, None)

    inputs_wide = tokens.astype(jnp.float32)
    normed_one = norm_scale(inputs_wide, gain_one).astype(jnp.bfloat16)
    queries_one = project(normed_one, query_full).astype(jnp.bfloat16)
    keys_local = project(normed_one, key_full).astype(jnp.bfloat16)
    values_local = project(normed_one, value_full).astype(jnp.bfloat16)
    memory_keys = project(memory, cross_key_full).astype(jnp.bfloat16)
    memory_values = project(memory, cross_value_full).astype(jnp.bfloat16)
    keys_all, values_all, memory_keys_all, memory_values_all = (
        lax.all_gather(keys_local, "ctx", axis=1, tiled=True),
        lax.all_gather(values_local, "ctx", axis=1, tiled=True),
        lax.all_gather(memory_keys, "ctx", axis=1, tiled=True),
        lax.all_gather(memory_values, "ctx", axis=1, tiled=True),
    )
    output_one, maximum_one, total_one = attend_forward(
        to_heads(queries_one), to_heads(keys_all), to_heads(values_all), self_extras
    )
    attended_one = from_heads(output_one).astype(jnp.bfloat16)
    hidden_one = inputs_wide + project(attended_one, output_full)
    normed_two = norm_scale(hidden_one, gain_two).astype(jnp.bfloat16)
    queries_two = project(normed_two, cross_query_full).astype(jnp.bfloat16)
    output_two, maximum_two, total_two = attend_forward(
        to_heads(queries_two), to_heads(memory_keys_all), to_heads(memory_values_all), cross_extras
    )
    attended_two = from_heads(output_two).astype(jnp.bfloat16)
    hidden_two = hidden_one + project(attended_two, cross_output_full)
    normed_three = norm_scale(hidden_two, gain_three).astype(jnp.bfloat16)
    before_gate = project(normed_three, inner_full)
    gated_wide, gate_pullback = jax.vjp(smooth_gate, before_gate)
    activated = gated_wide.astype(jnp.bfloat16)
    layer_output = (hidden_two + project(activated, outer_full)).astype(jnp.bfloat16)
    grad_wide = grad_output.astype(jnp.float32)
    grad_outer = weight_grad(activated, grad_output)
    grad_activated = project_back(grad_output, outer_full)
    grad_before = gate_pullback(grad_activated)[0].astype(jnp.bfloat16)
    grad_inner = weight_grad(normed_three, grad_before)
    ignored, norm_pullback = jax.vjp(norm_scale, hidden_two, gain_three)
    grad_hidden_part, grad_gain_three = norm_pullback(project_back(grad_before, inner_full))
    grad_hidden_two = grad_wide + grad_hidden_part
    branch_two = grad_hidden_two.astype(jnp.bfloat16)
    grad_cross_output = weight_grad(attended_two, branch_two)
    grad_attended_two = project_back(branch_two, cross_output_full).astype(jnp.bfloat16)
    keys_back, values_back, memory_keys_back, memory_values_back = (
        keys_all,
        values_all,
        memory_keys_all,
        memory_values_all,
    )
    grad_query_two, grad_memory_keys, grad_memory_values, unused_bias = attend_backward(
        to_heads(queries_two),
        to_heads(memory_keys_back),
        to_heads(memory_values_back),
        cross_extras,
        heads_first(grad_attended_two),
        output_two,
        maximum_two,
        total_two,
    )
    memory_key_sum, memory_value_sum = (
        lax.psum_scatter(
            grad_memory_keys.reshape(sequence_count, memory_length, D),
            "ctx",
            scatter_dimension=1,
            tiled=True,
        ),
        lax.psum_scatter(
            grad_memory_values.reshape(sequence_count, memory_length, D),
            "ctx",
            scatter_dimension=1,
            tiled=True,
        ),
    )
    memory_key_rounded = memory_key_sum.astype(jnp.bfloat16)
    memory_value_rounded = memory_value_sum.astype(jnp.bfloat16)
    query_two_rounded = grad_query_two.reshape(sequence_count, local_rows, D).astype(jnp.bfloat16)
    grad_cross_query = weight_grad(normed_two, query_two_rounded)
    grad_cross_key = weight_grad(memory, memory_key_rounded)
    grad_cross_value = weight_grad(memory, memory_value_rounded)
    grad_memory = (
        project_back(memory_key_rounded, cross_key_full)
        + project_back(memory_value_rounded, cross_value_full)
    ).astype(jnp.bfloat16)
    ignored, norm_pullback = jax.vjp(norm_scale, hidden_one, gain_two)
    grad_hidden_part, grad_gain_two = norm_pullback(
        project_back(query_two_rounded, cross_query_full)
    )
    grad_hidden_one = grad_hidden_two + grad_hidden_part
    branch_one = grad_hidden_one.astype(jnp.bfloat16)
    grad_self_output = weight_grad(attended_one, branch_one)
    grad_attended_one = project_back(branch_one, output_full).astype(jnp.bfloat16)
    grad_query_one, grad_keys_all, grad_values_all, grad_bias = attend_backward(
        to_heads(queries_one),
        to_heads(keys_back),
        to_heads(values_back),
        self_extras,
        heads_first(grad_attended_one),
        output_one,
        maximum_one,
        total_one,
    )
    key_sum, value_sum = (
        lax.psum_scatter(
            grad_keys_all.reshape(sequence_count, sequence_length, D),
            "ctx",
            scatter_dimension=1,
            tiled=True,
        ),
        lax.psum_scatter(
            grad_values_all.reshape(sequence_count, sequence_length, D),
            "ctx",
            scatter_dimension=1,
            tiled=True,
        ),
    )
    query_one_rounded = grad_query_one.reshape(sequence_count, local_rows, D).astype(jnp.bfloat16)
    first_key_bfloat_cast = key_sum.astype(jnp.bfloat16)
    value_one_rounded = value_sum.astype(jnp.bfloat16)
    grad_self_query = weight_grad(normed_one, query_one_rounded)
    grad_self_key = weight_grad(normed_one, first_key_bfloat_cast)
    grad_self_value = weight_grad(normed_one, value_one_rounded)
    grad_normed_one = (
        project_back(query_one_rounded, query_full)
        + project_back(first_key_bfloat_cast, key_full)
        + project_back(value_one_rounded, value_full)
    )
    ignored, norm_pullback = jax.vjp(norm_scale, inputs_wide, gain_one)
    grad_input_part, grad_gain_one = norm_pullback(grad_normed_one)
    grad_tokens = (grad_hidden_one + grad_input_part).astype(jnp.bfloat16)
    (
        shard_gain_one,
        shard_gain_two,
        shard_gain_three,
        shard_bias,
        shard_query,
        shard_key,
        shard_value,
        shard_output,
        shard_cross_query,
        shard_cross_key,
        shard_cross_value,
        shard_cross_output,
        shard_inner,
        shard_outer,
    ) = (
        lax.psum_scatter(
            grad_gain_one.astype(jnp.bfloat16), "fsdp", scatter_dimension=0, tiled=True
        ).astype(jnp.float32),
        lax.psum_scatter(
            grad_gain_two.astype(jnp.bfloat16), "fsdp", scatter_dimension=0, tiled=True
        ).astype(jnp.float32),
        lax.psum_scatter(
            grad_gain_three.astype(jnp.bfloat16), "fsdp", scatter_dimension=0, tiled=True
        ).astype(jnp.float32),
        lax.psum_scatter(
            grad_bias.astype(jnp.bfloat16), "fsdp", scatter_dimension=0, tiled=True
        ).astype(jnp.float32),
        lax.psum_scatter(
            grad_self_query.astype(jnp.bfloat16), "fsdp", scatter_dimension=0, tiled=True
        ).astype(jnp.float32),
        lax.psum_scatter(
            grad_self_key.astype(jnp.bfloat16), "fsdp", scatter_dimension=0, tiled=True
        ).astype(jnp.float32),
        lax.psum_scatter(
            grad_self_value.astype(jnp.bfloat16), "fsdp", scatter_dimension=0, tiled=True
        ).astype(jnp.float32),
        lax.psum_scatter(
            grad_self_output.astype(jnp.bfloat16), "fsdp", scatter_dimension=0, tiled=True
        ).astype(jnp.float32),
        lax.psum_scatter(
            grad_cross_query.astype(jnp.bfloat16), "fsdp", scatter_dimension=0, tiled=True
        ).astype(jnp.float32),
        lax.psum_scatter(
            grad_cross_key.astype(jnp.bfloat16), "fsdp", scatter_dimension=0, tiled=True
        ).astype(jnp.float32),
        lax.psum_scatter(
            grad_cross_value.astype(jnp.bfloat16), "fsdp", scatter_dimension=0, tiled=True
        ).astype(jnp.float32),
        lax.psum_scatter(
            grad_cross_output.astype(jnp.bfloat16), "fsdp", scatter_dimension=0, tiled=True
        ).astype(jnp.float32),
        lax.psum_scatter(
            grad_inner.astype(jnp.bfloat16), "fsdp", scatter_dimension=0, tiled=True
        ).astype(jnp.float32),
        lax.psum_scatter(
            grad_outer.astype(jnp.bfloat16), "fsdp", scatter_dimension=0, tiled=True
        ).astype(jnp.float32),
    )
    (
        total_gain_one,
        total_gain_two,
        total_gain_three,
        total_bias,
        total_query,
        total_key,
        total_value,
        total_output,
        total_cross_query,
        total_cross_key,
        total_cross_value,
        total_cross_output,
        total_inner,
        total_outer,
    ) = lax.psum(
        (
            shard_gain_one,
            shard_gain_two,
            shard_gain_three,
            shard_bias,
            shard_query,
            shard_key,
            shard_value,
            shard_output,
            shard_cross_query,
            shard_cross_key,
            shard_cross_value,
            shard_cross_output,
            shard_inner,
            shard_outer,
        ),
        "ctx",
    )
    return (
        layer_output,
        grad_tokens,
        grad_memory,
        total_gain_one,
        total_gain_two,
        total_gain_three,
        total_bias,
        total_query,
        total_key,
        total_value,
        total_output,
        total_cross_query,
        total_cross_key,
        total_cross_value,
        total_cross_output,
        total_inner,
        total_outer,
    )


def solution(mesh):
    return jax.shard_map(
        shards,
        mesh=mesh,
        in_specs=(
            P("fsdp", "ctx", None),
            P("fsdp", "ctx", None),
            P(),
            P(),
            P("fsdp", None),
            P("fsdp"),
            P("fsdp"),
            P("fsdp"),
            P("fsdp", None),
            P("fsdp", None),
            P("fsdp", None),
            P("fsdp", None),
            P("fsdp", None),
            P("fsdp", None),
            P("fsdp", None),
            P("fsdp", None),
            P("fsdp", None),
            P("fsdp", None),
            P("fsdp", None),
            P("fsdp", "ctx", None),
        ),
        out_specs=(
            P("fsdp", "ctx", None),
            P("fsdp", "ctx", None),
            P("fsdp", "ctx", None),
            P("fsdp"),
            P("fsdp"),
            P("fsdp"),
            P("fsdp", None),
            P("fsdp", None),
            P("fsdp", None),
            P("fsdp", None),
            P("fsdp", None),
            P("fsdp", None),
            P("fsdp", None),
            P("fsdp", None),
            P("fsdp", None),
            P("fsdp", None),
            P("fsdp", None),
        ),
        check_vma=False,
    )
```

profile of v0, /device:TPU:0, one launch (start us, length us, event | category | flops | bytes accessed | tf_op | source)
XLA Modules:
  0.0 3398.6 jit_solution(7504646194926650613)
XLA Ops:
  107.8 45.0 %all-gather.39.cloned.1.call-done = bf16[1024,768]{1,0:T(8,128)(2,1)} async-done(((bf16[128,768]{1,0:T(8,128)(2,1)}), bf16[1024,768]{1,0:T(8,128)(2,1)}) %all-gather.39.cloned.1.call-update) | async-done | bytes 1572880 | tf_op jit(solution)/shard_map/all_gather | solution.py:271
  154.5 44.1 %all-gather.41.cloned.1.call-done = bf16[1024,768]{1,0:T(8,128)(2,1)} async-done(((bf16[128,768]{1,0:T(8,128)(2,1)}), bf16[1024,768]{1,0:T(8,128)(2,1)}) %all-gather.41.cloned.1.call-update) | async-done | bytes 1572880 | tf_op jit(solution)/shard_map/all_gather | solution.py:272
  201.2 758.8 %while.76 = (s32[]{:T(128)}, f32[2,1,12,128]{3,2,1,0:T(8,128)S(1)}, f32[2,1,12,128]{3,2,1,0:T(8,128)S(1)}, f32[2,1,12,128,64]{3,4,2,1,0:T(8,128)}, s32[2]{0:T(12...) while((s32[]{:T(128)}, f32[2,1,12,128]{3,2,1,0:T(8,128)S(1)}, ...), condition=%wide.region_4.6_spmd.clone.clone, body=%wide.region_1.5_spmd.clone.clone.sunk | while | flops 261888512 | bytes 40516676 | solution.py:87
  203.2 362.7 %gather_fusion = s32[65536]{0:T(1024)S(1)} fusion(s32[2047]{0:T(1024)S(1)} %get-tuple-element.1867, s32[65536]{0:T(1024)S(1)} %broadcast_clamp_fusion.4), kind=kCustom, calls=%fused_computation.clone.clone.1 | custom fusion | bytes 786432 | tf_op jit(solution)/shard_map/while/body/eval_jaxpr/jit(_take)/gather | solution.py:238
  582.6 362.7 %gather_fusion = s32[65536]{0:T(1024)S(1)} fusion(s32[2047]{0:T(1024)S(1)} %get-tuple-element.1867, s32[65536]{0:T(1024)S(1)} %broadcast_clamp_fusion.4), kind=kCustom, calls=%fused_computation.clone.clone.1 | custom fusion | bytes 786432 | tf_op jit(solution)/shard_map/while/body/eval_jaxpr/jit(_take)/gather | solution.py:238
  988.3 72.2 %while.74 = (s32[]{:T(128)}, f32[10,1,12,128]{3,2,1,0:T(8,128)S(1)}, f32[10,1,12,128]{3,2,1,0:T(8,128)S(1)}, f32[10,1,12,128,64]{3,4,2,1,0:T(8,128)}, s32[10]{0:...) while((s32[]{:T(128)}, ...), condition=%wide.region_12.14_spmd, body=%wide.region_9.13_spmd.sunk | while | flops 207614976 | bytes 11659987 | solution.py:87
  1096.1 143.9 %while.75 = (s32[]{:T(128)}, f32[1,128,12,64]{1,3,2,0:T(8,128)}, f32[1,5120,12,64]{1,3,2,0:T(8,128)}, f32[1,5120,12,64]{1,3,2,0:T(8,128)}, s32[10]{0:T(128)S(1)}...) while((s32[]{:T(128)}, f32[1,128,12,64]{1,3,2,0:T(8,128)}, ...), condition=%wide.region_21.23_spmd.clone, body=%wide.region_19.22_spmd.clone.sunk | while | flops 511772160 | bytes 46966096 | solution.py:164
  1249.3 766.6 %while.77 = (s32[]{:T(128)}, f32[1,128,12,64]{1,3,2,0:T(8,128)}, f32[1,1024,12,64]{1,3,2,0:T(8,128)}, f32[1,1024,12,64]{1,3,2,0:T(8,128)}, f32[32,12]{0,1:T(8,12...) while((s32[]{:T(128)}, f32[1,128,12,64]{1,3,2,0:T(8,128)}, ...), condition=%wide.region_26.28_spmd.clone.clone.clone, body=%wide.region_24.27_spmd.clone.clone.clone.sunk | while | flops 673263744 | bytes 100371664 | solution.py:164
  1251.6 362.7 %gather_fusion.1 = s32[65536]{0:T(1024)S(1)} fusion(s32[2047]{0:T(1024)S(1)} %get-tuple-element.2011, s32[65536]{0:T(1024)S(1)} %broadcast_clamp_fusion.5), kind=kCustom, calls=%fused_computation.1.clone.clone.1 | custom fusion | bytes 786432 | tf_op jit(solution)/shard_map/while/body/eval_jaxpr/jit(_take)/gather | solution.py:238
  1634.8 362.7 %gather_fusion.1 = s32[65536]{0:T(1024)S(1)} fusion(s32[2047]{0:T(1024)S(1)} %get-tuple-element.2011, s32[65536]{0:T(1024)S(1)} %broadcast_clamp_fusion.5), kind=kCustom, calls=%fused_computation.1.clone.clone.1 | custom fusion | bytes 786432 | tf_op jit(solution)/shard_map/while/body/eval_jaxpr/jit(_take)/gather | solution.py:238
  2025.2 64.7 %reduce-scatter.19.cloned.1.call-done = f32[1,128,768]{1,2,0:T(8,128)} async-done(((f32[1,1024,768]{1,2,0:T(8,128)}), f32[1,128,768]{1,2,0:T(8,128)}) %reduce-scatter.19.cloned.1.call-update) | async-done | bytes 393232 | tf_op jit(solution)/shard_map/reduce_scatter | solution.py:363
  2092.6 75.0 %reduce-scatter.21.cloned.1.call-done = f32[1,128,768]{1,2,0:T(8,128)} async-done(((f32[1,1024,768]{1,2,0:T(8,128)}), f32[1,128,768]{1,2,0:T(8,128)}) %reduce-scatter.21.cloned.1.call-update) | async-done | bytes 393232 | tf_op jit(solution)/shard_map/reduce_scatter | solution.py:369
  2180.2 241.1 %reduce-scatter.23.cloned.1.call-done = f32[1,640,768]{1,2,0:T(8,128)} async-done(((f32[1,5120,768]{1,2,0:T(8,128)}), f32[1,640,768]{1,2,0:T(8,128)}) %reduce-scatter.23.cloned.1.call-update) | async-done | bytes 1966096 | tf_op jit(solution)/shard_map/reduce_scatter | solution.py:321
  2435.5 239.5 %reduce-scatter.25.cloned.1.call-done = f32[1,640,768]{1,2,0:T(8,128)} async-done(((f32[1,5120,768]{1,2,0:T(8,128)}), f32[1,640,768]{1,2,0:T(8,128)}) %reduce-scatter.25.cloned.1.call-update) | async-done | bytes 1966096 | tf_op jit(solution)/shard_map/reduce_scatter | solution.py:327
  2681.1 22.0 reduce-scatter.27.cloned.1.call-done
  2703.1 28.4 reduce-scatter.33.cloned.1.call-done
  2731.4 28.4 reduce-scatter.35.cloned.1.call-done
  2759.8 28.5 reduce-scatter.37.cloned.1.call-done
  2816.6 28.4 reduce-scatter.31.cloned.1.call-done
  2845.0 50.4 %reduce-scatter.39.cloned.1.call-done = bf16[192,3072]{1,0:T(8,128)(2,1)} async-done(((bf16[768,3072]{1,0:T(8,128)(2,1)}), bf16[192,3072]{1,0:T(8,128)(2,1)}) %reduce-scatter.39.cloned.1.call-update) | async-done | bytes 1179664 | tf_op jit(solution)/shard_map/reduce_scatter | solution.py:442
  2895.4 50.4 %reduce-scatter.41.cloned.1.call-done = bf16[768,768]{1,0:T(8,128)(2,1)} async-done(((bf16[3072,768]{1,0:T(8,128)(2,1)}), bf16[768,768]{1,0:T(8,128)(2,1)}) %reduce-scatter.41.cloned.1.call-update) | async-done | bytes 1179664 | tf_op jit(solution)/shard_map/reduce_scatter | solution.py:445
  2950.3 23.8 reduce-scatter.43.cloned.1.call-done
  2975.2 27.9 reduce-scatter.45.cloned.1.call-done
  3004.3 382.9 %all-reduce.11 = (f32[192]{0:T(256)}, f32[192]{0:T(256)}, f32[192]{0:T(256)}, f32[8,12]{1,0:T(8,128)}, f32[192,768]{1,0:T(8,128)}, /*index=5*/f32[192,768]{1,0:T...) all-reduce(f32[192]{0:T(256)S(1)} %copy-done.94, ...), channel_id=1, replica_groups=mesh['ctx'=8,'fsdp'=4] {'ctx'}, use_global_device_ids=true, to_apply=%region_34.36 | all-reduce | flops 2359968 | bytes 14161152 | tf_op jit(solution)/shard_map/psum | solution.py:464
  (814 shorter events, 531.8 us)
Async XLA Ops:
  10.0 96.0 %all-gather.21.cloned.1.call-start = ((), (), s32[]{:S(2)}) async-start(), calls=%async_computation.15 | async-start | bytes 1474560 | tf_op jit(solution)/shard_map/all_gather | solution.py:210
  10.6 142.2 %all-gather.39.cloned.1.call-start = ((), (), s32[]{:S(2)}) async-start(), calls=%async_computation.36 | async-start | bytes 1769472 | tf_op jit(solution)/shard_map/all_gather | solution.py:271
  32.3 166.3 %all-gather.41.cloned.1.call-start = ((), (), s32[]{:S(2)}) async-start(), calls=%async_computation.37 | async-start | bytes 1769472 | tf_op jit(solution)/shard_map/all_gather | solution.py:272
  51.4 911.4 %all-gather.25.cloned.1.call-start = ((), (), s32[]{:S(2)}) async-start(), calls=%async_computation.17 | async-start | bytes 1474560 | tf_op jit(solution)/shard_map/all_gather | solution.py:213
  52.2 913.0 %all-gather.29.cloned.1.call-start = ((), (), s32[]{:S(2)}) async-start(), calls=%async_computation.19 | async-start | bytes 1474560 | tf_op jit(solution)/shard_map/all_gather | solution.py:214
  52.9 914.1 %all-gather.43.cloned.1.call-start = ((), (), s32[]{:S(2)}) async-start(), calls=%async_computation.38 | async-start | bytes 8847360 | tf_op jit(solution)/shard_map/all_gather | solution.py:273
  71.3 906.3 %all-gather.45.cloned.1.call-start = ((), (), s32[]{:S(2)}) async-start(), calls=%async_computation.39 | async-start | bytes 8847360 | tf_op jit(solution)/shard_map/all_gather | solution.py:274
  90.3 974.5 %all-gather.33.cloned.1.call-start = ((), (), s32[]{:S(2)}) async-start(), calls=%async_computation.21 | async-start | bytes 1474560 | tf_op jit(solution)/shard_map/all_gather | solution.py:217
  90.8 976.4 %all-gather.35.cloned.1.call-start = ((), (), s32[]{:S(2)}) async-start(), calls=%async_computation.22 | async-start | bytes 5898240 | tf_op jit(solution)/shard_map/all_gather | solution.py:218
  91.6 979.3 %all-gather.37.cloned.1.call-start = ((), (), s32[]{:S(2)}) async-start(), calls=%async_computation.23 | async-start | bytes 5898240 | tf_op jit(solution)/shard_map/all_gather | solution.py:219
  92.2 1997.7 %reduce-scatter.19.cloned.1.call-start = ((), (), s32[]{:S(2)}) async-start(), calls=%async_computation.24 | async-start | bytes 3538944 | tf_op jit(solution)/shard_map/reduce_scatter | solution.py:363
  2016.0 151.7 %reduce-scatter.21.cloned.1.call-start = ((), (), s32[]{:S(2)}) async-start(), calls=%async_computation.25 | async-start | bytes 3538944 | tf_op jit(solution)/shard_map/reduce_scatter | solution.py:369
  2016.5 404.8 %reduce-scatter.23.cloned.1.call-start = ((), (), s32[]{:S(2)}) async-start(), calls=%async_computation.26 | async-start | bytes 17694720 | tf_op jit(solution)/shard_map/reduce_scatter | solution.py:321
  2017.1 657.9 %reduce-scatter.25.cloned.1.call-start = ((), (), s32[]{:S(2)}) async-start(), calls=%async_computation.27 | async-start | bytes 17694720 | tf_op jit(solution)/shard_map/reduce_scatter | solution.py:327
  2017.7 685.3 %reduce-scatter.27.cloned.1.call-start = ((), (), s32[]{:S(2)}) async-start(), calls=%async_computation.28 | async-start | bytes 1474560 | tf_op jit(solution)/shard_map/reduce_scatter | solution.py:418
  2019.9 711.6 %reduce-scatter.33.cloned.1.call-start = ((), (), s32[]{:S(2)}) async-start(), calls=%async_computation.31 | async-start | bytes 1474560 | tf_op jit(solution)/shard_map/reduce_scatter | solution.py:427
  2021.5 738.3 %reduce-scatter.35.cloned.1.call-start = ((), (), s32[]{:S(2)}) async-start(), calls=%async_computation.32 | async-start | bytes 1474560 | tf_op jit(solution)/shard_map/reduce_scatter | solution.py:430
  2023.6 764.7 %reduce-scatter.37.cloned.1.call-start = ((), (), s32[]{:S(2)}) async-start(), calls=%async_computation.33 | async-start | bytes 1474560 | tf_op jit(solution)/shard_map/reduce_scatter | solution.py:439
  2025.2 791.5 %reduce-scatter.29.cloned.1.call-start = ((), (), s32[]{:S(2)}) async-start(), calls=%async_computation.29 | async-start | bytes 1474560 | tf_op jit(solution)/shard_map/reduce_scatter | solution.py:421
  2092.6 752.4 %reduce-scatter.31.cloned.1.call-start = ((), (), s32[]{:S(2)}) async-start(), calls=%async_computation.30 | async-start | bytes 1474560 | tf_op jit(solution)/shard_map/reduce_scatter | solution.py:424
  2170.3 725.2 %reduce-scatter.39.cloned.1.call-start = ((), (), s32[]{:S(2)}) async-start(), calls=%async_computation.34 | async-start | bytes 5898240 | tf_op jit(solution)/shard_map/reduce_scatter | solution.py:442
  2174.0 771.8 %reduce-scatter.41.cloned.1.call-start = ((), (), s32[]{:S(2)}) async-start(), calls=%async_computation.35 | async-start | bytes 5898240 | tf_op jit(solution)/shard_map/reduce_scatter | solution.py:445
  2180.2 793.9 %reduce-scatter.43.cloned.1.call-start = ((), (), s32[]{:S(2)}) async-start(), calls=%async_computation.40 | async-start | bytes 1474560
  2427.4 575.7 %reduce-scatter.45.cloned.1.call-start = ((), (), s32[]{:S(2)}) async-start(), calls=%async_computation.41 | async-start | bytes 1474560
  (208 other events, 2209.6 us)
Sparse Core Ops, SparseCore 0:
  9.6 20.2 all-gather.18
  31.4 17.6 all-gather.22
  69.6 17.4 all-gather.30
  88.5 17.4 all-gather.20
  108.6 44.1 all-gather.38
  155.6 42.9 all-gather.40
  238.1 118.3 all-gather.42
  359.4 116.5 all-gather.44
  494.6 37.4 all-gather.34
  533.5 37.4 all-gather.36
  2016.1 73.7 reduce-scatter.18
  2093.4 74.2 reduce-scatter.20
  2171.1 250.2 reduce-scatter.22
  2424.8 250.2 reduce-scatter.24
  2678.2 24.8 reduce-scatter.26
  2705.7 25.7 reduce-scatter.32
  2734.0 25.7 reduce-scatter.34
  2762.5 25.7 reduce-scatter.36
  2790.9 25.7 reduce-scatter.28
  2819.2 25.7 reduce-scatter.30
  2847.5 47.8 reduce-scatter.38
  2898.0 47.8 reduce-scatter.40
  2948.3 25.7 reduce-scatter.42
  2977.4 25.7 reduce-scatter.44
  (4 shorter events, 66.6 us)
where the time goes:
time: 3410 us; the launch traced here: 3400 us
  local copies, waits for them, and re-layouts  1570 us (46%)
  waiting for transfers between devices  1070 us (31%)
  blocking collectives  409 us (12%)
  matrix products  277 us (8%)
  other arithmetic  34.7 us (1%)
    gather x8, local copies, waits for them, and re-layouts, self_extras(): jnp.take(bucket_table, key_block_position[None, :] - query_position[:, No...  1450 us
    psum x1, blocking collectives, shards(): lax.psum((shard_gain_one, shard_gain_two, shard_gain_three, shard_bias, s...  383 us
    reduce_scatter x1, waiting for transfers between devices, shards(): lax.psum_scatter(grad_memory_keys.reshape(sequence_count, memory_length,...  241 us
    reduce_scatter x1, waiting for transfers between devices, shards(): lax.psum_scatter(grad_memory_values.reshape(sequence_count, memory_length...  240 us
    reduce_scatter x1, waiting for transfers between devices, shards(): lax.psum_scatter(grad_values_all.reshape(sequence_count, sequence_length,...  75 us
  transfers between devices with their start and end apart: 28, of which 21 were waited for; matrix products, arithmetic and copies ran while one was open for 27% of the time, Pallas kernels for 0%

commit v1 on v0

--- a/solution.py
+++ b/solution.py
@@ -1,21 +1,318 @@
 import jax
 import jax.numpy as jnp
 from jax import lax
+from jax.experimental import pallas as pl
+from jax.experimental.pallas import tpu as pltpu
 from jax.sharding import PartitionSpec as P
 
 D = 768
 HEADS = 12
+PAIRS = HEADS // 2
 HEAD_DIM = 64
-BUCKETS = 32
 PIECE = 64
 BLOCK = 256
+PLEN = 256
 KBLK = 512
 PSG = 20
-PLEN = 256
-
-
+BUCKETS = 32
+RESIDENT_ROWS = 1024
+LANES = 128
 EPSILON = 1e-06
 NEGATIVE = -1e30
+F32 = jnp.float32
+BF16 = jnp.bfloat16
+VMEM_LIMIT = 60 * 2**20
+
+def nn(a, b):
+    return lax.dot_general(a, b, (((1,), (0,)), ((), ())), preferred_element_type=F32)
+def nt(a, b):
+    return lax.dot_general(a, b, (((1,), (1,)), ((), ())), preferred_element_type=F32)
+def tn(a, b):
+    return lax.dot_general(a, b, (((0,), (0,)), ((), ())), preferred_element_type=F32)
+
+def normed(x, gain):
+    return x * lax.rsqrt(jnp.mean(x * x, axis=-1, keepdims=True) + EPSILON) * gain
+
+def half_mask(x, half):
+    lane = lax.broadcasted_iota(jnp.int32, x.shape, 1) // HEAD_DIM
+    return jnp.where(lane == half, x, jnp.zeros_like(x))
+
+def lanes_of(pair):
+    return pl.ds(pl.multiple_of(pair * LANES, LANES), LANES)
+
+def shear(x, sign):
+    row = lax.broadcasted_iota(jnp.int32, x.shape, 0)
+    for bit in (1, 2, 4):
+        x = jnp.where(row & bit != 0, pltpu.roll(x, (sign * bit) % x.shape[1], 1), x)
+    return x
+
+def bias_tables_kernel(table, back_table, ahead, behind):
+    full = table.shape[1]
+    def head(h, c):
+        for src, out in ((table, ahead), (back_table, behind)):
+            base = shear(pltpu.roll(jnp.broadcast_to(src[pl.ds(h, 1), :], (8, full)), 1, 1), 1)
+            for parity in range(2):
+                for i in range(PIECE // 16):
+                    both = [pltpu.roll(base, (8 * g - 64 * parity) % full, 1) if (8 * g - 64 * parity) % full else base
+                            for g in (2 * i, 2 * i + 1)]
+                    out[parity, h, 16 * i:16 * i + 16, :] = jnp.concatenate(both, 0).astype(BF16)
+        return c
+    lax.fori_loop(0, HEADS, head, 0)
+
+def bias_tables(table, back_table):
+    full = table.shape[1]
+    return pl.pallas_call(
+        bias_tables_kernel,
+        name="bias_tables",
+        out_shape=[sds((2, HEADS, PIECE, full), BF16)] * 2,
+        in_specs=[full_spec()] * 2,
+        out_specs=[full_spec()] * 2,
+        compiler_params=pltpu.CompilerParams(vmem_limit_bytes=VMEM_LIMIT),
+    )(table, back_table)
+
+def piece_bias(tables, h, piece, length):
+    start = pl.multiple_of(length - (piece + piece % 2) * PIECE, LANES)
+    return tables[piece % 2, h, :, pl.ds(start, length)].astype(F32)
+
+def bias_rows(tables, h, own, count, length):
+    return jnp.concatenate([piece_bias(tables, h, own[i], length) for i in range(count)], 0)
+
+def add_diagonals(acc, block, piece):
+    rows, length = block.shape
+    wide = jnp.concatenate([block, jnp.zeros((rows, LANES), F32)], axis=1)
+    total = pltpu.roll(wide[0:8], LANES, 1)
+    for g in range(1, rows // 8):
+        total += pltpu.roll(wide[8 * g:8 * g + 8], LANES - 8 * g, 1)
+    start = pl.multiple_of(length - (piece - piece % 2) * PIECE - LANES, LANES)
+    where = (piece % 2, slice(None), pl.ds(start, length + LANES))
+    acc[where] += total
+
+def self_forward_kernel(order, own, tok_all, tok, w, gains, table, wo, wq2,
+                        q_nat, k_nat, v_nat, o1, h1, a1, a2, q2, lse, inv, q_own):
+    length = tok_all.shape[0]
+    rows = tok.shape[0]
+    slots, mine = length // PIECE, rows // PIECE
+    for s in range(slots):
+        inv[order[s]] = s
+    per = BLOCK // PIECE
+
+    def tile(t, c):
+        parts = [tok_all[pl.ds(pl.multiple_of(inv[t * per + i] * PIECE, PIECE), PIECE), :] for i in range(per)]
+        a = normed(jnp.concatenate(parts, 0).astype(F32), gains[0:1, :]).astype(BF16)
+        dst = pl.ds(pl.multiple_of(t * BLOCK, BLOCK), BLOCK)
+        for j, out in enumerate((q_nat, k_nat, v_nat)):
+            out[dst, :] = nn(a, w[:, j * D:(j + 1) * D]).astype(BF16)
+        return c
+
+    lax.fori_loop(0, length // BLOCK, tile, 0)
+    for i in range(mine):
+        q_own[i * PIECE:(i + 1) * PIECE, :] = q_nat[pl.ds(pl.multiple_of(own[i] * PIECE, PIECE), PIECE), :]
+    a1[...] = normed(tok[...].astype(F32), gains[0:1, :]).astype(BF16)
+    lane = lax.broadcasted_iota(jnp.int32, (rows, length), 1)
+    limit = jnp.concatenate([jnp.full((PIECE, 1), (own[i] // per + 1) * BLOCK, jnp.int32) for i in range(mine)], 0)
+    visible = lane < limit
+    stat_lane = lax.broadcasted_iota(jnp.int32, (rows, LANES), 1)
+
+    def pair(p, stats):
+        sl = lanes_of(p)
+        q, k, v = q_own[:, sl], k_nat[:, sl], v_nat[:, sl]
+        total = jnp.zeros((rows, LANES), F32)
+        for half in range(2):
+            h = 2 * p + half
+            s = jnp.where(visible, nt(q, half_mask(k, half)) + bias_rows(table, h, own, mine, length), NEGATIVE)
+            m = jnp.max(s, axis=1, keepdims=True)
+            e = jnp.exp(s - m)
+            l = jnp.sum(e, axis=1, keepdims=True)
+            total += nn(e.astype(BF16), half_mask(v, half)) / l
+            stats = jnp.where(stat_lane == h, m + jnp.log(l), stats)
+        o1[:, sl] = total.astype(BF16)
+        return stats
+
+    lse[...] = lax.fori_loop(0, PAIRS, pair, jnp.zeros((rows, LANES), F32))
+    h = tok[...].astype(F32) + nn(o1[...], wo[...])
+    h1[...] = h
+    a = normed(h, gains[1:2, :]).astype(BF16)
+    a2[...] = a
+    q2[...] = nn(a, wq2[...]).astype(BF16)
+
+def full_spec():
+    return pl.BlockSpec(memory_space=pltpu.VMEM)
+def smem_spec():
+    return pl.BlockSpec(memory_space=pltpu.SMEM)
+def sds(shape, dtype):
+    return jax.ShapeDtypeStruct(shape, dtype)
+
+def self_forward(order, own, tok_all, tok, w, gains, table, wo, wq2):
+    length, rows = tok_all.shape[0], tok.shape[0]
+    return pl.pallas_call(
+        self_forward_kernel,
+        name="self_forward",
+        out_shape=[sds((length, D), BF16)] * 3 + [sds((rows, D), BF16), sds((rows, D), F32), sds((rows, D), BF16),
+                   sds((rows, D), BF16), sds((rows, D), BF16), sds((rows, LANES), F32)],
+        in_specs=[smem_spec()] * 2 + [full_spec()] * 7,
+        out_specs=[full_spec()] * 9,
+        scratch_shapes=[pltpu.SMEM((length // PIECE,), jnp.int32), pltpu.VMEM((rows, D), BF16)],
+        compiler_params=pltpu.CompilerParams(vmem_limit_bytes=VMEM_LIMIT),
+    )(order, own, tok_all, tok, w, gains, table, wo, wq2)
+
+def cross_forward_kernel(q_all, k2, v2, mask, o, lse):
+    rows = q_all.shape[0]
+    step = BLOCK
+    stat_lane = lax.broadcasted_iota(jnp.int32, (step, LANES), 1)
+
+    def tile(t, c):
+        rs = pl.ds(pl.multiple_of(t * step, step), step)
+        def pair(p, stats):
+            sl = lanes_of(p)
+            q, k, v = q_all[rs, sl], k2[:, sl], v2[:, sl]
+            total = jnp.zeros((step, LANES), F32)
+            for half in range(2):
+                s = nt(q, half_mask(k, half)) + mask[...]
+                m = jnp.max(s, axis=1, keepdims=True)
+                e = jnp.exp(s - m)
+                l = jnp.sum(e, axis=1, keepdims=True)
+                total += nn(e.astype(BF16), half_mask(v, half)) / l
+                stats = jnp.where(stat_lane == 2 * p + half, m + jnp.log(l), stats)
+            o[rs, sl] = total.astype(BF16)
+            return stats
+        lse[rs, :] = lax.fori_loop(0, PAIRS, pair, jnp.zeros((step, LANES), F32))
+        return c
+    lax.fori_loop(0, rows // step, tile, 0)
+
+def cross_forward(q_all, k2, v2, mask):
+    rows = q_all.shape[0]
+    return pl.pallas_call(
+        cross_forward_kernel,
+        name="cross_forward",
+        out_shape=[sds((rows, D), BF16), sds((rows, LANES), F32)],
+        in_specs=[full_spec()] * 4,
+        out_specs=[full_spec()] * 2,
+        compiler_params=pltpu.CompilerParams(vmem_limit_bytes=VMEM_LIMIT),
+    )(q_all, k2, v2, mask)
+
+def cross_backward_kernel(q_all, do_all, stats, k2, v2, mask, dq, dk, dv):
+    rows = q_all.shape[0]
+    slots = k2.shape[0]
+    step = BLOCK
+
+    def pair(p, c):
+        sl = lanes_of(p)
+        ks = [half_mask(k2[:, sl], i) for i in range(2)]
+        vs = [half_mask(v2[:, sl], i) for i in range(2)]
+        def tile(t, carry):
+            dkp, dvp = carry
+            rs = pl.ds(pl.multiple_of(t * step, step), step)
+            q, do = q_all[rs, sl], do_all[rs, sl]
+            dqp = jnp.zeros((step, LANES), F32)
+            for half in range(2):
+                h = 2 * p + half
+                qm, dom = half_mask(q, half), half_mask(do, half)
+                s = nt(ks[half], q) + mask[...]
+                e = jnp.exp(s - stats[pl.ds(h, 1), rs])
+                dvp = dvp + nn(e.astype(BF16), dom)
+                ds = (e * (nt(vs[half], do) - stats[pl.ds(16 + h, 1), rs])).astype(BF16)
+                dkp = dkp + nn(ds, qm)
+                dqp = dqp + tn(ds, ks[half])
+            dq[rs, sl] = dqp.astype(dq.dtype)
+            return dkp, dvp
+        zero = jnp.zeros((slots, LANES), F32)
+        dkp, dvp = lax.fori_loop(0, rows // step, tile, (zero, zero))
+        dk[:, sl] = dkp.astype(BF16)
+        dv[:, sl] = dvp.astype(BF16)
+        return c
+    lax.fori_loop(0, PAIRS, pair, 0)
+
+def cross_backward(q_all, do_all, stats, k2, v2, mask):
+    rows, slots = q_all.shape[0], k2.shape[0]
+    return pl.pallas_call(
+        cross_backward_kernel,
+        name="cross_backward",
+        out_shape=[sds((rows, D), F32), sds((slots, D), BF16), sds((slots, D), BF16)],
+        in_specs=[full_spec()] * 6,
+        out_specs=[full_spec()] * 3,
+        compiler_params=pltpu.CompilerParams(vmem_limit_bytes=VMEM_LIMIT),
+    )(q_all, do_all, stats, k2, v2, mask)
+
+def self_backward_kernel(order, own, q_nat, k_nat, v_nat, do_slot, do_own, stat_slot, stat_own, delta_own, table, back_table,
+                         dq, dk, dv, diag, inv, q_own, k_own, v_own, do_nat, stat_nat, stat_t, acc):
+    length = q_nat.shape[0]
+    rows = do_own.shape[0]
+    full = 2 * length
+    slots, mine = length // PIECE, rows // PIECE
+    per = BLOCK // PIECE
+    for s in range(slots):
+        inv[order[s]] = s
+    def move(i, c):
+        src = pl.ds(pl.multiple_of(inv[i] * PIECE, PIECE), PIECE)
+        dst = pl.ds(pl.multiple_of(i * PIECE, PIECE), PIECE)
+        do_nat[dst, :] = do_slot[src, :]
+        stat_nat[dst, :] = stat_slot[src, :]
+        return c
+    lax.fori_loop(0, slots, move, 0)
+    for i in range(length // LANES):
+        stat_t[:, i * LANES:(i + 1) * LANES] = stat_nat[i * LANES:(i + 1) * LANES, :].T
+    for i in range(mine):
+        src = pl.ds(pl.multiple_of(own[i] * PIECE, PIECE), PIECE)
+        dst = slice(i * PIECE, (i + 1) * PIECE)
+        q_own[dst, :] = q_nat[src, :]
+        k_own[dst, :] = k_nat[src, :]
+        v_own[dst, :] = v_nat[src, :]
+    lane = lax.broadcasted_iota(jnp.int32, (rows, length), 1)
+    limit = jnp.concatenate([jnp.full((PIECE, 1), (own[i] // per + 1) * BLOCK, jnp.int32) for i in range(mine)], 0)
+    first = jnp.concatenate([jnp.full((PIECE, 1), (own[i] // per) * BLOCK, jnp.int32) for i in range(mine)], 0)
+    visible, seen = lane < limit, lane >= first
+    stat_lane = lax.broadcasted_iota(jnp.int32, (rows, LANES), 1)
+
+    def column(h):
+        return jnp.sum(jnp.where(stat_lane == h, stat_own[...], 0.0), axis=1, keepdims=True)
+
+    diag[...] = jnp.zeros_like(diag)
+    def pair(p, c):
+        sl = lanes_of(p)
+        q, k, v, do = q_own[:, sl], k_nat[:, sl], v_nat[:, sl], do_own[:, sl]
+        kq, vq, qa, da = k_own[:, sl], v_own[:, sl], q_nat[:, sl], do_nat[:, sl]
+        dqp = jnp.zeros((rows, LANES), F32)
+        dkp = jnp.zeros((rows, LANES), F32)
+        dvp = jnp.zeros((rows, LANES), F32)
+        for half in range(2):
+            h = 2 * p + half
+            bias = bias_rows(table, h, own, mine, length)
+            km, vm = half_mask(k, half), half_mask(v, half)
+            s = jnp.where(visible, nt(q, km) + bias, NEGATIVE)
+            e = jnp.exp(s - column(h))
+            ds = e * (nt(do, vm) - column(16 + h))
+            dqp += nn(ds.astype(BF16), km)
+            acc[...] = jnp.zeros_like(acc)
+            for i in range(mine):
+                add_diagonals(acc, ds[i * PIECE:(i + 1) * PIECE, :], own[i])
+            joined = shear(acc[0] + pltpu.roll(acc[1], full - PIECE, 1), -1)
+            diag[pl.ds(h, 1), :] = jnp.sum(pltpu.roll(joined, full - 1, 1), axis=0, keepdims=True)
+            bias = bias_rows(back_table, h, own, mine, length)
+            s = jnp.where(seen, nt(half_mask(kq, half), qa) + bias, NEGATIVE)
+            e = jnp.exp(s - stat_t[pl.ds(h, 1), :])
+            dvp += nn(e.astype(BF16), half_mask(da, half))
+            ds = e * (nt(half_mask(vq, half), da) - stat_t[pl.ds(16 + h, 1), :])
+            dkp += nn(ds.astype(BF16), half_mask(qa, half))
+        dq[:, sl] = dqp.astype(BF16)
+        dk[:, sl] = dkp.astype(BF16)
+        dv[:, sl] = dvp.astype(BF16)
+        return c
+    lax.fori_loop(0, PAIRS, pair, 0)
+
+def self_backward(order, own, q_nat, k_nat, v_nat, do_slot, do_own, stat_slot, stat_own, table, back_table):
+    length, rows = q_nat.shape[0], do_own.shape[0]
+    def kern(order, own, q_nat, k_nat, v_nat, do_slot, do_own, stat_slot, stat_own, table, back_table, *rest):
+        self_backward_kernel(order, own, q_nat, k_nat, v_nat, do_slot, do_own, stat_slot, stat_own, None, table, back_table, *rest)
+    return pl.pallas_call(
+        kern,
+        name="self_backward",
+        out_shape=[sds((rows, D), BF16)] * 3 + [sds((16, 2 * length), F32)],
+        in_specs=[smem_spec()] * 2 + [full_spec()] * 9,
+        out_specs=[full_spec()] * 4,
+        scratch_shapes=[pltpu.SMEM((length // PIECE,), jnp.int32)] + [pltpu.VMEM((rows, D), BF16)] * 3
+        + [pltpu.VMEM((length, D), BF16), pltpu.VMEM((length, LANES), F32), pltpu.VMEM((LANES, length), F32), pltpu.VMEM((2, 8, 2 * length), F32)],
+        compiler_params=pltpu.CompilerParams(vmem_limit_bytes=VMEM_LIMIT),
+    )(order, own, q_nat, k_nat, v_nat, do_slot, do_own, stat_slot, stat_own, table, back_table)
 
 
 def norm_scale(values, gain_vector):
@@ -165,7 +462,7 @@
     return result
 
 
-def shards(
+def streamed_shards(
     tokens,
     memory,
     piece_order,
@@ -501,9 +798,169 @@
     )
 
 
+def norm_back(x, gain, dy):
+    r = lax.rsqrt(jnp.mean(x * x, axis=-1, keepdims=True) + EPSILON)
+    gdy = gain * dy
+    dx = r * gdy - x * (r * r * r) * jnp.mean(x * gdy, axis=-1, keepdims=True)
+    return dx, jnp.sum(dy * x * r, axis=0)
+
+
+def gather(x, axis_name, axis=0):
+    return lax.all_gather(x, axis_name, axis=axis, tiled=True)
+
+
+def scatter(x, axis_name, axis=0):
+    return lax.psum_scatter(x, axis_name, scatter_dimension=axis, tiled=True)
+
+
+def shards(
+    tokens,
+    memory,
+    piece_order,
+    bucket_table,
+    passage_lengths,
+    self_gain,
+    cross_gain,
+    hidden_gain,
+    position_bias,
+    self_query,
+    self_attention_key,
+    self_value,
+    self_output,
+    cross_query,
+    cross_key,
+    cross_value,
+    cross_output,
+    hidden_in,
+    hidden_out,
+    grad_output,
+):
+    tok, mem, grad = tokens[0], memory[0], grad_output[0]
+    rows, slots = tok.shape[0], mem.shape[0]
+    length = (bucket_table.shape[0] + 1) // 2
+    peers = length // rows
+    index = lax.axis_index("ctx")
+    own = lax.dynamic_slice_in_dim(piece_order, index * (rows // PIECE), rows // PIECE)
+    tok_all = gather(tok, "ctx")
+    w_self = gather(jnp.concatenate([self_query, self_attention_key, self_value], 1), "fsdp")
+    w_mid = gather(jnp.concatenate([self_output, cross_query], 1), "fsdp")
+    w_mem = gather(jnp.concatenate([cross_key, cross_value], 1), "fsdp")
+    w_co = gather(cross_output, "fsdp")
+    gains = gather(jnp.stack([self_gain, cross_gain, hidden_gain]), "fsdp", 1).astype(F32)
+    bias_rows_all = gather(position_bias, "fsdp")
+    w_in = lax.all_to_all(hidden_in, "fsdp", split_axis=1, concat_axis=0, tiled=True)
+    wo, wq2 = w_mid[:, :D], w_mid[:, D:]
+    buckets = jnp.arange(BUCKETS, dtype=jnp.int32)[:, None]
+    hot = (bucket_table[None, :] == buckets).astype(BF16)
+    hot = jnp.pad(hot, ((0, 0), (0, 1)))
+    hot_back = jnp.pad(hot[:, -2::-1], ((0, 0), (0, 1)))
+    spread = lambda x: jnp.pad(jnp.einsum("lr,lh->hr", x, bias_rows_all, preferred_element_type=F32), ((0, 4), (0, 0)))
+    ahead, behind = bias_tables(spread(hot), spread(hot_back))
+    q1_nat, k1_nat, v1_nat, o1, h1, a1, a2, q2, lse1 = self_forward(
+        piece_order, own, tok_all, tok, w_self, jnp.pad(gains, ((0, 5), (0, 0))), ahead, wo, wq2
+    )
+    kv2 = project(mem, w_mem).astype(BF16)
+    k2, v2 = kv2[:, :D], kv2[:, D:]
+    slot = index * slots + jnp.arange(slots, dtype=jnp.int32)
+    hidden = jnp.where(slot % PLEN < jnp.take(passage_lengths[0], slot // PLEN), 0.0, NEGATIVE)
+    q2_all = gather(q2, "ctx")
+    part, part_lse = cross_forward(q2_all, k2, v2, hidden[None, :])
+    swap = lambda x: lax.all_to_all(x.reshape(peers, rows, x.shape[-1]), "ctx", 0, 0)
+    part, part_lse = swap(part), swap(part_lse)[:, :, :HEADS]
+    top = jnp.max(part_lse, axis=0)
+    share = jnp.exp(part_lse - top)
+    lse2 = top + jnp.log(jnp.sum(share, axis=0))
+    share = share / jnp.sum(share, axis=0)
+    out2 = jnp.sum(jnp.repeat(share, HEAD_DIM, axis=2) * part.astype(F32), axis=0)
+    o2 = out2.astype(BF16)
+    h2 = h1 + project(o2, w_co)
+    a3 = norm_scale(h2, gains[2]).astype(BF16)
+    a3_all, g_all = gather(a3, "fsdp"), gather(grad, "fsdp")
+    pre = project(a3_all, w_in)
+    act, pullback = jax.vjp(smooth_gate, pre)
+    act = act.astype(BF16)
+    out_part = project(act, hidden_out)
+    dpre = pullback(nt(g_all, hidden_out))[0].astype(BF16)
+    da3_part = nt(dpre, w_in)
+    da3 = scatter(da3_part.astype(BF16), "fsdp").astype(F32)
+    layer_output = (h2 + scatter(out_part.astype(BF16), "fsdp").astype(F32)).astype(BF16)
+    g_out = tn(act, g_all)
+    g_in = lax.all_to_all(tn(a3_all, dpre).astype(BF16), "fsdp", split_axis=0, concat_axis=1, tiled=True)
+    dx, gg3 = norm_back(h2, gains[2], da3)
+    dh2 = grad.astype(F32) + dx
+    branch2 = dh2.astype(BF16)
+    do2 = nt(branch2, w_co).astype(BF16)
+    delta = lambda d, o: jnp.sum((d.astype(F32) * o).reshape(rows, HEADS, HEAD_DIM), axis=2)
+    pad4 = lambda x: jnp.pad(x, ((0, 0), (0, 4)))
+    stat2 = jnp.concatenate([pad4(lse2), pad4(delta(do2, out2))], 1)
+    do2_all = gather(do2, "ctx")
+    stat2_all = gather(stat2.T, "ctx", 1)
+    dq2_part, dk2, dv2 = cross_backward(q2_all, do2_all, stat2_all, k2, v2, hidden[:, None])
+    dq2 = scatter(dq2_part, "ctx").astype(BF16)
+    dx, gg2 = norm_back(h1, gains[1], nt(dq2, wq2))
+    dh1 = dh2 + dx
+    branch1 = dh1.astype(BF16)
+    do1 = nt(branch1, wo).astype(BF16)
+    stat1 = jnp.pad(jnp.concatenate([lse1[:, :16], pad4(delta(do1, o1.astype(F32)))], 1), ((0, 0), (0, LANES - 32)))
+    do1_all = gather(do1, "ctx")
+    stat1_all = gather(stat1, "ctx")
+    dq1, dk1, dv1, diag = self_backward(
+        piece_order, own, q1_nat, k1_nat, v1_nat, do1_all, do1, stat1_all, stat1, ahead, behind
+    )
+    g_bias = jnp.einsum(
+        "hr,lr->lh", diag[:HEADS], hot.astype(F32), precision=lax.Precision.HIGHEST, preferred_element_type=F32
+    )
+    da1 = nt(dq1, w_self[:, :D]) + nt(dk1, w_self[:, D : 2 * D]) + nt(dv1, w_self[:, 2 * D :])
+    tok_wide = tok.astype(F32)
+    dx, gg1 = norm_back(tok_wide, gains[0], da1)
+    grad_tokens = (dh1 + dx).astype(BF16)
+    grad_memory = (nt(dk2, w_mem[:, :D]) + nt(dv2, w_mem[:, D:])).astype(BF16)
+    full = jnp.concatenate(
+        [
+            tn(a1, dq1),
+            tn(a1, dk1),
+            tn(a1, dv1),
+            tn(o1, branch1),
+            tn(a2, dq2),
+            tn(mem, dk2),
+            tn(mem, dv2),
+            tn(o2, branch2),
+        ],
+        1,
+    ).astype(BF16)
+    mine = scatter(full, "fsdp")
+    quarter = mine.shape[0]
+    mine = jnp.concatenate([mine, g_in, g_out.astype(BF16).reshape(quarter, -1)], 1)
+    total = lax.psum(mine, "ctx").astype(F32)
+    cut = lambda i: total[:, i * D : (i + 1) * D]
+    small = jnp.concatenate([jnp.stack([gg1, gg2, gg3]), jnp.pad(g_bias.T, ((0, 0), (0, D - BUCKETS)))], 0)
+    small = lax.psum(small, ("ctx", "fsdp"))
+    f = lax.axis_index("fsdp")
+    gain = lambda i: lax.dynamic_slice_in_dim(small[i], f * quarter, quarter)
+    eighth = position_bias.shape[0]
+    bias_out = lax.dynamic_slice_in_dim(small[3:].T, f * eighth, eighth)
+    return (
+        layer_output[None],
+        grad_tokens[None],
+        grad_memory[None],
+        gain(0),
+        gain(1),
+        gain(2),
+        bias_out,
+        *[cut(i) for i in range(8)],
+        total[:, 8 * D : 12 * D],
+        total[:, 12 * D :].reshape(-1, D),
+    )
+
+
+def pick(*arrays):
+    resident = (arrays[3].shape[0] + 1) // 2 <= RESIDENT_ROWS
+    return (shards if resident else streamed_shards)(*arrays)
+
+
 def solution(mesh):
     return jax.shard_map(
-        shards,
+        pick,
         mesh=mesh,
         in_specs=(
             P("fsdp", "ctx", None),

time: 3410 us -> 960 us (0.28)
  local copies, waits for them, and re-layouts: 1570 us -> 76.5 us
  waiting for transfers between devices: 1070 us -> 491 us
  blocking collectives: 409 us -> 149 us
  matrix products: 277 us -> 45.3 us
  Pallas kernels: 0 us -> 111 us
    gather x8 -> x1, local copies, waits for them, and re-layouts: 1450 us -> 0.74 us  [shards(): jnp.take(passage_lengths[0], slot // PLEN)]
    reduce_scatter x12 -> x3, waiting for transfers between devices: 863 us -> 114 us  [scatter(): return lax.psum_scatter(x, axis_name, scatter_dimension=axis, tiled=True)]
    psum x1, blocking collectives: 383 us -> 43.3 us  [shards(): small = lax.psum(small, ('ctx', 'fsdp'))]
    dot_general x112 -> x23, matrix products: 251 us -> 34.3 us  [the longest x10 19.1 us: tn(): lax.dot_general(a, b, (((0,), (0,)), ((), ())), preferred_element_type=F32)]
    psum x0 -> x1, waiting for transfers between devices: none -> 157 us  [shards(): total = lax.psum(mine, 'ctx').astype(F32)]
    pallas_call x0 -> x5, Pallas kernels: none -> 111 us  [the longest x1 34.2 us: cross_backward(): pl.pallas_call(cross_backward_kernel, name='cross_backward', out_shape=[s...]
    all_gather x1 -> x6, blocking collectives: 5.68 us -> 106 us  [gather(): return lax.all_gather(x, axis_name, axis=axis, tiled=True)]
    all_to_all x0 -> x4, waiting for transfers between devices: none -> 43.1 us  [the longest x2 33.5 us: shards(): lax.all_to_all(x.reshape(peers, rows, x.shape[-1]), 'ctx', 0, 0)]
  transfers between devices with their start and end apart: 28 -> 17, of which waited for: 21 -> 13; matrix products, arithmetic and copies ran while one was open for 27% -> 7% of each run, Pallas kernels for 0% -> 3%
where the time goes in v1:
time: 960 us; the launch traced here: 950 us
  waiting for transfers between devices  491 us (51%)
  blocking collectives  149 us (16%)
  Pallas kernels  111 us (12%)
  local copies, waits for them, and re-layouts  76.5 us (8%)
  matrix products  45.3 us (5%)
  other arithmetic  45.1 us (5%)
  starting transfers between devices  16.8 us (2%)
  between operations  15.1 us (2%)
    psum x1, waiting for transfers between devices, shards(): total = lax.psum(mine, 'ctx').astype(F32)  157 us
    all_gather x8, waiting for transfers between devices, gather(): return lax.all_gather(x, axis_name, axis=axis, tiled=True)  124 us
    reduce_scatter x3, waiting for transfers between devices, scatter(): return lax.psum_scatter(x, axis_name, scatter_dimension=axis, tiled=True)  114 us
    all_gather x6, blocking collectives, gather(): return lax.all_gather(x, axis_name, axis=axis, tiled=True)  106 us
    unnamed x14, waiting for transfers between devices  52.9 us
    psum x1, blocking collectives, shards(): small = lax.psum(small, ('ctx', 'fsdp'))  43.3 us
    unnamed x126, local copies, waits for them, and re-layouts  39.6 us
    pallas_call x1, Pallas kernels, cross_backward(): pl.pallas_call(cross_backward_kernel, name='cross_backward', out_shape=[s...  34.2 us
  transfers between devices with their start and end apart: 17, of which 13 were waited for; matrix products, arithmetic and copies ran while one was open for 7% of the time, Pallas kernels for 3%

profile of v1, /device:TPU:0, one launch (start us, length us, event | category | flops | bytes accessed | tf_op | source)
XLA Modules:
  0.0 950.3 jit_solution(16748518941462106530)
XLA Ops:
  28.4 12.9 %bias_tables.1 = (bf16[2,12,64,2048]{3,2,1,0:T(8,128)(2,1)}, bf16[2,12,64,2048]{3,2,1,0:T(8,128)(2,1)}) custom-call(f32[16,2048]{1,0:T(8,128)} %pad.38.table, f32[16,2048]{1,0:T(8,128)} %pad.40.back_table), custom_call_target="tpu_custom_call" | custom-call | tf_op jit(solution)/shard_map/bias_tables/pallas_call | solution.py:64
  44.5 39.2 %all-gather.26.cloned.1.call-done = bf16[1,1024,768]{2,1,0:T(8,128)(2,1)} async-done(((bf16[1,128,768]{2,1,0:T(8,128)(2,1)}), bf16[1,1024,768]{2,1,0:T(8,128)(2,1)}) %all-gather.26.cloned.1.call-update) | async-done | bytes 1572880 | tf_op jit(solution)/shard_map/all_gather | solution.py:809
  83.7 31.7 %all-gather.12.cloned.1.call-done.w = bf16[768,2304]{1,0:T(8,128)(2,1)} async-done(((bf16[192,2304]{1,0:T(8,128)(2,1)}), bf16[768,2304]{1,0:T(8,128)(2,1)}) %all-gather.12.cloned.1.call-update) | async-done | bytes 3538960 | tf_op jit(solution)/shard_map/all_gather | solution.py:809
  115.4 17.2 %self_forward.1 = (bf16[1024,768]{1,0:T(8,128)(2,1)}, bf16[1024,768]{1,0:T(8,128)(2,1)}, bf16[1024,768]{1,0:T(8,128)(2,1)}, bf16[128,768]{1,0:T(8,128)(2,1)}, f3...) custom-call(s32[16]{0:T(128)} %order.3, ...), custom_call_target="tpu_custom_call" | custom-call | tf_op jit(solution)/shard_map/self_forward/pallas_call | solution.py:147
  154.2 34.1 %all-gather.16.cloned.1.call-done.q_all = bf16[1024,768]{1,0:T(8,128)(2,1)} async-done(((bf16[128,768]{1,0:T(8,128)(2,1)}), bf16[1024,768]{1,0:T(8,128)(2,1)}) %all-gather.16.cloned.1.call-update) | async-done | bytes 1572880 | tf_op jit(solution)/shard_map/all_gather | solution.py:809
  188.4 27.8 %cross_forward.1 = (bf16[1024,768]{1,0:T(8,128)(2,1)}, f32[1024,128]{1,0:T(8,128)}) custom-call(bf16[1024,768]{1,0:T(8,128)(2,1)} %all-gather.16.cloned.1.call-done.q_all, bf16[640,768]{1,0:T(8,128)(2,1)} %get-tuple-element.181.k2, bf16[640,768]{1,0:T(8,128)(2,1)} %get-tuple-element.180.v2, f32[1,640]{1,0:T(1,128)} %compare_select_fusion.2.mask), custom_call_target="tpu_custom_call" | custom-call | tf_op jit(solution)/shard_map/cross_forward/pallas_call | solution.py:184
  222.2 11.8 %all-to-all-done = f32[8,128,128]{2,1,0:T(8,128)S(1)} async-done(((f32[8,128,128]{2,1,0:T(8,128)}), f32[8,128,128]{2,1,0:T(8,128)S(1)}, u32[]{:S(2)}, u32[]{:S(2)}) %all-to-all-start) | async-done | bytes 524320 | tf_op jit(solution)/shard_map/all_to_all | solution.py:868
  241.3 9.0 all-gather.1
  253.2 21.7 %all-to-all-done.1 = bf16[8,128,768]{1,2,0:T(8,128)(2,1)S(1)} async-done(((bf16[8,128,768]{1,2,0:T(8,128)(2,1)}), bf16[8,128,768]{1,2,0:T(8,128)(2,1)S(1)}, u32[]{:S(2)}, u32[]{:S(2)}) %all-to-all-start.1) | async-done | bytes 1572896 | tf_op jit(solution)/shard_map/all_to_all | solution.py:868
  282.5 17.6 %all_gather.50 = bf16[512,768]{1,0:T(8,128)(2,1)S(1)} all-gather(bf16[128,768]{1,0:T(8,128)(2,1)S(1)} %multiply_convert_fusion.1), channel_id=1, replica_groups=mesh['ctx'=8,'fsdp'=4] {'fsdp'}, dimensions={0}, use_global_device_ids=true | all-gather | bytes 983040 | tf_op jit(solution)/shard_map/all_gather | solution.py:809
  311.7 17.8 %reduce-scatter.9.cloned.1.call-done = bf16[128,768]{1,0:T(8,128)(2,1)} async-done(((bf16[512,768]{1,0:T(8,128)(2,1)}), bf16[128,768]{1,0:T(8,128)(2,1)}) %reduce-scatter.9.cloned.1.call-update) | async-done | bytes 196624 | tf_op jit(solution)/shard_map/reduce_scatter | solution.py:813
  330.6 24.9 %reduce-scatter.7.cloned.1.call-done = bf16[128,768]{1,0:T(8,128)(2,1)} async-done(((bf16[512,768]{1,0:T(8,128)(2,1)}), bf16[128,768]{1,0:T(8,128)(2,1)}) %reduce-scatter.7.cloned.1.call-update) | async-done | bytes 196624 | tf_op jit(solution)/shard_map/reduce_scatter | solution.py:813
  360.1 33.0 %all_gather.53.stats = f32[32,1024]{1,0:T(8,128)} all-gather(f32[32,128]{1,0:T(8,128)S(1)} %fusion.76), channel_id=1, replica_groups=mesh['ctx'=8,'fsdp'=4] {'ctx'}, dimensions={1}, use_global_device_ids=true | all-gather | bytes 147456 | tf_op jit(solution)/shard_map/all_gather | solution.py:809
  393.1 9.9 %all-gather.22.cloned.1.call-done.do_all = bf16[1024,768]{1,0:T(8,128)(2,1)} async-done(((bf16[128,768]{1,0:T(8,128)(2,1)}), bf16[1024,768]{1,0:T(8,128)(2,1)}) %all-gather.22.cloned.1.call-update) | async-done | bytes 1572880 | tf_op jit(solution)/shard_map/all_gather | solution.py:809
  403.0 34.2 %cross_backward.1 = (f32[1024,768]{1,0:T(8,128)}, bf16[640,768]{1,0:T(8,128)(2,1)}, bf16[640,768]{1,0:T(8,128)(2,1)}) custom-call(bf16[1024,768]{1,0:T(8,128)(2,1)} %all-gather.16.cloned.1.call-done.q_all, bf16[1024,768]{1,0:T(8,128)(2,1)} %all-gather.22.cloned.1.call-done.do_all, f32[32,1024]{1,0:T(8,128)} %all_gather.53.stats, ...), custom_call_target="tpu_custom_call" | custom-call | tf_op jit(solution)/shard_map/cross_backward/pallas_call | solution.py:227
  438.8 71.6 %reduce-scatter.11.cloned.1.call-done = f32[128,768]{1,0:T(8,128)} async-done(((f32[1024,768]{1,0:T(8,128)}), f32[128,768]{1,0:T(8,128)}) %reduce-scatter.11.cloned.1.call-update) | async-done | bytes 393232 | tf_op jit(solution)/shard_map/reduce_scatter | solution.py:813
  514.9 34.9 %all_gather.55.stat_slot = f32[1024,128]{1,0:T(8,128)} all-gather(f32[128,128]{1,0:T(8,128)S(1)} %pad.44.stat_own), channel_id=1, replica_groups=mesh['ctx'=8,'fsdp'=4] {'ctx'}, dimensions={0}, use_global_device_ids=true | all-gather | bytes 589824 | tf_op jit(solution)/shard_map/all_gather | solution.py:809
  558.7 18.9 %self_backward.1 = (bf16[128,768]{1,0:T(8,128)(2,1)}, bf16[128,768]{1,0:T(8,128)(2,1)}, bf16[128,768]{1,0:T(8,128)(2,1)}, f32[16,2048]{1,0:T(8,128)}) custom-call(s32[16]{0:T(128)} %order.3, s32[2]{0:T(128)} %dynamic_slice.21.own, bf16[1024,768]{1,0:T(8,128)(2,1)} %get-tuple-element.43.q_nat, bf16[1024,768]{1,0:T(8,128)(2,1)} %get-tuple-element.44.k_nat, ...), custom_call_target="tpu_custom_call" | custom-call | tf_op jit(solution)/shard_map/self_backward/pallas_call | solution.py:306
  592.2 12.7 %copy.173 = bf16[768,6144]{1,0:T(8,128)(2,1)} copy(bf16[768,6144]{0,1:T(8,128)(2,1)} %fusion.9) | data formatting | bytes 18874368
  618.9 9.5 %all-to-all-done.3 = bf16[4,192,768]{2,1,0:T(8,128)(2,1)} async-done(((bf16[4,192,768]{2,1,0:T(8,128)(2,1)}), bf16[4,192,768]{2,1,0:T(8,128)(2,1)}, u32[]{:S(2)}, u32[]{:S(2)}) %all-to-all-start.3) | async-done | bytes 1179680 | tf_op jit(solution)/shard_map/all_to_all | solution.py:888
  631.1 51.5 %reduce-scatter.13.cloned.1.call-done = bf16[192,6144]{1,0:T(8,128)(2,1)} async-done(((bf16[768,6144]{1,0:T(8,128)(2,1)}), bf16[192,6144]{1,0:T(8,128)(2,1)}) %reduce-scatter.13.cloned.1.call-update) | async-done | bytes 2359312
  687.1 16.1 %pad_maximum_fusion = bf16[192,12288]{0,1:T(8,128)(2,1)} fusion(bf16[192,3072]{0,1:T(8,128)(2,1)S(1)} %copy.160, bf16[192,3072]{0,1:T(8,128)(2,1)} %bitcast.127, bf16[192,6144]{0,1:T(8,128)(2,1)} %copy.174), kind=kLoop, calls=%fused_computation | loop fusion | flops 14155776 | bytes 9437184 | tf_op jit(solution)/shard_map/concatenate | solution.py:933
  711.7 43.3 %psum.14 = f32[15,768]{1,0:T(8,128)S(1)} all-reduce(f32[15,768]{1,0:T(8,128)S(1)} %select_maximum_fusion.1), channel_id=1, replica_groups=mesh['ctx'=8,'fsdp'=4] {'ctx','fsdp'}, use_global_device_ids=true, to_apply=%region_17.18 | all-reduce | flops 11520 | bytes 92160 | tf_op jit(solution)/shard_map/psum | solution.py:937
  758.5 157.1 %all-reduce.12.cloned.1.call-done = bf16[192,12288]{0,1:T(8,128)(2,1)} async-done(((bf16[192,12288]{0,1:T(8,128)(2,1)}), bf16[192,12288]{0,1:T(8,128)(2,1)}) %all-reduce.12.cloned.1.call-update) | async-done | bytes 4718608 | tf_op jit(solution)/shard_map/psum | solution.py:934
  (267 shorter events, 176.7 us)
Async XLA Ops:
  7.2 295.3 %copy-start = (bf16[768,768]{1,0:T(8,128)(2,1)S(1)}, bf16[768,768]{1,0:T(8,128)(2,1)}, u32[]{:S(2)}) copy-start(bf16[768,768]{1,0:T(8,128)(2,1)} %param.38) | copy-start | bytes 3538948
  7.2 34.0 %all-gather.14.cloned.1.call-start = ((), (), s32[]{:S(2)}) async-start(), calls=%async_computation.9 | async-start | bytes 2949120 | tf_op jit(solution)/shard_map/all_gather | solution.py:809
  9.4 74.3 %all-gather.26.cloned.1.call-start = ((), (), s32[]{:S(2)}) async-start(), calls=%async_computation.19 | async-start | bytes 1769472 | tf_op jit(solution)/shard_map/all_gather | solution.py:809
  10.1 105.3 %all-gather.12.cloned.1.call-start = ((), (), s32[]{:S(2)}) async-start(), calls=%async_computation.8 | async-start | bytes 4423680 | tf_op jit(solution)/shard_map/all_gather | solution.py:809
  11.2 138.2 %all-gather.18.cloned.1.call-start = ((), (), s32[]{:S(2)}) async-start(), calls=%async_computation.11 | async-start | bytes 2949120 | tf_op jit(solution)/shard_map/all_gather | solution.py:809
  12.2 176.2 %all-gather.16.cloned.1.call-start = ((), (), s32[]{:S(2)}) async-start(), calls=%async_computation.10 | async-start | bytes 1769472 | tf_op jit(solution)/shard_map/all_gather | solution.py:809
  18.6 25.9 %copy-start.13 = (bf16[32,2047]{1,0:T(8,128)(2,1)}, bf16[32,2047]{1,0:T(8,128)(2,1)S(1)}, u32[]{:S(2)}) copy-start(bf16[32,2047]{1,0:T(8,128)(2,1)S(1)} %fusion.59) | copy-start | bytes 393028
  115.4 20.2 %copy-start.33 = (s32[1,20]{1,0:T(1,128)S(1)}, s32[1,20]{1,0:T(1,128)}, u32[]{:S(2)}) copy-start(s32[1,20]{1,0:T(1,128)} %param.24) | copy-start | bytes 244
  115.4 34.0 %copy-start.44 = (bf16[1,640,768]{2,1,0:T(8,128)(2,1)S(1)}, bf16[1,640,768]{2,1,0:T(8,128)(2,1)}, u32[]{:S(2)}) copy-start(bf16[1,640,768]{2,1,0:T(8,128)(2,1)} %param.21) | copy-start | bytes 2949124
  216.2 17.9 %all-to-all-start = ((f32[8,128,128]{2,1,0:T(8,128)}), f32[8,128,128]{2,1,0:T(8,128)S(1)}, u32[]{:S(2)}, u32[]{:S(2)}) async-start(f32[8,128,128]{2,1,0:T(8,128)} %bitcast.136), calls=%async_computation | async-start | bytes 1048576 | tf_op jit(solution)/shard_map/all_to_all | solution.py:868
  234.1 40.8 %all-to-all-start.1 = ((bf16[8,128,768]{1,2,0:T(8,128)(2,1)}), bf16[8,128,768]{1,2,0:T(8,128)(2,1)S(1)}, u32[]{:S(2)}, u32[]{:S(2)}) async-start(bf16[8,128,768]{1,2,0:T(8,128)(2,1)} %copy.150), calls=%async_computation.1 | async-start | bytes 3145728 | tf_op jit(solution)/shard_map/all_to_all | solution.py:868
  237.7 42.7 %all-gather.20.cloned.1.call-start = ((), (), s32[]{:S(2)}) async-start(), calls=%async_computation.12 | async-start | bytes 1474560 | tf_op jit(solution)/shard_map/all_gather | solution.py:809
  274.9 25.2 %all-to-all-start.2 = ((bf16[192,4,768]{2,0,1:T(8,128)(2,1)}), bf16[192,4,768]{2,0,1:T(8,128)(2,1)}, u32[]{:S(2)}, u32[]{:S(2)}) async-start(bf16[192,4,768]{2,0,1:T(8,128)(2,1)} %bitcast.128), calls=%async_computation.2 | async-start | bytes 2359296 | tf_op jit(solution)/shard_map/all_to_all | solution.py:851
  279.2 50.3 %reduce-scatter.9.cloned.1.call-start = ((), (), s32[]{:S(2)}) async-start(), calls=%async_computation.14 | async-start | bytes 983040 | tf_op jit(solution)/shard_map/reduce_scatter | solution.py:813
  307.9 47.6 %reduce-scatter.7.cloned.1.call-start = ((), (), s32[]{:S(2)}) async-start(), calls=%async_computation.13 | async-start | bytes 983040 | tf_op jit(solution)/shard_map/reduce_scatter | solution.py:813
  311.4 45.9 %copy-start.7 = (bf16[768,768]{1,0:T(8,128)(2,1)S(1)}, bf16[768,768]{1,0:T(8,128)(2,1)}, u32[]{:S(2)}) copy-start(bf16[768,768]{1,0:T(8,128)(2,1)} %all-gather.20.cloned.1.call-done) | copy-start | bytes 3538948
  311.4 91.5 %all-gather.22.cloned.1.call-start = ((), (), s32[]{:S(2)}) async-start(), calls=%async_computation.15 | async-start | bytes 1769472 | tf_op jit(solution)/shard_map/all_gather | solution.py:809
  358.5 151.9 %reduce-scatter.11.cloned.1.call-start = ((), (), s32[]{:S(2)}) async-start(), calls=%async_computation.16 | async-start | bytes 3538944 | tf_op jit(solution)/shard_map/reduce_scatter | solution.py:813
  437.2 73.3 %copy-start.3 = (bf16[768,1536]{1,0:T(8,128)(2,1)S(1)}, bf16[768,1536]{1,0:T(8,128)(2,1)}, u32[]{:S(2)}) copy-start(bf16[768,1536]{1,0:T(8,128)(2,1)} %all-gather.14.cloned.1.call-done) | copy-start | bytes 7077892
  437.2 121.4 %all-gather.24.cloned.1.call-start = ((), (), s32[]{:S(2)}) async-start(), calls=%async_computation.17 | async-start | bytes 1769472 | tf_op jit(solution)/shard_map/all_gather | solution.py:809
  513.5 169.1 %reduce-scatter.13.cloned.1.call-start = ((), (), s32[]{:S(2)}) async-start(), calls=%async_computation.20 | async-start | bytes 11796480
  514.8 43.8 %copy-start.25 = (f32[128,128]{1,0:T(8,128)}, f32[128,128]{1,0:T(8,128)S(1)}, u32[]{:S(2)}) copy-start(f32[128,128]{1,0:T(8,128)S(1)} %pad.44.stat_own) | copy-start | bytes 196612
  608.1 20.4 %all-to-all-start.3 = ((bf16[4,192,768]{2,1,0:T(8,128)(2,1)}), bf16[4,192,768]{2,1,0:T(8,128)(2,1)}, u32[]{:S(2)}, u32[]{:S(2)}) async-start(bf16[4,192,768]{2,1,0:T(8,128)(2,1)} %bitcast.49), calls=%async_computation.6 | async-start | bytes 2359296 | tf_op jit(solution)/shard_map/all_to_all | solution.py:888
  612.5 303.1 %all-reduce.12.cloned.1.call-start = ((), (), s32[]{:S(2)}) async-start(), calls=%async_computation.18 | async-start | bytes 12582912 | tf_op jit(solution)/shard_map/psum | solution.py:934
  (49 other events, 154.6 us)
Sparse Core Ops, SparseCore 0:
  10.2 27.0 all-gather.13
  39.5 44.1 all-gather.25
  85.8 29.5 all-gather.11
  117.4 24.0 all-gather.17
  144.1 44.1 all-gather.15
  239.8 18.8 all-gather.19
  308.1 21.4 reduce-scatter.8
  332.2 23.2 reduce-scatter.6
  358.7 44.2 all-gather.21
  437.3 73.0 reduce-scatter.10
  513.7 44.9 all-gather.23
  605.0 77.5 reduce-scatter.12
  703.3 212.2 all-reduce.11

commit v2 on v1

--- a/solution.py
+++ b/solution.py
@@ -1,3 +1,5 @@
+import functools
+
 import jax
 import jax.numpy as jnp
 from jax import lax
@@ -798,6 +800,218 @@
     )
 
 
+MESH = pl.DeviceIdType.MESH
+WAYS = 4
+
+
+class Place:
+    def __init__(self, peers):
+        self.depth = peers // 2
+        c, f = lax.axis_index("ctx"), lax.axis_index("fsdp")
+        self.c, self.f = c, f
+        self.a, self.b, self.x, self.k = c // 2, c % 2, f // 2, f % 2
+        self.core = (c, self.x * 2 + 1 - self.k)
+        self.across = (c, (1 - self.x) * 2 + self.k)
+        self.beside = (self.a * 2 + 1 - self.b, f)
+
+    def ahead(self, d):
+        return lax.rem(self.a + d, self.depth)
+
+    def behind(self, d):
+        return lax.rem(self.a + self.depth - d, self.depth)
+
+    def column(self, a):
+        return (a * 2 + self.b, self.f)
+
+    def group(self, d):
+        return (self.c, lax.rem(self.f + d, WAYS))
+
+
+def greet(targets):
+    barrier = pltpu.get_barrier_semaphore()
+    for target in targets:
+        pl.semaphore_signal(barrier, inc=1, device_id=target, device_id_type=MESH)
+    pl.semaphore_wait(barrier, len(targets))
+
+
+def remote(src, dst, sems, index, target):
+    return pltpu.make_async_remote_copy(
+        src_ref=src,
+        dst_ref=dst,
+        send_sem=sems[0].at[index],
+        recv_sem=sems[1].at[index],
+        device_id=target,
+        device_id_type=MESH,
+    )
+
+
+def sems(count):
+    return [pltpu.SemaphoreType.DMA((count,)), pltpu.SemaphoreType.DMA((count,))]
+
+
+def reduce_kernel(peers, left_index, *refs):
+    n_left = len(set(left_index))
+    n_mats = len(left_index)
+    lefts, rights = refs[:n_left], refs[n_left : n_left + n_mats]
+    g_in, g_out, small, out, small_out = refs[n_left + n_mats : n_left + n_mats + 5]
+    (prod, own, sa, ra, sb, rb, sc, rc, sd, rd, tiny, tiny_in, *sem) = refs[n_left + n_mats + 5 :]
+    sem_a, sem_b, sem_c, sem_d, sem_e, sem_f, sem_g, sem_t = [sem[2 * i : 2 * i + 2] for i in range(8)]
+    at = Place(peers)
+    depth = at.depth
+    quarter, wide = out.shape[1], out.shape[2]
+    half, part = wide // 2, quarter // depth
+    total = out.shape[0]
+    sent = []
+
+    def go(copy):
+        copy.start()
+        sent.append(copy)
+        return copy
+
+    columns = lambda b: pl.ds(pl.multiple_of(b * half, LANES), half)
+    shard_rows = lambda f: pl.ds(pl.multiple_of(f * quarter, quarter), quarter)
+    part_rows = lambda a: pl.ds(pl.multiple_of(a * part, part), part)
+    mine, theirs = columns(at.b), columns(1 - at.b)
+
+    greet(
+        [at.core, at.across, at.beside]
+        + [at.column(at.ahead(d)) for d in range(1, depth)]
+        + [(at.c, (1 - at.x) * 2 + 1 - at.k)]
+    )
+
+    def stage_a(i):
+        prod[...] = tn(lefts[left_index[i]][...], rights[i][...])
+        for x in range(2):
+            own[i, x] = prod[shard_rows(x * 2 + at.k), :]
+            sa[i, x] = prod[shard_rows(x * 2 + 1 - at.k), :].astype(BF16)
+        go(remote(sa.at[i], ra.at[i], sem_a, i, at.core))
+
+    def stage_b(i):
+        remote(sa.at[i], ra.at[i], sem_a, i, at.core).wait_recv()
+        sb[i] = (own[i, 1 - at.x] + ra[i, 1 - at.x].astype(F32)).astype(BF16)
+        go(remote(sb.at[i], rb.at[i], sem_b, i, at.across))
+
+    def stage_c(j):
+        if j < n_mats:
+            remote(sb.at[j], rb.at[j], sem_b, j, at.across).wait_recv()
+            value = own[j, at.x] + ra[j, at.x].astype(F32) + rb[j].astype(F32)
+            sc[j] = value.astype(BF16)
+        go(remote(sc.at[j, :, theirs], rc.at[j], sem_c, j, at.beside))
+
+    def stage_d(j):
+        remote(sc.at[j, :, mine], rc.at[j], sem_c, j, at.beside).wait_recv()
+        value = sc[j, :, mine].astype(F32) + rc[j].astype(F32)
+        sd[j] = value.astype(BF16)
+        for d in range(1, depth):
+            go(remote(sd.at[j, part_rows(at.ahead(d))], rd.at[j, part_rows(at.a)], sem_d, j * depth + d, at.column(at.ahead(d))))
+
+    def stage_e(j):
+        value = sd[j, part_rows(at.a), :].astype(F32)
+        for d in range(1, depth):
+            slot = rd.at[j, part_rows(at.behind(d))]
+            remote(slot, slot, sem_d, j * depth + d, at.column(at.behind(d))).wait_recv()
+            value += slot[...].astype(F32)
+        spot = out.at[j, part_rows(at.a), mine]
+        spot[...] = value.astype(BF16)
+        for d in range(1, depth):
+            go(remote(spot, spot, sem_e, j * depth + d, at.column(at.ahead(d))))
+
+    def stage_f(j):
+        for d in range(1, depth):
+            spot = out.at[j, part_rows(at.behind(d)), mine]
+            remote(spot, spot, sem_e, j * depth + d, at.column(at.behind(d))).wait_recv()
+        go(remote(out.at[j, :, mine], out.at[j, :, mine], sem_f, j, at.beside))
+
+    def stage_g(j):
+        remote(out.at[j, :, theirs], out.at[j, :, theirs], sem_f, j, at.beside).wait_recv()
+
+    order = list(range(n_mats + WAYS, n_mats + 2 * WAYS)) + list(range(n_mats)) + list(range(n_mats, n_mats + WAYS))
+    for q in range(WAYS):
+        sc[n_mats + WAYS + q] = g_out[q * quarter : (q + 1) * quarter, :]
+    tiny[0] = small[...]
+    hops = [at.core, at.across, at.beside]
+    for t in range(total + 4):
+        if 4 <= t:
+            stage_g(order[t - 4])
+        if 3 <= t < total + 3:
+            stage_f(order[t - 3])
+        if 2 <= t < total + 2:
+            stage_e(order[t - 2])
+        if 1 <= t < total + 1:
+            stage_d(order[t - 1])
+        if t == total - WAYS:
+            for d in range(1, WAYS):
+                slot = sc.at[n_mats + lax.rem(at.f + WAYS - d, WAYS)]
+                remote(slot, slot, sem_g, d, at.group(WAYS - d)).wait_recv()
+        if t < total:
+            stage_c(order[t])
+        if 1 <= t <= n_mats:
+            stage_b(t - 1)
+        if t < n_mats:
+            stage_a(t)
+        if t == n_mats:
+            sc[n_mats + at.f] = g_in[shard_rows(at.f), :]
+            for d in range(1, WAYS):
+                f = lax.rem(at.f + d, WAYS)
+                go(remote(g_in.at[shard_rows(f)], sc.at[n_mats + at.f], sem_g, d, at.group(d)))
+        if t < 4:
+            if t:
+                remote(tiny.at[t - 1], tiny_in.at[t - 1], sem_t, t - 1, hops[t - 1]).wait_recv()
+                tiny[t] = tiny[t - 1] + tiny_in[t - 1]
+            if t < 3:
+                go(remote(tiny.at[t], tiny_in.at[t], sem_t, t, hops[t]))
+            else:
+                for d in range(1, depth):
+                    go(remote(tiny.at[3], tiny_in.at[2 + d], sem_t, 2 + d, at.column(at.ahead(d))))
+        if t == 4:
+            value = tiny[3]
+            for d in range(1, depth):
+                remote(tiny.at[3], tiny_in.at[2 + d], sem_t, 2 + d, at.column(at.behind(d))).wait_recv()
+                value += tiny_in[2 + d]
+            small_out[...] = value
+    for copy in sent:
+        copy.wait_send()
+
+
+def reduce_grads(peers, pairs, g_in, g_out, small):
+    lefts, left_index = [], []
+    for left, _ in pairs:
+        for i, seen in enumerate(lefts):
+            if seen is left:
+                break
+        else:
+            lefts.append(left)
+            i = len(lefts) - 1
+        left_index.append(i)
+    rights = [right for _, right in pairs]
+    n, total = len(pairs), len(pairs) + 2 * WAYS
+    width = g_in.shape[1]
+    quarter, half, depth = width // WAYS, width // 2, peers // 2
+    return pl.pallas_call(
+        functools.partial(reduce_kernel, peers, left_index),
+        name="reduce_grads",
+        out_shape=[sds((total, quarter, width), BF16), sds(small.shape, F32)],
+        in_specs=[full_spec()] * (len(lefts) + n + 3),
+        out_specs=[full_spec()] * 2,
+        scratch_shapes=[
+            pltpu.VMEM((width, width), F32),
+            pltpu.VMEM((n, 2, quarter, width), F32),
+            pltpu.VMEM((n, 2, quarter, width), BF16),
+            pltpu.VMEM((n, 2, quarter, width), BF16),
+            pltpu.VMEM((n, quarter, width), BF16),
+            pltpu.VMEM((n, quarter, width), BF16),
+            pltpu.VMEM((total, quarter, width), BF16),
+            pltpu.VMEM((total, quarter, half), BF16),
+            pltpu.VMEM((total, quarter, half), BF16),
+            pltpu.VMEM((total, quarter, half), BF16),
+            pltpu.VMEM((4,) + small.shape, F32),
+            pltpu.VMEM((3 + depth,) + small.shape, F32),
+        ]
+        + sems(n) + sems(n) + sems(total) + sems(total * depth) + sems(total * depth) + sems(total) + sems(WAYS) + sems(3 + depth),
+        compiler_params=pltpu.CompilerParams(collective_id=0, has_side_effects=True, vmem_limit_bytes=VMEM_LIMIT),
+    )(*lefts, *rights, g_in, g_out, small)
+
+
 def norm_back(x, gain, dy):
     r = lax.rsqrt(jnp.mean(x * x, axis=-1, keepdims=True) + EPSILON)
     gdy = gain * dy
@@ -884,8 +1098,8 @@
     da3_part = nt(dpre, w_in)
     da3 = scatter(da3_part.astype(BF16), "fsdp").astype(F32)
     layer_output = (h2 + scatter(out_part.astype(BF16), "fsdp").astype(F32)).astype(BF16)
-    g_out = tn(act, g_all)
-    g_in = lax.all_to_all(tn(a3_all, dpre).astype(BF16), "fsdp", split_axis=0, concat_axis=1, tiled=True)
+    g_out = tn(act, g_all).astype(BF16)
+    g_in = tn(a3_all, dpre).astype(BF16)
     dx, gg3 = norm_back(h2, gains[2], da3)
     dh2 = grad.astype(F32) + dx
     branch2 = dh2.astype(BF16)
@@ -915,30 +1129,27 @@
     dx, gg1 = norm_back(tok_wide, gains[0], da1)
     grad_tokens = (dh1 + dx).astype(BF16)
     grad_memory = (nt(dk2, w_mem[:, :D]) + nt(dv2, w_mem[:, D:])).astype(BF16)
-    full = jnp.concatenate(
-        [
-            tn(a1, dq1),
-            tn(a1, dk1),
-            tn(a1, dv1),
-            tn(o1, branch1),
-            tn(a2, dq2),
-            tn(mem, dk2),
-            tn(mem, dv2),
-            tn(o2, branch2),
-        ],
-        1,
-    ).astype(BF16)
-    mine = scatter(full, "fsdp")
-    quarter = mine.shape[0]
-    mine = jnp.concatenate([mine, g_in, g_out.astype(BF16).reshape(quarter, -1)], 1)
-    total = lax.psum(mine, "ctx").astype(F32)
-    cut = lambda i: total[:, i * D : (i + 1) * D]
-    small = jnp.concatenate([jnp.stack([gg1, gg2, gg3]), jnp.pad(g_bias.T, ((0, 0), (0, D - BUCKETS)))], 0)
-    small = lax.psum(small, ("ctx", "fsdp"))
+    quarter, eighth = self_query.shape[0], position_bias.shape[0]
+    small = jnp.concatenate(
+        [jnp.stack([gg1, gg2, gg3]), jnp.pad(g_bias, ((0, 0), (0, D - HEADS)))], 0
+    )
+    small = jnp.pad(small, ((0, -small.shape[0] % 8), (0, 0)))
+    pairs = [
+        (a1, dq1),
+        (a1, dk1),
+        (a1, dv1),
+        (o1, branch1),
+        (a2, dq2),
+        (mem, dk2),
+        (mem, dv2),
+        (o2, branch2),
+    ]
+    total, small = reduce_grads(peers, pairs, g_in, g_out, small)
+    total = total.astype(F32)
     f = lax.axis_index("fsdp")
     gain = lambda i: lax.dynamic_slice_in_dim(small[i], f * quarter, quarter)
-    eighth = position_bias.shape[0]
-    bias_out = lax.dynamic_slice_in_dim(small[3:].T, f * eighth, eighth)
+    bias_out = lax.dynamic_slice_in_dim(small[3:], f * eighth, eighth)[:, :HEADS]
+    count = len(pairs)
     return (
         layer_output[None],
         grad_tokens[None],
@@ -947,9 +1158,9 @@
         gain(1),
         gain(2),
         bias_out,
-        *[cut(i) for i in range(8)],
-        total[:, 8 * D : 12 * D],
-        total[:, 12 * D :].reshape(-1, D),
+        *[total[i] for i in range(count)],
+        jnp.concatenate([total[count + i] for i in range(WAYS)], 1),
+        total[count + WAYS :].reshape(-1, D),
     )
 
 

time: 960 us -> 777 us (0.81)
  waiting for transfers between devices: 491 us -> 267 us
  Pallas kernels: 111 us -> 275 us
  local copies, waits for them, and re-layouts: 76.5 us -> 30.8 us
  blocking collectives: 149 us -> 106 us
  other arithmetic: 45.1 us -> 32.2 us
  matrix products: 45.3 us -> 34.5 us
    psum x1 -> x0, waiting for transfers between devices: 157 us -> none  [shards(): total = lax.psum(mine, 'ctx').astype(F32)]
    pallas_call x0 -> x1, Pallas kernels: none -> 155 us  [reduce_grads(): pl.pallas_call(functools.partial(reduce_kernel, peers, left_index), name=...]
    unnamed x14 -> x11, waiting for transfers between devices: 52.9 us -> 1.37 us
    psum x1 -> x0, blocking collectives: 43.3 us -> none  [shards(): small = lax.psum(small, ('ctx', 'fsdp'))]
    unnamed x126 -> x100, local copies, waits for them, and re-layouts: 39.6 us -> 2.9 us
    concatenate x2, other arithmetic: 16.1 us -> 1.71 us  [the longest x1 1.69 us: shards(): jnp.concatenate([total[count + i] for i in range(WAYS)], 1)]
    dot_general x10 -> x2, matrix products: 19.1 us -> 5.13 us  [tn(): lax.dot_general(a, b, (((0,), (0,)), ((), ())), preferred_element_type=F32)]
  transfers between devices with their start and end apart: 17 -> 14, of which waited for: 13 -> 10; matrix products, arithmetic and copies ran while one was open for 7% -> 8% of each run, Pallas kernels for 3% -> 4%
where the time goes in v2:
time: 777 us; the launch traced here: 773 us
  Pallas kernels  275 us (35%)
  waiting for transfers between devices  267 us (34%)
  blocking collectives  106 us (14%)
  matrix products  34.5 us (4%)
  other arithmetic  32.2 us (4%)
  local copies, waits for them, and re-layouts  30.8 us (4%)
  between operations  14.8 us (2%)
  starting transfers between devices  12.1 us (2%)
    pallas_call x1, Pallas kernels, reduce_grads(): pl.pallas_call(functools.partial(reduce_kernel, peers, left_index), name=...  155 us
    all_gather x8, waiting for transfers between devices, gather(): return lax.all_gather(x, axis_name, axis=axis, tiled=True)  117 us
    reduce_scatter x3, waiting for transfers between devices, scatter(): return lax.psum_scatter(x, axis_name, scatter_dimension=axis, tiled=True)  114 us
    all_gather x6, blocking collectives, gather(): return lax.all_gather(x, axis_name, axis=axis, tiled=True)  106 us
    pallas_call x1, Pallas kernels, cross_backward(): pl.pallas_call(cross_backward_kernel, name='cross_backward', out_shape=[s...  34.2 us
    all_to_all x2, waiting for transfers between devices, shards(): lax.all_to_all(x.reshape(peers, rows, x.shape[-1]), 'ctx', 0, 0)  34.2 us
    pallas_call x1, Pallas kernels, self_backward(): pl.pallas_call(kern, name='self_backward', out_shape=[sds((rows, D), BF16...  28.4 us
    pallas_call x1, Pallas kernels, cross_forward(): pl.pallas_call(cross_forward_kernel, name='cross_forward', out_shape=[sds...  27.8 us
  transfers between devices with their start and end apart: 14, of which 10 were waited for; matrix products, arithmetic and copies ran while one was open for 8% of the time, Pallas kernels for 4%

profile of v2, /device:TPU:0, one launch (start us, length us, event | category | flops | bytes accessed | tf_op | source)
XLA Modules:
  0.0 772.5 jit_solution(16050947688503733750)
XLA Ops:
  12.3 6.1 all-gather.2
  20.6 5.4 all_gather.45
  28.4 12.9 %bias_tables.1 = (bf16[2,12,64,2048]{3,2,1,0:T(8,128)(2,1)}, bf16[2,12,64,2048]{3,2,1,0:T(8,128)(2,1)}) custom-call(f32[16,2048]{1,0:T(8,128)} %pad.42.table, f32[16,2048]{1,0:T(8,128)} %pad.44.back_table), custom_call_target="tpu_custom_call" | custom-call | tf_op jit(solution)/shard_map/bias_tables/pallas_call | solution.py:66
  44.5 39.2 %all-gather.26.cloned.1.call-done = bf16[1,1024,768]{2,1,0:T(8,128)(2,1)} async-done(((bf16[1,128,768]{2,1,0:T(8,128)(2,1)}), bf16[1,1024,768]{2,1,0:T(8,128)(2,1)}) %all-gather.26.cloned.1.call-update) | async-done | bytes 1572880 | tf_op jit(solution)/shard_map/all_gather | solution.py:1023
  83.7 31.7 %all-gather.12.cloned.1.call-done.w = bf16[768,2304]{1,0:T(8,128)(2,1)} async-done(((bf16[192,2304]{1,0:T(8,128)(2,1)}), bf16[768,2304]{1,0:T(8,128)(2,1)}) %all-gather.12.cloned.1.call-update) | async-done | bytes 3538960 | tf_op jit(solution)/shard_map/all_gather | solution.py:1023
  115.4 17.1 %self_forward.1 = (bf16[1024,768]{1,0:T(8,128)(2,1)}, bf16[1024,768]{1,0:T(8,128)(2,1)}, bf16[1024,768]{1,0:T(8,128)(2,1)}, bf16[128,768]{1,0:T(8,128)(2,1)}, f3...) custom-call(s32[16]{0:T(128)} %order.3, ...), custom_call_target="tpu_custom_call" | custom-call | tf_op jit(solution)/shard_map/self_forward/pallas_call | solution.py:149
  136.2 4.3 select_reduce_fusion
  140.6 8.0 %select_select_fusion = s32[640]{0:T(1024)S(1)} fusion(pred[640]{0:T(1024)(128)(4,1)S(1)} %get-tuple-element.125, pred[640]{0:T(1024)(128)(4,1)S(1)} %get-tuple-element.126, pred[640]{0:T(1024)(128)(4,1)S(1)} %get-tuple-element.127, pred[640]{0:T(1024)(128)(4,1)S(1)} %get-tuple-element.128, pred[640]{0:T(1024)(128)(4,1)S(1)} %get-tuple-element.129, ...), kind=kLoop, calls=%fused_computation.145 | loop fusion | flops 8320 | bytes 13492 | tf_op jit(solution)/shard_map/jit(_take)/gather | solution.py:1079
  154.3 34.1 %all-gather.16.cloned.1.call-done.q_all = bf16[1024,768]{1,0:T(8,128)(2,1)} async-done(((bf16[128,768]{1,0:T(8,128)(2,1)}), bf16[1024,768]{1,0:T(8,128)(2,1)}) %all-gather.16.cloned.1.call-update) | async-done | bytes 1572880 | tf_op jit(solution)/shard_map/all_gather | solution.py:1023
  188.4 27.8 %cross_forward.1 = (bf16[1024,768]{1,0:T(8,128)(2,1)}, f32[1024,128]{1,0:T(8,128)}) custom-call(bf16[1024,768]{1,0:T(8,128)(2,1)} %all-gather.16.cloned.1.call-done.q_all, bf16[640,768]{1,0:T(8,128)(2,1)} %get-tuple-element.87.k2, bf16[640,768]{1,0:T(8,128)(2,1)} %get-tuple-element.86.v2, f32[1,640]{1,0:T(1,128)} %compare_select_fusion.2.mask), custom_call_target="tpu_custom_call" | custom-call | tf_op jit(solution)/shard_map/cross_forward/pallas_call | solution.py:186
  222.2 11.8 %all-to-all-done = f32[8,128,128]{2,1,0:T(8,128)S(1)} async-done(((f32[8,128,128]{2,1,0:T(8,128)}), f32[8,128,128]{2,1,0:T(8,128)S(1)}, u32[]{:S(2)}, u32[]{:S(2)}) %all-to-all-start) | async-done | bytes 524320 | tf_op jit(solution)/shard_map/all_to_all | solution.py:1082
  241.3 9.0 %all-gather.1 = bf16[1,512,768]{2,1,0:T(8,128)(2,1)} all-gather(bf16[1,128,768]{2,1,0:T(8,128)(2,1)S(1)} %copy-done.10), channel_id=3, replica_groups=mesh['ctx'=8,'fsdp'=4] {'fsdp'}, dimensions={1}, use_global_device_ids=true | all-gather | bytes 983040 | tf_op jit(solution)/shard_map/all_gather | solution.py:1023
  252.6 22.3 %all-to-all-done.1 = bf16[8,128,768]{1,2,0:T(8,128)(2,1)S(1)} async-done(((bf16[8,128,768]{1,2,0:T(8,128)(2,1)}), bf16[8,128,768]{1,2,0:T(8,128)(2,1)S(1)}, u32[]{:S(2)}, u32[]{:S(2)}) %all-to-all-start.1) | async-done | bytes 1572896 | tf_op jit(solution)/shard_map/all_to_all | solution.py:1082
  274.9 4.3 all-to-all-start.2
  282.0 18.5 %all_gather.50 = bf16[512,768]{1,0:T(8,128)(2,1)} all-gather(bf16[128,768]{1,0:T(8,128)(2,1)S(1)} %multiply_convert_fusion.1), channel_id=1, replica_groups=mesh['ctx'=8,'fsdp'=4] {'fsdp'}, dimensions={0}, use_global_device_ids=true | all-gather | bytes 983040 | tf_op jit(solution)/shard_map/all_gather | solution.py:1023
  308.5 21.5 %reduce-scatter.6.cloned.1.call-done = bf16[128,768]{1,0:T(8,128)(2,1)} async-done(((bf16[512,768]{1,0:T(8,128)(2,1)}), bf16[128,768]{1,0:T(8,128)(2,1)}) %reduce-scatter.6.cloned.1.call-update) | async-done | bytes 196624 | tf_op jit(solution)/shard_map/reduce_scatter | solution.py:1027
  336.3 32.9 %all_gather.53.stats = f32[32,1024]{1,0:T(8,128)} all-gather(f32[32,128]{1,0:T(8,128)S(1)} %fusion.54), channel_id=1, replica_groups=mesh['ctx'=8,'fsdp'=4] {'ctx'}, dimensions={1}, use_global_device_ids=true | all-gather | bytes 147456 | tf_op jit(solution)/shard_map/all_gather | solution.py:1023
  369.1 9.2 %all-gather.22.cloned.1.call-done.do_all = bf16[1024,768]{1,0:T(8,128)(2,1)} async-done(((bf16[128,768]{1,0:T(8,128)(2,1)}), bf16[1024,768]{1,0:T(8,128)(2,1)}) %all-gather.22.cloned.1.call-update) | async-done | bytes 1572880 | tf_op jit(solution)/shard_map/all_gather | solution.py:1023
  378.4 34.2 %cross_backward.1 = (f32[1024,768]{1,0:T(8,128)}, bf16[640,768]{1,0:T(8,128)(2,1)}, bf16[640,768]{1,0:T(8,128)(2,1)}) custom-call(bf16[1024,768]{1,0:T(8,128)(2,1)} %all-gather.16.cloned.1.call-done.q_all, bf16[1024,768]{1,0:T(8,128)(2,1)} %all-gather.22.cloned.1.call-done.do_all, f32[32,1024]{1,0:T(8,128)} %all_gather.53.stats, ...), custom_call_target="tpu_custom_call" | custom-call | tf_op jit(solution)/shard_map/cross_backward/pallas_call | solution.py:229
  416.4 69.9 %reduce-scatter.8.cloned.1.call-done = f32[128,768]{1,0:T(8,128)} async-done(((f32[1024,768]{1,0:T(8,128)}), f32[128,768]{1,0:T(8,128)}) %reduce-scatter.8.cloned.1.call-update) | async-done | bytes 393232 | tf_op jit(solution)/shard_map/reduce_scatter | solution.py:1027
  489.3 22.5 %reduce-scatter.4.cloned.1.call-done = bf16[128,768]{1,0:T(8,128)(2,1)} async-done(((bf16[512,768]{1,0:T(8,128)(2,1)}), bf16[128,768]{1,0:T(8,128)(2,1)}) %reduce-scatter.4.cloned.1.call-update) | async-done | bytes 196624 | tf_op jit(solution)/shard_map/reduce_scatter | solution.py:1027
  527.0 34.3 %all_gather.55.stat_slot = f32[1024,128]{1,0:T(8,128)} all-gather(f32[128,128]{1,0:T(8,128)S(1)} %pad.48.stat_own), channel_id=1, replica_groups=mesh['ctx'=8,'fsdp'=4] {'ctx'}, dimensions={0}, use_global_device_ids=true | all-gather | bytes 589824 | tf_op jit(solution)/shard_map/all_gather | solution.py:1023
  564.4 28.4 %self_backward.1 = (bf16[128,768]{1,0:T(8,128)(2,1)}, bf16[128,768]{1,0:T(8,128)(2,1)}, bf16[128,768]{1,0:T(8,128)(2,1)}, f32[16,2048]{1,0:T(8,128)}) custom-call(s32[16]{0:T(128)} %order.3, s32[2]{0:T(128)} %dynamic_slice.21.own, bf16[1024,768]{1,0:T(8,128)(2,1)} %get-tuple-element.45.q_nat, bf16[1024,768]{1,0:T(8,128)(2,1)} %get-tuple-element.46.k_nat, ...), custom_call_target="tpu_custom_call" | custom-call | tf_op jit(solution)/shard_map/self_backward/pallas_call | solution.py:308
  598.0 154.7 %reduce_grads.1 = (bf16[16,192,768]{2,1,0:T(8,128)(2,1)}, f32[40,768]{1,0:T(8,128)}) custom-call(bf16[128,768]{1,0:T(8,128)(2,1)} %get-tuple-element.56.refs_0_, bf16[128,768]{1,0:T(8,128)(2,1)} %get-tuple-element.49.refs_1_, bf16[128,768]{1,0:T(8,128)(2,1)} %get-tuple-element.57.refs_2_, bf16[640,768]{1,0:T(8,128)(2,1)} %bitcast.142, ...), custom_call_target="tpu_custom_call" | custom-call | tf_op jit(solution)/shard_map/reduce_grads/pallas_call | solution.py:990
  (224 shorter events, 97.5 us)
Async XLA Ops:
  7.2 295.7 %copy-start = (bf16[768,768]{1,0:T(8,128)(2,1)S(1)}, bf16[768,768]{1,0:T(8,128)(2,1)}, u32[]{:S(2)}) copy-start(bf16[768,768]{1,0:T(8,128)(2,1)} %param.38) | copy-start | bytes 3538948
  7.2 34.0 %all-gather.14.cloned.1.call-start = ((), (), s32[]{:S(2)}) async-start(), calls=%async_computation.7 | async-start | bytes 2949120 | tf_op jit(solution)/shard_map/all_gather | solution.py:1023
  9.4 74.3 %all-gather.26.cloned.1.call-start = ((), (), s32[]{:S(2)}) async-start(), calls=%async_computation.16 | async-start | bytes 1769472 | tf_op jit(solution)/shard_map/all_gather | solution.py:1023
  10.1 105.3 %all-gather.12.cloned.1.call-start = ((), (), s32[]{:S(2)}) async-start(), calls=%async_computation.6 | async-start | bytes 4423680 | tf_op jit(solution)/shard_map/all_gather | solution.py:1023
  11.2 137.9 %all-gather.18.cloned.1.call-start = ((), (), s32[]{:S(2)}) async-start(), calls=%async_computation.9 | async-start | bytes 2949120 | tf_op jit(solution)/shard_map/all_gather | solution.py:1023
  12.2 176.2 %all-gather.16.cloned.1.call-start = ((), (), s32[]{:S(2)}) async-start(), calls=%async_computation.8 | async-start | bytes 1769472 | tf_op jit(solution)/shard_map/all_gather | solution.py:1023
  115.4 20.1 %copy-start.28 = (s32[1,20]{1,0:T(1,128)S(1)}, s32[1,20]{1,0:T(1,128)}, u32[]{:S(2)}) copy-start(s32[1,20]{1,0:T(1,128)} %param.24) | copy-start | bytes 244
  216.1 17.9 %all-to-all-start = ((f32[8,128,128]{2,1,0:T(8,128)}), f32[8,128,128]{2,1,0:T(8,128)S(1)}, u32[]{:S(2)}, u32[]{:S(2)}) async-start(f32[8,128,128]{2,1,0:T(8,128)} %bitcast.143), calls=%async_computation | async-start | bytes 1048576 | tf_op jit(solution)/shard_map/all_to_all | solution.py:1082
  234.1 40.8 %all-to-all-start.1 = ((bf16[8,128,768]{1,2,0:T(8,128)(2,1)}), bf16[8,128,768]{1,2,0:T(8,128)(2,1)S(1)}, u32[]{:S(2)}, u32[]{:S(2)}) async-start(bf16[8,128,768]{1,2,0:T(8,128)(2,1)} %copy.94), calls=%async_computation.1 | async-start | bytes 3145728 | tf_op jit(solution)/shard_map/all_to_all | solution.py:1082
  237.7 42.3 %all-gather.20.cloned.1.call-start = ((), (), s32[]{:S(2)}) async-start(), calls=%async_computation.10 | async-start | bytes 1474560 | tf_op jit(solution)/shard_map/all_gather | solution.py:1023
  274.9 25.6 %all-to-all-start.2 = ((bf16[192,4,768]{2,0,1:T(8,128)(2,1)}), bf16[192,4,768]{2,0,1:T(8,128)(2,1)}, u32[]{:S(2)}, u32[]{:S(2)}) async-start(bf16[192,4,768]{2,0,1:T(8,128)(2,1)} %bitcast.133), calls=%async_computation.2 | async-start | bytes 2359296 | tf_op jit(solution)/shard_map/all_to_all | solution.py:1065
  279.2 50.8 %reduce-scatter.6.cloned.1.call-start = ((), (), s32[]{:S(2)}) async-start(), calls=%async_computation.12 | async-start | bytes 983040 | tf_op jit(solution)/shard_map/reduce_scatter | solution.py:1027
  280.0 20.5 %copy-start.7 = (bf16[128,768]{1,0:T(8,128)(2,1)}, bf16[128,768]{1,0:T(8,128)(2,1)S(1)}, u32[]{:S(2)}) copy-start(bf16[128,768]{1,0:T(8,128)(2,1)S(1)} %convert_element_type.111.refs_4_) | copy-start | bytes 589828
  308.4 23.9 %copy-start.4 = (bf16[768,768]{1,0:T(8,128)(2,1)S(1)}, bf16[768,768]{1,0:T(8,128)(2,1)}, u32[]{:S(2)}) copy-start(bf16[768,768]{1,0:T(8,128)(2,1)} %all-gather.20.cloned.1.call-done) | copy-start | bytes 3538948
  308.4 70.0 %all-gather.22.cloned.1.call-start = ((), (), s32[]{:S(2)}) async-start(), calls=%async_computation.13 | async-start | bytes 1769472 | tf_op jit(solution)/shard_map/all_gather | solution.py:1023
  333.7 152.5 %reduce-scatter.8.cloned.1.call-start = ((), (), s32[]{:S(2)}) async-start(), calls=%async_computation.14 | async-start | bytes 3538944 | tf_op jit(solution)/shard_map/reduce_scatter | solution.py:1027
  412.7 99.1 %reduce-scatter.4.cloned.1.call-start = ((), (), s32[]{:S(2)}) async-start(), calls=%async_computation.11 | async-start | bytes 983040 | tf_op jit(solution)/shard_map/reduce_scatter | solution.py:1027
  416.2 95.6 %copy-start.9 = (bf16[128,768]{1,0:T(8,128)(2,1)S(1)}, bf16[128,768]{1,0:T(8,128)(2,1)}, u32[]{:S(2)}) copy-start(bf16[128,768]{1,0:T(8,128)(2,1)} %reduce-scatter.6.cloned.1.call-done) | copy-start | bytes 589828
  416.2 95.6 %copy-start.11 = (bf16[1,128,768]{2,1,0:T(8,128)(2,1)S(1)}, bf16[1,128,768]{2,1,0:T(8,128)(2,1)}, u32[]{:S(2)}) copy-start(bf16[1,128,768]{2,1,0:T(8,128)(2,1)} %param.39) | copy-start | bytes 589828
  416.2 148.2 %all-gather.24.cloned.1.call-start = ((), (), s32[]{:S(2)}) async-start(), calls=%async_computation.15 | async-start | bytes 1769472 | tf_op jit(solution)/shard_map/all_gather | solution.py:1023
  487.2 24.5 %copy-start.21 = (bf16[128,768]{1,0:T(8,128)(2,1)}, bf16[128,768]{1,0:T(8,128)(2,1)S(1)}, u32[]{:S(2)}) copy-start(bf16[128,768]{1,0:T(8,128)(2,1)S(1)} %convert_element_type.124.refs_9_) | copy-start | bytes 589828
  489.2 24.5 %copy-start.19 = (bf16[128,768]{1,0:T(8,128)(2,1)S(1)}, bf16[128,768]{1,0:T(8,128)(2,1)}, u32[]{:S(2)}) copy-start(bf16[128,768]{1,0:T(8,128)(2,1)} %get-tuple-element.49.refs_1_) | copy-start | bytes 589828
  527.0 37.4 %copy-start.22 = (f32[128,128]{1,0:T(8,128)}, f32[128,128]{1,0:T(8,128)S(1)}, u32[]{:S(2)}) copy-start(f32[128,128]{1,0:T(8,128)S(1)} %pad.48.stat_own) | copy-start | bytes 196612
  564.4 29.6 %copy-start.3 = (bf16[768,2304]{1,0:T(8,128)(2,1)S(1)}, bf16[768,2304]{1,0:T(8,128)(2,1)}, u32[]{:S(2)}) copy-start(bf16[768,2304]{1,0:T(8,128)(2,1)} %all-gather.12.cloned.1.call-done.w) | copy-start | bytes 10616836
  (39 other events, 118.9 us)
Sparse Core Ops, SparseCore 0:
  10.2 27.0 all-gather.13
  39.5 44.1 all-gather.25
  85.8 29.5 all-gather.11
  117.4 24.0 all-gather.17
  144.1 44.1 all-gather.15
  239.8 18.8 all-gather.19
  308.5 21.4 reduce-scatter.5
  333.8 44.5 all-gather.21
  412.8 73.3 reduce-scatter.7
  489.3 22.3 reduce-scatter.3
  516.5 47.8 all-gather.23

commit v3 on v2

--- a/solution.py
+++ b/solution.py
@@ -48,36 +48,19 @@
         x = jnp.where(row & bit != 0, pltpu.roll(x, (sign * bit) % x.shape[1], 1), x)
     return x
 
-def bias_tables_kernel(table, back_table, ahead, behind):
-    full = table.shape[1]
-    def head(h, c):
-        for src, out in ((table, ahead), (back_table, behind)):
-            base = shear(pltpu.roll(jnp.broadcast_to(src[pl.ds(h, 1), :], (8, full)), 1, 1), 1)
-            for parity in range(2):
-                for i in range(PIECE // 16):
-                    both = [pltpu.roll(base, (8 * g - 64 * parity) % full, 1) if (8 * g - 64 * parity) % full else base
-                            for g in (2 * i, 2 * i + 1)]
-                    out[parity, h, 16 * i:16 * i + 16, :] = jnp.concatenate(both, 0).astype(BF16)
-        return c
-    lax.fori_loop(0, HEADS, head, 0)
-
-def bias_tables(table, back_table):
-    full = table.shape[1]
-    return pl.pallas_call(
-        bias_tables_kernel,
-        name="bias_tables",
-        out_shape=[sds((2, HEADS, PIECE, full), BF16)] * 2,
-        in_specs=[full_spec()] * 2,
-        out_specs=[full_spec()] * 2,
-        compiler_params=pltpu.CompilerParams(vmem_limit_bytes=VMEM_LIMIT),
-    )(table, back_table)
-
 def piece_bias(tables, h, piece, length):
     start = pl.multiple_of(length - (piece + piece % 2) * PIECE, LANES)
     return tables[piece % 2, h, :, pl.ds(start, length)].astype(F32)
 
 def bias_rows(tables, h, own, count, length):
     return jnp.concatenate([piece_bias(tables, h, own[i], length) for i in range(count)], 0)
+
+def bias_at(tables, h, own, count, length):
+    parts = []
+    for i in range(count):
+        parts.append(tables[own[i, 1], h, :, pl.ds(own[i, 2] * LANES, length)].astype(F32))
+    return jnp.concatenate(parts, 0)
+
 
 def add_diagonals(acc, block, piece):
     rows, length = block.shape
@@ -89,73 +72,12 @@
     where = (piece % 2, slice(None), pl.ds(start, length + LANES))
     acc[where] += total
 
-def self_forward_kernel(order, own, tok_all, tok, w, gains, table, wo, wq2,
-                        q_nat, k_nat, v_nat, o1, h1, a1, a2, q2, lse, inv, q_own):
-    length = tok_all.shape[0]
-    rows = tok.shape[0]
-    slots, mine = length // PIECE, rows // PIECE
-    for s in range(slots):
-        inv[order[s]] = s
-    per = BLOCK // PIECE
-
-    def tile(t, c):
-        parts = [tok_all[pl.ds(pl.multiple_of(inv[t * per + i] * PIECE, PIECE), PIECE), :] for i in range(per)]
-        a = normed(jnp.concatenate(parts, 0).astype(F32), gains[0:1, :]).astype(BF16)
-        dst = pl.ds(pl.multiple_of(t * BLOCK, BLOCK), BLOCK)
-        for j, out in enumerate((q_nat, k_nat, v_nat)):
-            out[dst, :] = nn(a, w[:, j * D:(j + 1) * D]).astype(BF16)
-        return c
-
-    lax.fori_loop(0, length // BLOCK, tile, 0)
-    for i in range(mine):
-        q_own[i * PIECE:(i + 1) * PIECE, :] = q_nat[pl.ds(pl.multiple_of(own[i] * PIECE, PIECE), PIECE), :]
-    a1[...] = normed(tok[...].astype(F32), gains[0:1, :]).astype(BF16)
-    lane = lax.broadcasted_iota(jnp.int32, (rows, length), 1)
-    limit = jnp.concatenate([jnp.full((PIECE, 1), (own[i] // per + 1) * BLOCK, jnp.int32) for i in range(mine)], 0)
-    visible = lane < limit
-    stat_lane = lax.broadcasted_iota(jnp.int32, (rows, LANES), 1)
-
-    def pair(p, stats):
-        sl = lanes_of(p)
-        q, k, v = q_own[:, sl], k_nat[:, sl], v_nat[:, sl]
-        total = jnp.zeros((rows, LANES), F32)
-        for half in range(2):
-            h = 2 * p + half
-            s = jnp.where(visible, nt(q, half_mask(k, half)) + bias_rows(table, h, own, mine, length), NEGATIVE)
-            m = jnp.max(s, axis=1, keepdims=True)
-            e = jnp.exp(s - m)
-            l = jnp.sum(e, axis=1, keepdims=True)
-            total += nn(e.astype(BF16), half_mask(v, half)) / l
-            stats = jnp.where(stat_lane == h, m + jnp.log(l), stats)
-        o1[:, sl] = total.astype(BF16)
-        return stats
-
-    lse[...] = lax.fori_loop(0, PAIRS, pair, jnp.zeros((rows, LANES), F32))
-    h = tok[...].astype(F32) + nn(o1[...], wo[...])
-    h1[...] = h
-    a = normed(h, gains[1:2, :]).astype(BF16)
-    a2[...] = a
-    q2[...] = nn(a, wq2[...]).astype(BF16)
-
 def full_spec():
     return pl.BlockSpec(memory_space=pltpu.VMEM)
 def smem_spec():
     return pl.BlockSpec(memory_space=pltpu.SMEM)
 def sds(shape, dtype):
     return jax.ShapeDtypeStruct(shape, dtype)
-
-def self_forward(order, own, tok_all, tok, w, gains, table, wo, wq2):
-    length, rows = tok_all.shape[0], tok.shape[0]
-    return pl.pallas_call(
-        self_forward_kernel,
-        name="self_forward",
-        out_shape=[sds((length, D), BF16)] * 3 + [sds((rows, D), BF16), sds((rows, D), F32), sds((rows, D), BF16),
-                   sds((rows, D), BF16), sds((rows, D), BF16), sds((rows, LANES), F32)],
-        in_specs=[smem_spec()] * 2 + [full_spec()] * 7,
-        out_specs=[full_spec()] * 9,
-        scratch_shapes=[pltpu.SMEM((length // PIECE,), jnp.int32), pltpu.VMEM((rows, D), BF16)],
-        compiler_params=pltpu.CompilerParams(vmem_limit_bytes=VMEM_LIMIT),
-    )(order, own, tok_all, tok, w, gains, table, wo, wq2)
 
 def cross_forward_kernel(q_all, k2, v2, mask, o, lse):
     rows = q_all.shape[0]
@@ -849,6 +771,219 @@
     return [pltpu.SemaphoreType.DMA((count,)), pltpu.SemaphoreType.DMA((count,))]
 
 
+class Wire:
+    def __init__(self, peers):
+        self.at = Place(peers)
+        self.depth = self.at.depth
+        self.sent = []
+
+    def go(self, copy):
+        copy.start()
+        self.sent.append(copy)
+
+    def drain(self):
+        for copy in self.sent:
+            copy.wait_send()
+
+    def partners(self):
+        at = self.at
+        return (
+            [at.group(d) for d in range(1, WAYS)]
+            + [at.beside]
+            + [at.column(at.ahead(d)) for d in range(1, self.depth)]
+        )
+
+    def near(self, step):
+        a, last = self.at.a, self.depth - 1
+        low = jnp.where(step - 1 < a, step - 1, step)
+        mirrored = jnp.where(step - 1 < last - a, step - 1, step)
+        return jnp.where(2 * a < last, low, last - mirrored)
+
+    def slot(self, buf, c):
+        if len(buf.shape) == 3:
+            return buf.at[c]
+        rows = buf.shape[0] // (2 * self.depth)
+        return buf.at[pl.ds(pl.multiple_of(c * rows, rows), rows)]
+
+    def spread(self, src, buf, sem):
+        at = self.at
+        slot = self.slot(buf, at.c)
+        self.go(remote(src, slot, sem, at.a, at.beside))
+        for step in range(1, self.depth):
+            self.go(remote(src, slot, sem, self.depth + at.a, at.column(self.near(step))))
+
+    def relay(self, buf, sem, step):
+        a = self.near(step)
+        slot = self.slot(buf, a * 2 + self.at.b)
+        remote(slot, slot, sem, self.depth + a, self.at.beside).wait_recv()
+        self.go(remote(slot, slot, sem, a, self.at.beside))
+
+    def from_beside(self, buf, sem, a):
+        slot = self.slot(buf, a * 2 + 1 - self.at.b)
+        remote(slot, slot, sem, a, self.at.beside).wait_recv()
+
+    def shard(self, full, f):
+        quarter = full.shape[0] // WAYS
+        return full.at[pl.ds(pl.multiple_of(f * quarter, quarter), quarter)]
+
+    def weight_start(self, src, full, sem, i):
+        at = self.at
+        slot = self.shard(full, at.f)
+        slot[...] = src[...]
+        self.go(remote(src, slot, sem, 3 * i, at.across))
+        self.go(remote(src, slot, sem, 3 * i + 1, at.core))
+
+    def weight_relay(self, full, sem, i):
+        at = self.at
+        slot = self.shard(full, (1 - at.x) * 2 + at.k)
+        remote(slot, slot, sem, 3 * i, at.across).wait_recv()
+        self.go(remote(slot, slot, sem, 3 * i + 2, at.core))
+
+    def weight_ready(self, full, sem, i):
+        at = self.at
+        slot = self.shard(full, at.x * 2 + 1 - at.k)
+        remote(slot, slot, sem, 3 * i + 1, at.core).wait_recv()
+        slot = self.shard(full, (1 - at.x) * 2 + 1 - at.k)
+        remote(slot, slot, sem, 3 * i + 2, at.core).wait_recv()
+
+
+def fill_tables(table, out):
+    full = table.shape[1]
+
+    def head(h, c):
+        base = shear(pltpu.roll(jnp.broadcast_to(table[pl.ds(h, 1), :], (8, full)), 1, 1), 1)
+        for parity in range(2):
+            for i in range(PIECE // 16):
+                shifts = [(8 * g - 64 * parity) % full for g in (2 * i, 2 * i + 1)]
+                both = [pltpu.roll(base, s, 1) if s else base for s in shifts]
+                out[parity, h, 16 * i : 16 * i + 16, :] = jnp.concatenate(both, 0).astype(BF16)
+        return c
+
+    lax.fori_loop(0, HEADS, head, 0)
+
+
+N_FRONT = 7
+N_GAINS = 16
+
+
+def front_kernel(peers, *refs):
+    inv, own, tok, pack, buckets, buckets_back = refs[:6]
+    shards_in = refs[6 : 6 + N_FRONT]
+    (weights, gains, ahead, behind, q_nat, k_nat, v_nat, a1, o1, h1, a2, q2, lse) = refs[6 + N_FRONT : 19 + N_FRONT]
+    (tok_all, pack_all, table, q_own, *sem) = refs[19 + N_FRONT :]
+    sem_t, sem_w, sem_p = sem[0:2], sem[2:4], sem[4:6]
+    wire = Wire(peers)
+    at, depth = wire.at, wire.depth
+    rows = tok.shape[0]
+    length = peers * rows
+    mine, per = rows // PIECE, BLOCK // PIECE
+    greet(wire.partners())
+    for d in range(1, WAYS):
+        wire.go(remote(pack, pack_all.at[at.f], sem_p, d, at.group(d)))
+    wire.spread(tok, tok_all, sem_t)
+    for i in range(3):
+        wire.weight_start(shards_in[i], weights.at[i], sem_w, i)
+    wire.slot(tok_all, at.c)[...] = tok[...]
+    pack_all[at.f] = pack[...]
+    for d in range(1, WAYS):
+        slot = pack_all.at[lax.rem(at.f + WAYS - d, WAYS)]
+        remote(slot, slot, sem_p, d, at.group(WAYS - d)).wait_recv()
+    everything = pack_all[0].astype(F32) + pack_all[1].astype(F32) + pack_all[2].astype(F32) + pack_all[3].astype(F32)
+    gains[...] = everything[0:8, :]
+    bias = everything[N_GAINS:, 0:LANES].astype(BF16)
+    bucket = lax.broadcasted_iota(jnp.int32, (bias.shape[0], 2 * length), 0)
+    for line, out in ((buckets, ahead), (buckets_back, behind)):
+        hot = jnp.where(line[...] == bucket, 1.0, 0.0).astype(BF16)
+        table[...] = tn(bias, hot)[0:16, :]
+        fill_tables(table, out)
+    for step in range(1, depth):
+        wire.relay(tok_all, sem_t, step)
+    for i in range(3):
+        wire.weight_relay(weights.at[i], sem_w, i)
+    for i in range(3, N_FRONT):
+        wire.weight_start(shards_in[i], weights.at[i], sem_w, i)
+    first = gains[0:1, :]
+    a1[...] = normed(tok[...].astype(F32), first).astype(BF16)
+    for i in range(3):
+        wire.weight_ready(weights.at[i], sem_w, i)
+    for step in range(depth):
+        wire.from_beside(tok_all, sem_t, step)
+
+    def tile(t, c):
+        parts = []
+        for i in range(per):
+            parts.append(tok_all[pl.ds(inv[t * per + i] * PIECE, PIECE), :])
+        a = normed(jnp.concatenate(parts, 0).astype(F32), first).astype(BF16)
+        dst = pl.ds(pl.multiple_of(t * BLOCK, BLOCK), BLOCK)
+        for j, out in enumerate((q_nat, k_nat, v_nat)):
+            out[dst, :] = nn(a, weights[j]).astype(BF16)
+        return c
+
+    lax.fori_loop(0, length // BLOCK, tile, 0)
+    for i in range(mine):
+        q_own[i * PIECE : (i + 1) * PIECE, :] = q_nat[pl.ds(own[i, 0] * PIECE, PIECE), :]
+    wire.weight_relay(weights.at[3], sem_w, 3)
+    lane = lax.broadcasted_iota(jnp.int32, (rows, length), 1)
+    limit = jnp.concatenate([jnp.full((PIECE, 1), own[i, 3], jnp.int32) for i in range(mine)], 0)
+    visible = lane < limit
+    stat_lane = lax.broadcasted_iota(jnp.int32, (rows, LANES), 1)
+
+    def pair(p, stats):
+        sl = lanes_of(p)
+        q, k, v = q_own[:, sl], k_nat[:, sl], v_nat[:, sl]
+        total = jnp.zeros((rows, LANES), F32)
+        for half in range(2):
+            h = 2 * p + half
+            s = jnp.where(visible, nt(q, half_mask(k, half)) + bias_at(ahead, h, own, mine, length), NEGATIVE)
+            m = jnp.max(s, axis=1, keepdims=True)
+            e = jnp.exp(s - m)
+            l = jnp.sum(e, axis=1, keepdims=True)
+            total += nn(e.astype(BF16), half_mask(v, half)) / l
+            stats = jnp.where(stat_lane == h, m + jnp.log(l), stats)
+        o1[:, sl] = total.astype(BF16)
+        return stats
+
+    stats = lax.fori_loop(0, PAIRS // 2, pair, jnp.zeros((rows, LANES), F32))
+    wire.weight_relay(weights.at[4], sem_w, 4)
+    lse[...] = lax.fori_loop(PAIRS // 2, PAIRS, pair, stats)
+    wire.weight_relay(weights.at[5], sem_w, 5)
+    wire.weight_ready(weights.at[3], sem_w, 3)
+    h = tok[...].astype(F32) + nn(o1[...], weights[3])
+    h1[...] = h
+    a = normed(h, gains[1:2, :]).astype(BF16)
+    a2[...] = a
+    wire.weight_ready(weights.at[4], sem_w, 4)
+    q2[...] = nn(a, weights[4]).astype(BF16)
+    wire.weight_relay(weights.at[6], sem_w, 6)
+    for i in (5, 6):
+        wire.weight_ready(weights.at[i], sem_w, i)
+    wire.drain()
+
+
+def front(peers, inv, own, tok, pack, buckets, buckets_back, weight_shards):
+    rows = tok.shape[0]
+    length, depth = peers * rows, peers // 2
+    block = lambda dtype: sds((rows, D), dtype)
+    return pl.pallas_call(
+        functools.partial(front_kernel, peers),
+        name="front",
+        out_shape=[sds((N_FRONT, D, D), BF16), sds((8, D), F32)]
+        + [sds((2, HEADS, PIECE, 2 * length), BF16)] * 2
+        + [sds((length, D), BF16)] * 3
+        + [block(BF16), block(BF16), block(F32), block(BF16), block(BF16), sds((rows, LANES), F32)],
+        in_specs=[smem_spec()] * 2 + [full_spec()] * (4 + N_FRONT),
+        out_specs=[full_spec()] * 13,
+        scratch_shapes=[
+            pltpu.VMEM((length, D), BF16),
+            pltpu.VMEM((WAYS,) + pack.shape, BF16),
+            pltpu.VMEM((16, 2 * length), F32),
+            pltpu.VMEM((rows, D), BF16),
+        ]
+        + sems(2 * depth) + sems(3 * N_FRONT) + sems(WAYS),
+        compiler_params=pltpu.CompilerParams(collective_id=1, has_side_effects=True, vmem_limit_bytes=VMEM_LIMIT),
+    )(inv, own, tok, pack, buckets, buckets_back, *weight_shards)
+
+
 def reduce_kernel(peers, left_index, *refs):
     n_left = len(set(left_index))
     n_mats = len(left_index)
@@ -1055,26 +1190,33 @@
     peers = length // rows
     index = lax.axis_index("ctx")
     own = lax.dynamic_slice_in_dim(piece_order, index * (rows // PIECE), rows // PIECE)
-    tok_all = gather(tok, "ctx")
-    w_self = gather(jnp.concatenate([self_query, self_attention_key, self_value], 1), "fsdp")
-    w_mid = gather(jnp.concatenate([self_output, cross_query], 1), "fsdp")
-    w_mem = gather(jnp.concatenate([cross_key, cross_value], 1), "fsdp")
+    f = lax.axis_index("fsdp")
+    quarter, eighth = self_query.shape[0], position_bias.shape[0]
+    slots_all = jnp.arange(piece_order.shape[0], dtype=jnp.int32)
+    inv = jnp.sum(jnp.where(piece_order[None, :] == slots_all[:, None], slots_all[None, :], 0), axis=1)
+    own_facts = jnp.stack(
+        [own, own % 2, (length - (own + own % 2) * PIECE) // LANES, (own * PIECE // BLOCK + 1) * BLOCK], axis=1
+    )
+    pack = jnp.zeros((N_GAINS + BUCKETS, D), BF16)
+    pack = lax.dynamic_update_slice(pack, jnp.stack([self_gain, cross_gain, hidden_gain]), (0, f * quarter))
+    pack = lax.dynamic_update_slice(pack, position_bias, (N_GAINS + f * eighth, 0))
+    buckets = jnp.pad(bucket_table, (0, 1), constant_values=-1)[None]
+    buckets_back = jnp.pad(bucket_table[::-1], (0, 1), constant_values=-1)[None]
+    hot = (buckets == jnp.arange(BUCKETS, dtype=jnp.int32)[:, None]).astype(F32)
+    weights, gains, ahead, behind, q1_nat, k1_nat, v1_nat, a1, o1, h1, a2, q2, lse1 = front(
+        peers,
+        inv,
+        own_facts,
+        tok,
+        pack,
+        buckets,
+        buckets_back,
+        [self_query, self_attention_key, self_value, self_output, cross_query, cross_key, cross_value],
+    )
+    wq1, wk1, wv1, wo, wq2, wk2, wv2 = [weights[i] for i in range(N_FRONT)]
     w_co = gather(cross_output, "fsdp")
-    gains = gather(jnp.stack([self_gain, cross_gain, hidden_gain]), "fsdp", 1).astype(F32)
-    bias_rows_all = gather(position_bias, "fsdp")
     w_in = lax.all_to_all(hidden_in, "fsdp", split_axis=1, concat_axis=0, tiled=True)
-    wo, wq2 = w_mid[:, :D], w_mid[:, D:]
-    buckets = jnp.arange(BUCKETS, dtype=jnp.int32)[:, None]
-    hot = (bucket_table[None, :] == buckets).astype(BF16)
-    hot = jnp.pad(hot, ((0, 0), (0, 1)))
-    hot_back = jnp.pad(hot[:, -2::-1], ((0, 0), (0, 1)))
-    spread = lambda x: jnp.pad(jnp.einsum("lr,lh->hr", x, bias_rows_all, preferred_element_type=F32), ((0, 4), (0, 0)))
-    ahead, behind = bias_tables(spread(hot), spread(hot_back))
-    q1_nat, k1_nat, v1_nat, o1, h1, a1, a2, q2, lse1 = self_forward(
-        piece_order, own, tok_all, tok, w_self, jnp.pad(gains, ((0, 5), (0, 0))), ahead, wo, wq2
-    )
-    kv2 = project(mem, w_mem).astype(BF16)
-    k2, v2 = kv2[:, :D], kv2[:, D:]
+    k2, v2 = project(mem, wk2).astype(BF16), project(mem, wv2).astype(BF16)
     slot = index * slots + jnp.arange(slots, dtype=jnp.int32)
     hidden = jnp.where(slot % PLEN < jnp.take(passage_lengths[0], slot // PLEN), 0.0, NEGATIVE)
     q2_all = gather(q2, "ctx")
@@ -1122,14 +1264,13 @@
         piece_order, own, q1_nat, k1_nat, v1_nat, do1_all, do1, stat1_all, stat1, ahead, behind
     )
     g_bias = jnp.einsum(
-        "hr,lr->lh", diag[:HEADS], hot.astype(F32), precision=lax.Precision.HIGHEST, preferred_element_type=F32
-    )
-    da1 = nt(dq1, w_self[:, :D]) + nt(dk1, w_self[:, D : 2 * D]) + nt(dv1, w_self[:, 2 * D :])
+        "hr,lr->lh", diag[:HEADS], hot, precision=lax.Precision.HIGHEST, preferred_element_type=F32
+    )
+    da1 = nt(dq1, wq1) + nt(dk1, wk1) + nt(dv1, wv1)
     tok_wide = tok.astype(F32)
     dx, gg1 = norm_back(tok_wide, gains[0], da1)
     grad_tokens = (dh1 + dx).astype(BF16)
-    grad_memory = (nt(dk2, w_mem[:, :D]) + nt(dv2, w_mem[:, D:])).astype(BF16)
-    quarter, eighth = self_query.shape[0], position_bias.shape[0]
+    grad_memory = (nt(dk2, wk2) + nt(dv2, wv2)).astype(BF16)
     small = jnp.concatenate(
         [jnp.stack([gg1, gg2, gg3]), jnp.pad(g_bias, ((0, 0), (0, D - HEADS)))], 0
     )
@@ -1146,7 +1287,6 @@
     ]
     total, small = reduce_grads(peers, pairs, g_in, g_out, small)
     total = total.astype(F32)
-    f = lax.axis_index("fsdp")
     gain = lambda i: lax.dynamic_slice_in_dim(small[i], f * quarter, quarter)
     bias_out = lax.dynamic_slice_in_dim(small[3:], f * eighth, eighth)[:, :HEADS]
     count = len(pairs)

time: 777 us -> 727 us (0.936); the launches traced: 773 us -> 713 us
  waiting for transfers between devices: 267 us -> 174 us
  Pallas kernels: 275 us -> 310 us
  blocking collectives: 106 us -> 93 us
    all_gather x8 -> x4, waiting for transfers between devices: 117 us -> 28.8 us  [gather(): return lax.all_gather(x, axis_name, axis=axis, tiled=True)]
    pallas_call x2 -> x1, Pallas kernels: 29.9 us -> 67.7 us  [front(): pl.pallas_call(functools.partial(front_kernel, peers), name='front', out_...]
    all_gather x6 -> x4, blocking collectives: 106 us -> 93 us  [gather(): return lax.all_gather(x, axis_name, axis=axis, tiled=True)]
    gather x9 -> x15, other arithmetic: 15.3 us -> 17.4 us  [shards(): jnp.take(passage_lengths[0], slot // PLEN)]
  transfers between devices with their start and end apart: 14 -> 10, of which waited for: 10 -> 8; matrix products, arithmetic and copies ran while one was open for 8% -> 8% of each run, Pallas kernels for 4% -> 0%
where the time goes in v3:
time: 727 us; the launch traced here: 713 us
  Pallas kernels  310 us (43%)
  waiting for transfers between devices  174 us (24%)
  blocking collectives  93 us (13%)
  matrix products  39.6 us (5%)
  other arithmetic  34.3 us (5%)
  local copies, waits for them, and re-layouts  33.5 us (5%)
  between operations  16.1 us (2%)
  starting transfers between devices  11.7 us (2%)
    pallas_call x1, Pallas kernels, reduce_grads(): pl.pallas_call(functools.partial(reduce_kernel, peers, left_index), name=...  152 us
    reduce_scatter x3, waiting for transfers between devices, scatter(): return lax.psum_scatter(x, axis_name, scatter_dimension=axis, tiled=True)  113 us
    all_gather x4, blocking collectives, gather(): return lax.all_gather(x, axis_name, axis=axis, tiled=True)  93 us
    pallas_call x1, Pallas kernels, front(): pl.pallas_call(functools.partial(front_kernel, peers), name='front', out_...  67.7 us
    pallas_call x1, Pallas kernels, cross_backward(): pl.pallas_call(cross_backward_kernel, name='cross_backward', out_shape=[s...  34.3 us
    all_to_all x2, waiting for transfers between devices, shards(): lax.all_to_all(x.reshape(peers, rows, x.shape[-1]), 'ctx', 0, 0)  32.2 us
    all_gather x4, waiting for transfers between devices, gather(): return lax.all_gather(x, axis_name, axis=axis, tiled=True)  28.8 us
    pallas_call x1, Pallas kernels, self_backward(): pl.pallas_call(kern, name='self_backward', out_shape=[sds((rows, D), BF16...  28.4 us
  transfers between devices with their start and end apart: 10, of which 8 were waited for; matrix products, arithmetic and copies ran while one was open for 8% of the time, Pallas kernels for 0%

profile of v3, /device:TPU:0, one launch (start us, length us, event | category | flops | bytes accessed | tf_op | source)
XLA Modules:
  0.0 712.8 jit_solution(14827463905257079477)
XLA Ops:
  18.1 67.7 %front.1 = (bf16[7,768,768]{2,1,0:T(8,128)(2,1)}, f32[8,768]{1,0:T(8,128)}, bf16[2,12,64,2048]{3,2,1,0:T(8,128)(2,1)}, bf16[2,12,64,2048]{3,2,1,0:T(8,128)(2,1)}...) custom-call(s32[16]{0:T(128)} %select_reduce_fusion.1.refs_0_, ...), custom_call_target="tpu_custom_call" | custom-call | tf_op jit(solution)/shard_map/front/pallas_call | solution.py:967
  91.2 4.3 select_reduce_fusion
  95.6 8.4 %select_select_fusion = s32[640]{0:T(1024)S(1)} fusion(pred[640]{0:T(1024)(128)(4,1)S(1)} %compare_reduce_fusion, pred[640]{0:T(1024)(128)(4,1)S(1)} %compare_reduce_fusion.1, pred[640]{0:T(1024)(128)(4,1)S(1)} %compare_reduce_fusion.2, pred[640]{0:T(1024)(128)(4,1)S(1)} %compare_reduce_fusion.3, pred[640]{0:T(1024)(128)(4,1)S(1)} %compare_reduce_fusion.4, ...), kind=kLoop, calls=%fused_computation.155 | loop fusion | flops 8320 | bytes 13492 | tf_op jit(solution)/shard_map/jit(_take)/gather | solution.py:1221
  104.6 3.2 fusion.9.v2
  107.8 3.1 fusion.8.k2
  110.9 18.1 %all-gather.6.cloned.1.call-done.q_all = bf16[1024,768]{1,0:T(8,128)(2,1)} async-done(((bf16[128,768]{1,0:T(8,128)(2,1)}), bf16[1024,768]{1,0:T(8,128)(2,1)}) %all-gather.6.cloned.1.call-update) | async-done | bytes 1572880 | tf_op jit(solution)/shard_map/all_gather | solution.py:1158
  129.1 28.0 %cross_forward.1 = (bf16[1024,768]{1,0:T(8,128)(2,1)}, f32[1024,128]{1,0:T(8,128)}) custom-call(bf16[1024,768]{1,0:T(8,128)(2,1)} %all-gather.6.cloned.1.call-done.q_all, bf16[640,768]{1,0:T(8,128)(2,1)} %fusion.8.k2, bf16[640,768]{1,0:T(8,128)(2,1)} %fusion.9.v2, f32[1,640]{1,0:T(1,128)} %compare_select_fusion.2.mask), custom_call_target="tpu_custom_call" | custom-call | tf_op jit(solution)/shard_map/cross_forward/pallas_call | solution.py:108
  157.1 3.5 all-to-all-start
  163.2 11.8 %all-to-all-done = f32[8,128,128]{2,1,0:T(8,128)S(1)} async-done(((f32[8,128,128]{2,1,0:T(8,128)}), f32[8,128,128]{2,1,0:T(8,128)S(1)}, u32[]{:S(2)}, u32[]{:S(2)}) %all-to-all-start) | async-done | bytes 524320 | tf_op jit(solution)/shard_map/all_to_all | solution.py:1224
  175.0 3.6 all-to-all-start.1
  183.1 9.0 %all-gather = bf16[1,512,768]{2,1,0:T(8,128)(2,1)} all-gather(bf16[1,128,768]{2,1,0:T(8,128)(2,1)S(1)} %copy-done.9), channel_id=2, replica_groups=mesh['ctx'=8,'fsdp'=4] {'fsdp'}, dimensions={1}, use_global_device_ids=true | all-gather | bytes 983040 | tf_op jit(solution)/shard_map/all_gather | solution.py:1158
  195.5 20.3 %all-to-all-done.1 = bf16[8,128,768]{1,2,0:T(8,128)(2,1)S(1)} async-done(((bf16[8,128,768]{1,2,0:T(8,128)(2,1)}), bf16[8,128,768]{1,2,0:T(8,128)(2,1)S(1)}, u32[]{:S(2)}, u32[]{:S(2)}) %all-to-all-start.1) | async-done | bytes 1572896 | tf_op jit(solution)/shard_map/all_to_all | solution.py:1224
  215.8 4.3 all-to-all-start.2
  224.9 16.6 %all_gather.26 = bf16[512,768]{1,0:T(8,128)(2,1)} all-gather(bf16[128,768]{1,0:T(8,128)(2,1)S(1)} %multiply_convert_fusion.1), channel_id=1, replica_groups=mesh['ctx'=8,'fsdp'=4] {'fsdp'}, dimensions={0}, use_global_device_ids=true | all-gather | bytes 983040 | tf_op jit(solution)/shard_map/all_gather | solution.py:1158
  249.4 21.4 %reduce-scatter.6.cloned.1.call-done = bf16[128,768]{1,0:T(8,128)(2,1)} async-done(((bf16[512,768]{1,0:T(8,128)(2,1)}), bf16[128,768]{1,0:T(8,128)(2,1)}) %reduce-scatter.6.cloned.1.call-update) | async-done | bytes 196624 | tf_op jit(solution)/shard_map/reduce_scatter | solution.py:1162
  279.2 32.9 %all_gather.29.stats = f32[32,1024]{1,0:T(8,128)} all-gather(f32[32,128]{1,0:T(8,128)S(1)} %fusion.70), channel_id=1, replica_groups=mesh['ctx'=8,'fsdp'=4] {'ctx'}, dimensions={1}, use_global_device_ids=true | all-gather | bytes 147456 | tf_op jit(solution)/shard_map/all_gather | solution.py:1158
  312.1 7.7 %all-gather.10.cloned.1.call-done.do_all = bf16[1024,768]{1,0:T(8,128)(2,1)} async-done(((bf16[128,768]{1,0:T(8,128)(2,1)}), bf16[1024,768]{1,0:T(8,128)(2,1)}) %all-gather.10.cloned.1.call-update) | async-done | bytes 1572880 | tf_op jit(solution)/shard_map/all_gather | solution.py:1158
  319.8 34.3 %cross_backward.1 = (f32[1024,768]{1,0:T(8,128)}, bf16[640,768]{1,0:T(8,128)(2,1)}, bf16[640,768]{1,0:T(8,128)(2,1)}) custom-call(bf16[1024,768]{1,0:T(8,128)(2,1)} %all-gather.6.cloned.1.call-done.q_all, bf16[1024,768]{1,0:T(8,128)(2,1)} %all-gather.10.cloned.1.call-done.do_all, f32[32,1024]{1,0:T(8,128)} %all_gather.29.stats, bf16[640,768]{1,0:T(8,128)(2,1)} %fusion.8.k2, ...), custom_call_target="tpu_custom_call" | custom-call | tf_op jit(solution)/shard_map/cross_backward/pallas_call | solution.py:151
  357.7 69.6 %reduce-scatter.8.cloned.1.call-done = f32[128,768]{1,0:T(8,128)} async-done(((f32[1024,768]{1,0:T(8,128)}), f32[128,768]{1,0:T(8,128)}) %reduce-scatter.8.cloned.1.call-update) | async-done | bytes 393232 | tf_op jit(solution)/shard_map/reduce_scatter | solution.py:1162
  431.0 21.9 %reduce-scatter.4.cloned.1.call-done = bf16[128,768]{1,0:T(8,128)(2,1)} async-done(((bf16[512,768]{1,0:T(8,128)(2,1)}), bf16[128,768]{1,0:T(8,128)(2,1)}) %reduce-scatter.4.cloned.1.call-update) | async-done | bytes 196624 | tf_op jit(solution)/shard_map/reduce_scatter | solution.py:1162
  464.2 3.3 fusion.10
  467.9 34.4 %all_gather.31.stat_slot = f32[1024,128]{1,0:T(8,128)} all-gather(f32[128,128]{1,0:T(8,128)S(1)} %pad.34.stat_own), channel_id=1, replica_groups=mesh['ctx'=8,'fsdp'=4] {'ctx'}, dimensions={0}, use_global_device_ids=true | all-gather | bytes 589824 | tf_op jit(solution)/shard_map/all_gather | solution.py:1158
  505.3 28.4 %self_backward.1 = (bf16[128,768]{1,0:T(8,128)(2,1)}, bf16[128,768]{1,0:T(8,128)(2,1)}, bf16[128,768]{1,0:T(8,128)(2,1)}, f32[16,2048]{1,0:T(8,128)}) custom-call(s32[16]{0:T(128)} %order.1, s32[2]{0:T(128)} %copy-done.33, bf16[1024,768]{1,0:T(8,128)(2,1)} %get-tuple-element.48.q_nat, bf16[1024,768]{1,0:T(8,128)(2,1)} %get-tuple-element.49.k_nat, ...), custom_call_target="tpu_custom_call" | custom-call | tf_op jit(solution)/shard_map/self_backward/pallas_call | solution.py:230
  541.3 151.7 %reduce_grads.1 = (bf16[16,192,768]{2,1,0:T(8,128)(2,1)}, f32[40,768]{1,0:T(8,128)}) custom-call(bf16[128,768]{1,0:T(8,128)(2,1)} %get-tuple-element.60.refs_0_, bf16[128,768]{1,0:T(8,128)(2,1)} %get-tuple-element.52.refs_1_, bf16[128,768]{1,0:T(8,128)(2,1)} %get-tuple-element.61.refs_2_, bf16[640,768]{1,0:T(8,128)(2,1)} %bitcast.170, ...), custom_call_target="tpu_custom_call" | custom-call | tf_op jit(solution)/shard_map/reduce_grads/pallas_call | solution.py:1125
  (204 shorter events, 89.0 us)
Async XLA Ops:
  8.0 235.9 %copy-start = (bf16[768,768]{1,0:T(8,128)(2,1)S(1)}, bf16[768,768]{1,0:T(8,128)(2,1)}, u32[]{:S(2)}) copy-start(bf16[768,768]{1,0:T(8,128)(2,1)} %param.38) | copy-start | bytes 3538948
  8.0 82.5 %copy-start.25 = (s32[1,20]{1,0:T(1,128)S(1)}, s32[1,20]{1,0:T(1,128)}, u32[]{:S(2)}) copy-start(s32[1,20]{1,0:T(1,128)} %param.24) | copy-start | bytes 244
  8.0 96.6 %copy-start.13 = (bf16[1,640,768]{2,1,0:T(8,128)(2,1)S(1)}, bf16[1,640,768]{2,1,0:T(8,128)(2,1)}, u32[]{:S(2)}) copy-start(bf16[1,640,768]{2,1,0:T(8,128)(2,1)} %param.21) | copy-start | bytes 2949124
  8.1 121.0 %all-gather.6.cloned.1.call-start = ((), (), s32[]{:S(2)}) async-start(), calls=%async_computation.6 | async-start | bytes 1769472 | tf_op jit(solution)/shard_map/all_gather | solution.py:1158
  157.1 17.9 %all-to-all-start = ((f32[8,128,128]{2,1,0:T(8,128)}), f32[8,128,128]{2,1,0:T(8,128)S(1)}, u32[]{:S(2)}, u32[]{:S(2)}) async-start(f32[8,128,128]{2,1,0:T(8,128)} %bitcast.171), calls=%async_computation | async-start | bytes 1048576 | tf_op jit(solution)/shard_map/all_to_all | solution.py:1224
  175.0 40.8 %all-to-all-start.1 = ((bf16[8,128,768]{1,2,0:T(8,128)(2,1)}), bf16[8,128,768]{1,2,0:T(8,128)(2,1)S(1)}, u32[]{:S(2)}, u32[]{:S(2)}) async-start(bf16[8,128,768]{1,2,0:T(8,128)(2,1)} %copy.101), calls=%async_computation.1 | async-start | bytes 3145728 | tf_op jit(solution)/shard_map/all_to_all | solution.py:1224
  178.7 43.8 %all-gather.8.cloned.1.call-start = ((), (), s32[]{:S(2)}) async-start(), calls=%async_computation.7 | async-start | bytes 1474560 | tf_op jit(solution)/shard_map/all_gather | solution.py:1158
  215.8 25.7 %all-to-all-start.2 = ((bf16[192,4,768]{2,0,1:T(8,128)(2,1)}), bf16[192,4,768]{2,0,1:T(8,128)(2,1)}, u32[]{:S(2)}, u32[]{:S(2)}) async-start(bf16[192,4,768]{2,0,1:T(8,128)(2,1)} %bitcast.163), calls=%async_computation.2 | async-start | bytes 2359296 | tf_op jit(solution)/shard_map/all_to_all | solution.py:1218
  220.2 50.6 %reduce-scatter.6.cloned.1.call-start = ((), (), s32[]{:S(2)}) async-start(), calls=%async_computation.9 | async-start | bytes 983040 | tf_op jit(solution)/shard_map/reduce_scatter | solution.py:1162
  249.3 24.3 %copy-start.3 = (bf16[768,768]{1,0:T(8,128)(2,1)S(1)}, bf16[768,768]{1,0:T(8,128)(2,1)}, u32[]{:S(2)}) copy-start(bf16[768,768]{1,0:T(8,128)(2,1)} %all-gather.8.cloned.1.call-done) | copy-start | bytes 3538948
  249.3 70.5 %all-gather.10.cloned.1.call-start = ((), (), s32[]{:S(2)}) async-start(), calls=%async_computation.10 | async-start | bytes 1769472 | tf_op jit(solution)/shard_map/all_gather | solution.py:1158
  275.0 152.4 %reduce-scatter.8.cloned.1.call-start = ((), (), s32[]{:S(2)}) async-start(), calls=%async_computation.11 | async-start | bytes 3538944 | tf_op jit(solution)/shard_map/reduce_scatter | solution.py:1162
  354.1 98.7 %reduce-scatter.4.cloned.1.call-start = ((), (), s32[]{:S(2)}) async-start(), calls=%async_computation.8 | async-start | bytes 983040 | tf_op jit(solution)/shard_map/reduce_scatter | solution.py:1162
  357.5 70.9 %copy-start.29 = (f32[768]{0:T(1024)S(1)}, f32[768]{0:T(1024)}, u32[]{:S(2)}) copy-start(f32[768]{0:T(1024)} %get-tuple-element.72) | copy-start | bytes 9220
  357.5 95.4 %copy-start.8 = (bf16[128,768]{1,0:T(8,128)(2,1)S(1)}, bf16[128,768]{1,0:T(8,128)(2,1)}, u32[]{:S(2)}) copy-start(bf16[128,768]{1,0:T(8,128)(2,1)} %reduce-scatter.6.cloned.1.call-done) | copy-start | bytes 589828
  357.5 95.4 %copy-start.10 = (bf16[1,128,768]{2,1,0:T(8,128)(2,1)S(1)}, bf16[1,128,768]{2,1,0:T(8,128)(2,1)}, u32[]{:S(2)}) copy-start(bf16[1,128,768]{2,1,0:T(8,128)(2,1)} %param.39) | copy-start | bytes 589828
  357.5 95.4 %copy-start.31 = (f32[128]{0:T(128)S(1)}, f32[128]{0:T(128)}, u32[]{:S(2)}) copy-start(f32[128]{0:T(128)} %copy-done.30) | copy-start | bytes 1540
  357.5 95.3 %copy-start.34 = (f32[128]{0:T(128)S(1)}, f32[128]{0:T(128)}, u32[]{:S(2)}) copy-start(f32[128]{0:T(128)} %get-tuple-element.99) | copy-start | bytes 1540
  357.5 95.3 %copy-start.36 = (f32[128]{0:T(128)S(1)}, f32[128]{0:T(128)}, u32[]{:S(2)}) copy-start(f32[128]{0:T(128)} %copy-done.35) | copy-start | bytes 1540
  357.5 147.7 %all-gather.12.cloned.1.call-start = ((), (), s32[]{:S(2)}) async-start(), calls=%async_computation.12 | async-start | bytes 1769472 | tf_op jit(solution)/shard_map/all_gather | solution.py:1158
  428.4 24.5 %copy-start.21 = (bf16[128,768]{1,0:T(8,128)(2,1)}, bf16[128,768]{1,0:T(8,128)(2,1)S(1)}, u32[]{:S(2)}) copy-start(bf16[128,768]{1,0:T(8,128)(2,1)S(1)} %convert_element_type.114.refs_9_) | copy-start | bytes 589828
  431.0 23.7 %copy-start.19 = (bf16[128,768]{1,0:T(8,128)(2,1)S(1)}, bf16[128,768]{1,0:T(8,128)(2,1)}, u32[]{:S(2)}) copy-start(bf16[128,768]{1,0:T(8,128)(2,1)} %get-tuple-element.52.refs_1_) | copy-start | bytes 589828
  467.9 37.3 %copy-start.22 = (f32[128,128]{1,0:T(8,128)}, f32[128,128]{1,0:T(8,128)S(1)}, u32[]{:S(2)}) copy-start(f32[128,128]{1,0:T(8,128)S(1)} %pad.34.stat_own) | copy-start | bytes 196612
  505.3 28.4 %copy-start.27 = (s32[2048]{0:T(1024)S(1)}, s32[2048]{0:T(1024)}, u32[]{:S(2)}) copy-start(s32[2048]{0:T(1024)} %pad.29) | copy-start | bytes 24580
  (30 other events, 105.0 us)
Sparse Core Ops, SparseCore 0:
  86.0 43.0 all-gather.5
  275.1 44.7 all-gather.9
  354.3 73.0 reduce-scatter.7
  430.5 22.3 reduce-scatter.3
  457.5 47.7 all-gather.11
Sparse Core Ops, SparseCore 1:
  180.7 18.6 all-gather.7
  249.4 21.3 reduce-scatter.5

commit v4 on v3

--- a/solution.py
+++ b/solution.py
@@ -78,84 +78,6 @@
     return pl.BlockSpec(memory_space=pltpu.SMEM)
 def sds(shape, dtype):
     return jax.ShapeDtypeStruct(shape, dtype)
-
-def cross_forward_kernel(q_all, k2, v2, mask, o, lse):
-    rows = q_all.shape[0]
-    step = BLOCK
-    stat_lane = lax.broadcasted_iota(jnp.int32, (step, LANES), 1)
-
-    def tile(t, c):
-        rs = pl.ds(pl.multiple_of(t * step, step), step)
-        def pair(p, stats):
-            sl = lanes_of(p)
-            q, k, v = q_all[rs, sl], k2[:, sl], v2[:, sl]
-            total = jnp.zeros((step, LANES), F32)
-            for half in range(2):
-                s = nt(q, half_mask(k, half)) + mask[...]
-                m = jnp.max(s, axis=1, keepdims=True)
-                e = jnp.exp(s - m)
-                l = jnp.sum(e, axis=1, keepdims=True)
-                total += nn(e.astype(BF16), half_mask(v, half)) / l
-                stats = jnp.where(stat_lane == 2 * p + half, m + jnp.log(l), stats)
-            o[rs, sl] = total.astype(BF16)
-            return stats
-        lse[rs, :] = lax.fori_loop(0, PAIRS, pair, jnp.zeros((step, LANES), F32))
-        return c
-    lax.fori_loop(0, rows // step, tile, 0)
-
-def cross_forward(q_all, k2, v2, mask):
-    rows = q_all.shape[0]
-    return pl.pallas_call(
-        cross_forward_kernel,
-        name="cross_forward",
-        out_shape=[sds((rows, D), BF16), sds((rows, LANES), F32)],
-        in_specs=[full_spec()] * 4,
-        out_specs=[full_spec()] * 2,
-        compiler_params=pltpu.CompilerParams(vmem_limit_bytes=VMEM_LIMIT),
-    )(q_all, k2, v2, mask)
-
-def cross_backward_kernel(q_all, do_all, stats, k2, v2, mask, dq, dk, dv):
-    rows = q_all.shape[0]
-    slots = k2.shape[0]
-    step = BLOCK
-
-    def pair(p, c):
-        sl = lanes_of(p)
-        ks = [half_mask(k2[:, sl], i) for i in range(2)]
-        vs = [half_mask(v2[:, sl], i) for i in range(2)]
-        def tile(t, carry):
-            dkp, dvp = carry
-            rs = pl.ds(pl.multiple_of(t * step, step), step)
-            q, do = q_all[rs, sl], do_all[rs, sl]
-            dqp = jnp.zeros((step, LANES), F32)
-            for half in range(2):
-                h = 2 * p + half
-                qm, dom = half_mask(q, half), half_mask(do, half)
-                s = nt(ks[half], q) + mask[...]
-                e = jnp.exp(s - stats[pl.ds(h, 1), rs])
-                dvp = dvp + nn(e.astype(BF16), dom)
-                ds = (e * (nt(vs[half], do) - stats[pl.ds(16 + h, 1), rs])).astype(BF16)
-                dkp = dkp + nn(ds, qm)
-                dqp = dqp + tn(ds, ks[half])
-            dq[rs, sl] = dqp.astype(dq.dtype)
-            return dkp, dvp
-        zero = jnp.zeros((slots, LANES), F32)
-        dkp, dvp = lax.fori_loop(0, rows // step, tile, (zero, zero))
-        dk[:, sl] = dkp.astype(BF16)
-        dv[:, sl] = dvp.astype(BF16)
-        return c
-    lax.fori_loop(0, PAIRS, pair, 0)
-
-def cross_backward(q_all, do_all, stats, k2, v2, mask):
-    rows, slots = q_all.shape[0], k2.shape[0]
-    return pl.pallas_call(
-        cross_backward_kernel,
-        name="cross_backward",
-        out_shape=[sds((rows, D), F32), sds((slots, D), BF16), sds((slots, D), BF16)],
-        in_specs=[full_spec()] * 6,
-        out_specs=[full_spec()] * 3,
-        compiler_params=pltpu.CompilerParams(vmem_limit_bytes=VMEM_LIMIT),
-    )(q_all, do_all, stats, k2, v2, mask)
 
 def self_backward_kernel(order, own, q_nat, k_nat, v_nat, do_slot, do_own, stat_slot, stat_own, delta_own, table, back_table,
                          dq, dk, dv, diag, inv, q_own, k_own, v_own, do_nat, stat_nat, stat_t, acc):
@@ -869,8 +791,9 @@
 def front_kernel(peers, *refs):
     inv, own, tok, pack, buckets, buckets_back = refs[:6]
     shards_in = refs[6 : 6 + N_FRONT]
-    (weights, gains, ahead, behind, q_nat, k_nat, v_nat, a1, o1, h1, a2, q2, lse) = refs[6 + N_FRONT : 19 + N_FRONT]
-    (tok_all, pack_all, table, q_own, *sem) = refs[19 + N_FRONT :]
+    (w_self, w_rest, gains, ahead, behind, q_nat, k_nat, v_nat, a1, o1, h1, a2, q2, lse) = refs[6 + N_FRONT : 20 + N_FRONT]
+    (tok_all, pack_all, table, q_own, *sem) = refs[20 + N_FRONT :]
+    weights = [w_self.at[i] for i in range(3)] + [w_rest.at[i] for i in range(N_FRONT - 3)]
     sem_t, sem_w, sem_p = sem[0:2], sem[2:4], sem[4:6]
     wire = Wire(peers)
     at, depth = wire.at, wire.depth
@@ -882,7 +805,7 @@
         wire.go(remote(pack, pack_all.at[at.f], sem_p, d, at.group(d)))
     wire.spread(tok, tok_all, sem_t)
     for i in range(3):
-        wire.weight_start(shards_in[i], weights.at[i], sem_w, i)
+        wire.weight_start(shards_in[i], weights[i], sem_w, i)
     wire.slot(tok_all, at.c)[...] = tok[...]
     pack_all[at.f] = pack[...]
     for d in range(1, WAYS):
@@ -899,13 +822,13 @@
     for step in range(1, depth):
         wire.relay(tok_all, sem_t, step)
     for i in range(3):
-        wire.weight_relay(weights.at[i], sem_w, i)
+        wire.weight_relay(weights[i], sem_w, i)
     for i in range(3, N_FRONT):
-        wire.weight_start(shards_in[i], weights.at[i], sem_w, i)
+        wire.weight_start(shards_in[i], weights[i], sem_w, i)
     first = gains[0:1, :]
     a1[...] = normed(tok[...].astype(F32), first).astype(BF16)
     for i in range(3):
-        wire.weight_ready(weights.at[i], sem_w, i)
+        wire.weight_ready(weights[i], sem_w, i)
     for step in range(depth):
         wire.from_beside(tok_all, sem_t, step)
 
@@ -916,13 +839,13 @@
         a = normed(jnp.concatenate(parts, 0).astype(F32), first).astype(BF16)
         dst = pl.ds(pl.multiple_of(t * BLOCK, BLOCK), BLOCK)
         for j, out in enumerate((q_nat, k_nat, v_nat)):
-            out[dst, :] = nn(a, weights[j]).astype(BF16)
+            out[dst, :] = nn(a, weights[j][...]).astype(BF16)
         return c
 
     lax.fori_loop(0, length // BLOCK, tile, 0)
     for i in range(mine):
         q_own[i * PIECE : (i + 1) * PIECE, :] = q_nat[pl.ds(own[i, 0] * PIECE, PIECE), :]
-    wire.weight_relay(weights.at[3], sem_w, 3)
+    wire.weight_relay(weights[3], sem_w, 3)
     lane = lax.broadcasted_iota(jnp.int32, (rows, length), 1)
     limit = jnp.concatenate([jnp.full((PIECE, 1), own[i, 3], jnp.int32) for i in range(mine)], 0)
     visible = lane < limit
@@ -944,19 +867,19 @@
         return stats
 
     stats = lax.fori_loop(0, PAIRS // 2, pair, jnp.zeros((rows, LANES), F32))
-    wire.weight_relay(weights.at[4], sem_w, 4)
+    wire.weight_relay(weights[4], sem_w, 4)
     lse[...] = lax.fori_loop(PAIRS // 2, PAIRS, pair, stats)
-    wire.weight_relay(weights.at[5], sem_w, 5)
-    wire.weight_ready(weights.at[3], sem_w, 3)
-    h = tok[...].astype(F32) + nn(o1[...], weights[3])
+    wire.weight_relay(weights[5], sem_w, 5)
+    wire.weight_ready(weights[3], sem_w, 3)
+    h = tok[...].astype(F32) + nn(o1[...], weights[3][...])
     h1[...] = h
     a = normed(h, gains[1:2, :]).astype(BF16)
     a2[...] = a
-    wire.weight_ready(weights.at[4], sem_w, 4)
-    q2[...] = nn(a, weights[4]).astype(BF16)
-    wire.weight_relay(weights.at[6], sem_w, 6)
+    wire.weight_ready(weights[4], sem_w, 4)
+    q2[...] = nn(a, weights[4][...]).astype(BF16)
+    wire.weight_relay(weights[6], sem_w, 6)
     for i in (5, 6):
-        wire.weight_ready(weights.at[i], sem_w, i)
+        wire.weight_ready(weights[i], sem_w, i)
     wire.drain()
 
 
@@ -967,12 +890,12 @@
     return pl.pallas_call(
         functools.partial(front_kernel, peers),
         name="front",
-        out_shape=[sds((N_FRONT, D, D), BF16), sds((8, D), F32)]
+        out_shape=[sds((3, D, D), BF16), sds((N_FRONT - 3, D, D), BF16), sds((8, D), F32)]
         + [sds((2, HEADS, PIECE, 2 * length), BF16)] * 2
         + [sds((length, D), BF16)] * 3
         + [block(BF16), block(BF16), block(F32), block(BF16), block(BF16), sds((rows, LANES), F32)],
         in_specs=[smem_spec()] * 2 + [full_spec()] * (4 + N_FRONT),
-        out_specs=[full_spec()] * 13,
+        out_specs=[full_spec()] * 14,
         scratch_shapes=[
             pltpu.VMEM((length, D), BF16),
             pltpu.VMEM((WAYS,) + pack.shape, BF16),
@@ -982,6 +905,348 @@
         + sems(2 * depth) + sems(3 * N_FRONT) + sems(WAYS),
         compiler_params=pltpu.CompilerParams(collective_id=1, has_side_effects=True, vmem_limit_bytes=VMEM_LIMIT),
     )(inv, own, tok, pack, buckets, buckets_back, *weight_shards)
+
+
+STAT = 16
+
+
+def split(x):
+    high = x.astype(BF16)
+    return high, (x - high.astype(F32)).astype(BF16)
+
+
+def head_matrix(rows):
+    row = lax.broadcasted_iota(jnp.int32, (rows, D), 0)
+    lane = lax.broadcasted_iota(jnp.int32, (rows, D), 1)
+    return jnp.where(lane // HEAD_DIM == row, 1.0, 0.0).astype(BF16)
+
+
+def per_head_sums(x, heads):
+    high, low = split(x)
+    return nt(heads, high) + nt(heads, low)
+
+
+def blend(parts, stats, heads):
+    top = functools.reduce(jnp.maximum, stats)
+    shares = [jnp.exp(s - top) for s in stats]
+    total = functools.reduce(jnp.add, shares)
+    value = 0.0
+    for part, share in zip(parts, shares):
+        high, low = split(share / total)
+        value = value + (tn(high, heads) + tn(low, heads)) * part.astype(F32)
+    return value, top + jnp.log(total)
+
+
+def norm_back_rows(x, gain, dy):
+    r = lax.rsqrt(jnp.mean(x * x, axis=-1, keepdims=True) + EPSILON)
+    gdy = gain * dy
+    dx = r * gdy - x * (r * r * r) * jnp.mean(x * gdy, axis=-1, keepdims=True)
+    return dx, jnp.sum(dy * x * r, axis=0, keepdims=True)
+
+
+def round_trip(wire, gathered, filler, compute, ship, fold):
+    at = wire.at
+    b = at.b
+    first, second, third = [wire.near(step) for step in (1, 2, 3)]
+
+    def relay(step):
+        for buf, sem in gathered:
+            wire.relay(buf, sem, step)
+
+    def ready(a):
+        for buf, sem in gathered:
+            wire.from_beside(buf, sem, a)
+
+    filler()
+    relay(1)
+    ready(at.a)
+    compute(at.c, at.a * 2 + 1 - b)
+    ship(at.a)
+    relay(2)
+    relay(3)
+    compute(first * 2 + b, second * 2 + b)
+    ready(third)
+    ready(second)
+    compute(third * 2 + 1 - b, second * 2 + 1 - b)
+    ship(third)
+    ship(second)
+    ready(first)
+    compute(third * 2 + b, first * 2 + 1 - b)
+    ship(first)
+    fold(third)
+    fold(second)
+    fold(first)
+
+
+def middle_kernel(peers, *refs):
+    (q2, h1, o1, lse1, w_rest, gains, mem, mask_row, mask_col, grad, co_shard, in_shard, w_out) = refs[:13]
+    (o2_out, branch2_out, dq2_out, dk2_out, dv2_out, branch1_out, dh1_out, do1_out, do1_all, stat1_all, g_in, g_out, layer_out, gmem_out, small) = refs[13:28]
+    (q_all, k2, v2, part, part_lse, from_b, from_b_lse, joined, joined_lse, from_z, from_z_lse,
+     w_co, w_in, g_all, a3_all, dact, act, dpre, da3_send, da3_in, out_send, out_in,
+     do_all, stat_all, stat_own, dk_acc, dv_acc, dqp, dq_b, dq_j, dq_z, *sem) = refs[28:]
+    sem = [sem[2 * i : 2 * i + 2] for i in range(len(sem) // 2)]
+    (s_q, s_w, s_in, s_g, s_y, s_yl, s_z, s_zl, s_a3, s_da3, s_out, s_do, s_st, s_dy, s_dz, s_do1, s_st1) = sem
+    wire = Wire(peers)
+    at, depth = wire.at, wire.depth
+    rows = q2.shape[0]
+    heads = head_matrix(STAT)
+    quarter = co_shard.shape[0]
+    units = w_out.shape[0]
+    block = lambda f: pl.ds(pl.multiple_of(f * rows, rows), rows)
+    greet(wire.partners())
+    wire.spread(q2, q_all, s_q)
+    q_all[at.c] = q2[...]
+    wire.weight_start(co_shard, w_co, s_w, 0)
+    for d in range(1, WAYS):
+        f = lax.rem(at.f + d, WAYS)
+        wire.go(remote(grad, g_all.at[block(at.f)], s_g, d, at.group(d)))
+        wire.go(remote(in_shard.at[:, pl.ds(pl.multiple_of(f * units, LANES), units)], wire.shard(w_in, at.f), s_in, d, at.group(d)))
+    g_all[block(at.f), :] = grad[...]
+    wire.shard(w_in, at.f)[...] = in_shard[:, pl.ds(pl.multiple_of(at.f * units, LANES), units)]
+
+    def project_memory():
+        k2[...] = nn(mem[...], w_rest[2]).astype(BF16)
+        v2[...] = nn(mem[...], w_rest[3]).astype(BF16)
+
+    stat_lane = lax.broadcasted_iota(jnp.int32, (2 * rows, LANES), 1)
+
+    def attend(c1, c2):
+        def pair(p, stats):
+            sl = lanes_of(p)
+            q = jnp.concatenate([q_all[c1, :, sl], q_all[c2, :, sl]], 0)
+            k, v = k2[:, sl], v2[:, sl]
+            total = jnp.zeros((2 * rows, LANES), F32)
+            for half in range(2):
+                s = nt(q, half_mask(k, half)) + mask_row[...]
+                m = jnp.max(s, axis=1, keepdims=True)
+                e = jnp.exp(s - m)
+                l = jnp.sum(e, axis=1, keepdims=True)
+                total += nn(e.astype(BF16), half_mask(v, half)) / l
+                stats = jnp.where(stat_lane == 2 * p + half, m + jnp.log(l), stats)
+            part[c1, :, sl] = total[:rows].astype(BF16)
+            part[c2, :, sl] = total[rows:].astype(BF16)
+            return stats
+
+        stats = lax.fori_loop(0, PAIRS, pair, jnp.zeros((2 * rows, LANES), F32))
+        part_lse[c1] = stats[:rows].T[:STAT]
+        part_lse[c2] = stats[rows:].T[:STAT]
+
+    def ship_part(a):
+        other = a * 2 + 1 - at.b
+        wire.go(remote(part.at[other], from_b.at[a], s_y, a, at.beside))
+        wire.go(remote(part_lse.at[other], from_b_lse.at[a], s_yl, a, at.beside))
+
+    def blend_column(a):
+        remote(from_b.at[a], from_b.at[a], s_y, a, at.beside).wait_recv()
+        remote(from_b_lse.at[a], from_b_lse.at[a], s_yl, a, at.beside).wait_recv()
+        c = a * 2 + at.b
+        return blend([part[c], from_b[a]], [part_lse[c], from_b_lse[a]], heads)
+
+    def fold_part(a):
+        value, stat = blend_column(a)
+        joined[a] = value.astype(BF16)
+        joined_lse[a] = stat
+        wire.go(remote(joined.at[a], from_z.at[at.a], s_z, at.a, at.column(a)))
+        wire.go(remote(joined_lse.at[a], from_z_lse.at[at.a], s_zl, at.a, at.column(a)))
+
+    round_trip(wire, [(q_all, s_q)], project_memory, attend, ship_part, fold_part)
+    wire.weight_relay(w_co, s_w, 0)
+    value, stat = blend_column(at.a)
+    parts, stats = [value], [stat]
+    for step in range(1, depth):
+        a = wire.near(step)
+        remote(from_z.at[a], from_z.at[a], s_z, a, at.column(a)).wait_recv()
+        remote(from_z_lse.at[a], from_z_lse.at[a], s_zl, a, at.column(a)).wait_recv()
+        parts.append(from_z[a])
+        stats.append(from_z_lse[a])
+    out2, lse2 = blend(parts, stats, heads)
+    o2 = out2.astype(BF16)
+    o2_out[...] = o2
+    wire.weight_ready(w_co, s_w, 0)
+    h2 = h1[...] + nn(o2, w_co[...])
+    a3 = normed(h2, gains[2:3, :]).astype(BF16)
+    a3_all[block(at.f), :] = a3
+    for d in range(1, WAYS):
+        spot = a3_all.at[block(at.f)]
+        wire.go(remote(spot, spot, s_a3, d, at.group(d)))
+
+    def arrive(buf, sem, size):
+        for d in range(1, WAYS):
+            f = lax.rem(at.f + WAYS - d, WAYS)
+            spot = buf.at[pl.ds(pl.multiple_of(f * size, size), size)]
+            remote(spot, spot, sem, d, at.group(WAYS - d)).wait_recv()
+
+    arrive(g_all, s_g, rows)
+    tiles = [slice(2 * rows * t, 2 * rows * (t + 1)) for t in range(WAYS // 2)]
+    for rs in tiles:
+        dact[rs, :] = nt(g_all[rs, :], w_out[...])
+    arrive(w_in, s_in, quarter)
+    arrive(a3_all, s_a3, rows)
+    for rs in tiles:
+        pre = nn(a3_all[rs, :], w_in[...])
+        square = pre * pre
+        t = jnp.tanh(0.7978845608028654 * (pre + 0.044715 * pre * square))
+        act[rs, :] = (0.5 * pre * (1.0 + t)).astype(BF16)
+        slope = 0.5 * (1.0 + t) + 0.5 * pre * (1.0 - t * t) * (0.7978845608028654 * (1.0 + 3 * 0.044715 * square))
+        d = (dact[rs, :] * slope).astype(BF16)
+        dpre[rs, :] = d
+        da3_send[rs, :] = nt(d, w_in[...]).astype(BF16)
+
+    def exchange(src, dst, sem):
+        for d in range(1, WAYS):
+            f = lax.rem(at.f + d, WAYS)
+            wire.go(remote(src.at[block(f)], dst.at[block(at.f)], sem, d, at.group(d)))
+
+    def collect(src, dst, sem):
+        arrive(dst, sem, rows)
+        value = src[block(at.f), :].astype(F32)
+        for d in range(1, WAYS):
+            value += dst[block(lax.rem(at.f + WAYS - d, WAYS)), :].astype(F32)
+        return value
+
+    exchange(da3_send, da3_in, s_da3)
+    for rs in tiles:
+        out_send[rs, :] = nn(act[rs, :], w_out[...]).astype(BF16)
+    exchange(out_send, out_in, s_out)
+    da3 = collect(da3_send, da3_in, s_da3)
+    dx, dgain = norm_back_rows(h2, gains[2:3, :], da3)
+    small[...] = jnp.zeros_like(small)
+    small[1:2, :] = dgain
+    dh2 = grad[...].astype(F32) + dx
+    branch2 = dh2.astype(BF16)
+    branch2_out[...] = branch2
+    do2 = nt(branch2, w_co[...]).astype(BF16)
+    do_all[at.c] = do2
+    stat_own[0] = jnp.concatenate([lse2, per_head_sums(do2.astype(F32) * out2, heads)], 0)
+    stat_all[at.c] = stat_own[0]
+    wire.spread(do_all.at[at.c], do_all, s_do)
+    wire.spread(stat_own.at[0], stat_all, s_st)
+
+    def feed_forward_grads():
+        layer_out[...] = (h2 + collect(out_send, out_in, s_out)).astype(BF16)
+        g_out[...] = tn(act[...], g_all[...]).astype(BF16)
+        g_in[...] = tn(a3_all[...], dpre[...]).astype(BF16)
+        dk_acc[...] = jnp.zeros_like(dk_acc)
+        dv_acc[...] = jnp.zeros_like(dv_acc)
+
+    def attend_back(c1, c2):
+        def pair(p, carry):
+            sl = lanes_of(p)
+            q = jnp.concatenate([q_all[c1, :, sl], q_all[c2, :, sl]], 0)
+            do = jnp.concatenate([do_all[c1, :, sl], do_all[c2, :, sl]], 0)
+            k, v = k2[:, sl], v2[:, sl]
+            dkp, dvp = dk_acc[:, sl], dv_acc[:, sl]
+            dq = jnp.zeros((2 * rows, LANES), F32)
+            for half in range(2):
+                line = lambda i: jnp.concatenate([stat_all[c1, pl.ds(i, 1), :], stat_all[c2, pl.ds(i, 1), :]], 1)
+                h = 2 * p + half
+                km = half_mask(k, half)
+                s = nt(km, q) + mask_col[...]
+                e = jnp.exp(s - line(h))
+                dvp = dvp + nn(e.astype(BF16), half_mask(do, half))
+                ds = (e * (nt(half_mask(v, half), do) - line(STAT + h))).astype(BF16)
+                dkp = dkp + nn(ds, half_mask(q, half))
+                dq = dq + tn(ds, km)
+            dk_acc[:, sl] = dkp
+            dv_acc[:, sl] = dvp
+            dqp[c1, :, sl] = dq[:rows].astype(BF16)
+            dqp[c2, :, sl] = dq[rows:].astype(BF16)
+            return carry
+
+        lax.fori_loop(0, PAIRS, pair, 0)
+
+    def ship_dq(a):
+        wire.go(remote(dqp.at[a * 2 + 1 - at.b], dq_b.at[a], s_dy, a, at.beside))
+
+    def column_dq(a):
+        remote(dq_b.at[a], dq_b.at[a], s_dy, a, at.beside).wait_recv()
+        return dqp[a * 2 + at.b].astype(F32) + dq_b[a].astype(F32)
+
+    def fold_dq(a):
+        dq_j[a] = column_dq(a).astype(BF16)
+        wire.go(remote(dq_j.at[a], dq_z.at[at.a], s_dz, at.a, at.column(a)))
+
+    round_trip(wire, [(do_all, s_do), (stat_all, s_st)], feed_forward_grads, attend_back, ship_dq, fold_dq)
+    dk2_out[...] = dk_acc[...].astype(BF16)
+    dv2_out[...] = dv_acc[...].astype(BF16)
+    value = column_dq(at.a)
+    for step in range(1, depth):
+        a = wire.near(step)
+        remote(dq_z.at[a], dq_z.at[a], s_dz, a, at.column(a)).wait_recv()
+        value += dq_z[a].astype(F32)
+    dq2 = value.astype(BF16)
+    dq2_out[...] = dq2
+    dx, dgain = norm_back_rows(h1[...], gains[1:2, :], nt(dq2, w_rest[1]))
+    small[0:1, :] = dgain
+    dh1 = dh2 + dx
+    dh1_out[...] = dh1
+    branch1 = dh1.astype(BF16)
+    branch1_out[...] = branch1
+    do1 = nt(branch1, w_rest[0]).astype(BF16)
+    do1_out[...] = do1
+    stat_own[1] = jnp.concatenate([lse1[...].T[:STAT], per_head_sums(do1.astype(F32) * o1[...].astype(F32), heads)], 0)
+    wire.slot(do1_all, at.c)[...] = do1
+    stat1_all[at.c] = stat_own[1]
+    wire.spread(do1_out, do1_all, s_do1)
+    wire.spread(stat_own.at[1], stat1_all, s_st1)
+    gmem_out[...] = (nt(dk2_out[...], w_rest[2]) + nt(dv2_out[...], w_rest[3])).astype(BF16)
+    both = [(do1_all, s_do1), (stat1_all, s_st1)]
+    for step in range(1, depth):
+        for buf, s in both:
+            wire.relay(buf, s, step)
+    for a in range(depth):
+        for buf, s in both:
+            wire.from_beside(buf, s, a)
+    wire.drain()
+
+
+def middle(peers, q2, h1, o1, lse1, w_rest, gains, mem, mask_row, mask_col, grad, co_shard, in_shard, w_out):
+    rows, slots = q2.shape[0], mem.shape[0]
+    length, depth = peers * rows, peers // 2
+    units = w_out.shape[0]
+    row = lambda dtype: sds((rows, D), dtype)
+    store = lambda n, dtype=BF16: pltpu.VMEM((n, rows, D), dtype)
+    stat = lambda n, k=STAT: pltpu.VMEM((n, k, rows), F32)
+    group = lambda width, dtype=BF16: pltpu.VMEM((WAYS * rows, width), dtype)
+    return pl.pallas_call(
+        functools.partial(middle_kernel, peers),
+        name="middle",
+        out_shape=[
+            row(BF16),
+            row(BF16),
+            row(BF16),
+            sds((slots, D), BF16),
+            sds((slots, D), BF16),
+            row(BF16),
+            row(F32),
+            row(BF16),
+            sds((length, D), BF16),
+            sds((peers, 2 * STAT, rows), F32),
+            sds((D, units), BF16),
+            sds((units, D), BF16),
+            row(BF16),
+            sds((slots, D), BF16),
+            sds((8, D), F32),
+        ],
+        in_specs=[full_spec()] * 13,
+        out_specs=[full_spec()] * 15,
+        scratch_shapes=[
+            store(peers), pltpu.VMEM((slots, D), BF16), pltpu.VMEM((slots, D), BF16),
+            store(peers), stat(peers), store(depth), stat(depth), store(depth), stat(depth), store(depth), stat(depth),
+            pltpu.VMEM((D, D), BF16), pltpu.VMEM((D, units), BF16),
+            group(D), group(D), group(units, F32), group(units), group(units), group(D), group(D), group(D), group(D),
+            store(peers), stat(peers, 2 * STAT), stat(2, 2 * STAT),
+            pltpu.VMEM((slots, D), F32), pltpu.VMEM((slots, D), F32),
+            store(peers), store(depth), store(depth), store(depth),
+        ]
+        + sems(2 * depth) + sems(3) + sems(WAYS) + sems(WAYS)
+        + sems(depth) * 4
+        + sems(WAYS) * 3
+        + sems(2 * depth) * 2
+        + sems(depth) * 2
+        + sems(2 * depth) * 2,
+        compiler_params=pltpu.CompilerParams(collective_id=2, has_side_effects=True, vmem_limit_bytes=VMEM_LIMIT),
+    )(q2, h1, o1, lse1, w_rest, gains, mem, mask_row, mask_col, grad, co_shard, in_shard, w_out)
 
 
 def reduce_kernel(peers, left_index, *refs):
@@ -1154,14 +1419,6 @@
     return dx, jnp.sum(dy * x * r, axis=0)
 
 
-def gather(x, axis_name, axis=0):
-    return lax.all_gather(x, axis_name, axis=axis, tiled=True)
-
-
-def scatter(x, axis_name, axis=0):
-    return lax.psum_scatter(x, axis_name, scatter_dimension=axis, tiled=True)
-
-
 def shards(
     tokens,
     memory,
@@ -1203,7 +1460,7 @@
     buckets = jnp.pad(bucket_table, (0, 1), constant_values=-1)[None]
     buckets_back = jnp.pad(bucket_table[::-1], (0, 1), constant_values=-1)[None]
     hot = (buckets == jnp.arange(BUCKETS, dtype=jnp.int32)[:, None]).astype(F32)
-    weights, gains, ahead, behind, q1_nat, k1_nat, v1_nat, a1, o1, h1, a2, q2, lse1 = front(
+    w_self, w_rest, gains, ahead, behind, q1_nat, k1_nat, v1_nat, a1, o1, h1, a2, q2, lse1 = front(
         peers,
         inv,
         own_facts,
@@ -1213,66 +1470,54 @@
         buckets_back,
         [self_query, self_attention_key, self_value, self_output, cross_query, cross_key, cross_value],
     )
-    wq1, wk1, wv1, wo, wq2, wk2, wv2 = [weights[i] for i in range(N_FRONT)]
-    w_co = gather(cross_output, "fsdp")
-    w_in = lax.all_to_all(hidden_in, "fsdp", split_axis=1, concat_axis=0, tiled=True)
-    k2, v2 = project(mem, wk2).astype(BF16), project(mem, wv2).astype(BF16)
     slot = index * slots + jnp.arange(slots, dtype=jnp.int32)
     hidden = jnp.where(slot % PLEN < jnp.take(passage_lengths[0], slot // PLEN), 0.0, NEGATIVE)
-    q2_all = gather(q2, "ctx")
-    part, part_lse = cross_forward(q2_all, k2, v2, hidden[None, :])
-    swap = lambda x: lax.all_to_all(x.reshape(peers, rows, x.shape[-1]), "ctx", 0, 0)
-    part, part_lse = swap(part), swap(part_lse)[:, :, :HEADS]
-    top = jnp.max(part_lse, axis=0)
-    share = jnp.exp(part_lse - top)
-    lse2 = top + jnp.log(jnp.sum(share, axis=0))
-    share = share / jnp.sum(share, axis=0)
-    out2 = jnp.sum(jnp.repeat(share, HEAD_DIM, axis=2) * part.astype(F32), axis=0)
-    o2 = out2.astype(BF16)
-    h2 = h1 + project(o2, w_co)
-    a3 = norm_scale(h2, gains[2]).astype(BF16)
-    a3_all, g_all = gather(a3, "fsdp"), gather(grad, "fsdp")
-    pre = project(a3_all, w_in)
-    act, pullback = jax.vjp(smooth_gate, pre)
-    act = act.astype(BF16)
-    out_part = project(act, hidden_out)
-    dpre = pullback(nt(g_all, hidden_out))[0].astype(BF16)
-    da3_part = nt(dpre, w_in)
-    da3 = scatter(da3_part.astype(BF16), "fsdp").astype(F32)
-    layer_output = (h2 + scatter(out_part.astype(BF16), "fsdp").astype(F32)).astype(BF16)
-    g_out = tn(act, g_all).astype(BF16)
-    g_in = tn(a3_all, dpre).astype(BF16)
-    dx, gg3 = norm_back(h2, gains[2], da3)
-    dh2 = grad.astype(F32) + dx
-    branch2 = dh2.astype(BF16)
-    do2 = nt(branch2, w_co).astype(BF16)
-    delta = lambda d, o: jnp.sum((d.astype(F32) * o).reshape(rows, HEADS, HEAD_DIM), axis=2)
-    pad4 = lambda x: jnp.pad(x, ((0, 0), (0, 4)))
-    stat2 = jnp.concatenate([pad4(lse2), pad4(delta(do2, out2))], 1)
-    do2_all = gather(do2, "ctx")
-    stat2_all = gather(stat2.T, "ctx", 1)
-    dq2_part, dk2, dv2 = cross_backward(q2_all, do2_all, stat2_all, k2, v2, hidden[:, None])
-    dq2 = scatter(dq2_part, "ctx").astype(BF16)
-    dx, gg2 = norm_back(h1, gains[1], nt(dq2, wq2))
-    dh1 = dh2 + dx
-    branch1 = dh1.astype(BF16)
-    do1 = nt(branch1, wo).astype(BF16)
-    stat1 = jnp.pad(jnp.concatenate([lse1[:, :16], pad4(delta(do1, o1.astype(F32)))], 1), ((0, 0), (0, LANES - 32)))
-    do1_all = gather(do1, "ctx")
-    stat1_all = gather(stat1, "ctx")
+    (
+        o2,
+        branch2,
+        dq2,
+        dk2,
+        dv2,
+        branch1,
+        dh1,
+        do1,
+        do1_all,
+        stat1_all,
+        g_in,
+        g_out,
+        layer_output,
+        grad_memory,
+        small_mid,
+    ) = middle(
+        peers,
+        q2,
+        h1,
+        o1,
+        lse1,
+        w_rest,
+        gains,
+        mem,
+        hidden[None, :],
+        hidden[:, None],
+        grad,
+        cross_output,
+        hidden_in,
+        hidden_out,
+    )
+    stat1_all = jnp.pad(jnp.transpose(stat1_all, (0, 2, 1)).reshape(length, 2 * STAT), ((0, 0), (0, LANES - 2 * STAT)))
+    stat1 = lax.dynamic_slice_in_dim(stat1_all, index * rows, rows)
     dq1, dk1, dv1, diag = self_backward(
         piece_order, own, q1_nat, k1_nat, v1_nat, do1_all, do1, stat1_all, stat1, ahead, behind
     )
     g_bias = jnp.einsum(
         "hr,lr->lh", diag[:HEADS], hot, precision=lax.Precision.HIGHEST, preferred_element_type=F32
     )
-    da1 = nt(dq1, wq1) + nt(dk1, wk1) + nt(dv1, wv1)
+    da1 = nt(dq1, w_self[0]) + nt(dk1, w_self[1]) + nt(dv1, w_self[2])
     tok_wide = tok.astype(F32)
     dx, gg1 = norm_back(tok_wide, gains[0], da1)
     grad_tokens = (dh1 + dx).astype(BF16)
-    grad_memory = (nt(dk2, wk2) + nt(dv2, wv2)).astype(BF16)
     small = jnp.concatenate(
-        [jnp.stack([gg1, gg2, gg3]), jnp.pad(g_bias, ((0, 0), (0, D - HEADS)))], 0
+        [gg1[None], small_mid[:2], jnp.pad(g_bias, ((0, 0), (0, D - HEADS)))], 0
     )
     small = jnp.pad(small, ((0, -small.shape[0] % 8), (0, 0)))
     pairs = [

time: 727 us -> 483 us (0.66)
  waiting for transfers between devices: 174 us -> 0 us
  Pallas kernels: 310 us -> 418 us
  blocking collectives: 93 us -> 0 us
  matrix products: 39.6 us -> 6.09 us
  between operations: 16.1 us -> 1.1 us
  local copies, waits for them, and re-layouts: 33.5 us -> 21.5 us
  starting transfers between devices: 11.7 us -> 0 us
    pallas_call x2 -> x1, Pallas kernels: 62.3 us -> 182 us  [middle(): pl.pallas_call(functools.partial(middle_kernel, peers), name='middle', ou...]
    reduce_scatter x3 -> x0, waiting for transfers between devices: 113 us -> none  [scatter(): return lax.psum_scatter(x, axis_name, scatter_dimension=axis, tiled=True)]
    all_gather x4 -> x0, blocking collectives: 93 us -> none  [gather(): return lax.all_gather(x, axis_name, axis=axis, tiled=True)]
    all_to_all x3 -> x0, waiting for transfers between devices: 32.2 us -> none  [the longest x2 32.2 us: shards(): lax.all_to_all(x.reshape(peers, rows, x.shape[-1]), 'ctx', 0, 0)]
    all_gather x4 -> x0, waiting for transfers between devices: 28.8 us -> none  [gather(): return lax.all_gather(x, axis_name, axis=axis, tiled=True)]
    dot_general x10 -> x3, matrix products: 22.3 us -> 5.84 us  [nt(): lax.dot_general(a, b, (((1,), (1,)), ((), ())), preferred_element_type=F32)]
    dot_general x7 -> x0, matrix products: 16.1 us -> none  [the longest x5 12.3 us: project(): return jnp.dot(operand, matrix, preferred_element_type=jnp.float32)]
    all_to_all x3 -> x0, starting transfers between devices: 11.4 us -> none  [the longest x2 7.13 us: shards(): lax.all_to_all(x.reshape(peers, rows, x.shape[-1]), 'ctx', 0, 0)]
  transfers between devices with their start and end apart: 10 -> 0, of which waited for: 8 -> 0; matrix products, arithmetic and copies ran while one was open for 8% -> 0% of each run, Pallas kernels for 0% -> 0%
where the time goes in v4:
time: 483 us; the launch traced here: 476 us
  Pallas kernels  418 us (87%)
  other arithmetic  28.6 us (6%)
  local copies, waits for them, and re-layouts  21.5 us (4%)
  matrix products  6.09 us (1%)
    pallas_call x1, Pallas kernels, middle(): pl.pallas_call(functools.partial(middle_kernel, peers), name='middle', ou...  182 us
    pallas_call x1, Pallas kernels, reduce_grads(): pl.pallas_call(functools.partial(reduce_kernel, peers, left_index), name=...  150 us
    pallas_call x1, Pallas kernels, front(): pl.pallas_call(functools.partial(front_kernel, peers), name='front', out_...  67.7 us
    pallas_call x1, Pallas kernels, self_backward(): pl.pallas_call(kern, name='self_backward', out_shape=[sds((rows, D), BF16...  19.3 us
    gather x15, other arithmetic, shards(): jnp.take(passage_lengths[0], slot // PLEN)  18 us

profile of v4, /device:TPU:0, one launch (start us, length us, event | category | flops | bytes accessed | tf_op | source)
XLA Modules:
  0.0 475.5 jit_solution(11462372830625006113)
XLA Ops:
  0.7 2.0 fusion.29
  2.7 5.0 %select_reduce_fusion = s32[640]{0:T(1024)S(1)} fusion(s32[]{:T(128)} %bitcast.21, s32[]{:T(128)} %bitcast.22, s32[]{:T(128)} %bitcast.23, s32[]{:T(128)} %bitcast.24, s32[]{:T(128)} %bitcast.25, s32[]{:T(128)} %bitcast.94, s32[]{:T(128)} %bitcast.26, s32[]{:T(128)S(6)} %mul.99), kind=kLoop, calls=%fused_computation.42 | loop fusion | flops 19840 | bytes 2592 | tf_op jit(solution)/shard_map/jit(_take)/gather | solution.py:1474
  12.3 8.4 %select_select_fusion = s32[640]{0:T(1024)S(1)} fusion(pred[640]{0:T(1024)(128)(4,1)S(1)} %compare_reduce_fusion, pred[640]{0:T(1024)(128)(4,1)S(1)} %compare_reduce_fusion.1, pred[640]{0:T(1024)(128)(4,1)S(1)} %compare_reduce_fusion.2, pred[640]{0:T(1024)(128)(4,1)S(1)} %compare_reduce_fusion.3, pred[640]{0:T(1024)(128)(4,1)S(1)} %compare_reduce_fusion.4, ...), kind=kLoop, calls=%fused_computation.81 | loop fusion | flops 8320 | bytes 13492 | tf_op jit(solution)/shard_map/jit(_take)/gather | solution.py:1474
  20.7 1.1 fusion.20.refs_8_
  26.9 1.6 dynamic_update_slice.7.refs_3_
  28.5 1.3 pad.19
  29.8 0.8 reverse
  31.3 1.3 select_reduce_fusion.1.refs_0_
  32.5 67.7 %front.1 = (bf16[3,768,768]{2,1,0:T(8,128)(2,1)}, bf16[4,768,768]{2,1,0:T(8,128)(2,1)}, f32[8,768]{1,0:T(8,128)}, bf16[2,12,64,2048]{3,2,1,0:T(8,128)(2,1)}, bf1...) custom-call(s32[16]{0:T(128)} %select_reduce_fusion.1.refs_0_, ...), custom_call_target="tpu_custom_call" | custom-call | tf_op jit(solution)/shard_map/front/pallas_call | solution.py:890
  100.2 181.8 %middle.1 = (bf16[128,768]{1,0:T(8,128)(2,1)}, bf16[128,768]{1,0:T(8,128)(2,1)}, bf16[128,768]{1,0:T(8,128)(2,1)}, bf16[640,768]{1,0:T(8,128)(2,1)}, bf16[640,76...) custom-call(bf16[128,768]{1,0:T(8,128)(2,1)} %get-tuple-element.52.r, ...), custom_call_target="tpu_custom_call" | custom-call | tf_op jit(solution)/shard_map/middle/pallas_call | solution.py:1211
  282.0 1.1 copy.55
  283.2 0.8 pad.21.stat_slot
  284.6 19.3 %self_backward.1 = (bf16[128,768]{1,0:T(8,128)(2,1)}, bf16[128,768]{1,0:T(8,128)(2,1)}, bf16[128,768]{1,0:T(8,128)(2,1)}, f32[16,2048]{1,0:T(8,128)}) custom-call(s32[16]{0:T(128)} %order.1, s32[2]{0:T(128)} %copy-done.9, bf16[1024,768]{1,0:T(8,128)(2,1)} %get-tuple-element.60.q_nat, bf16[1024,768]{1,0:T(8,128)(2,1)} %get-tuple-element.61.k_nat, ...), custom_call_target="tpu_custom_call" | custom-call | tf_op jit(solution)/shard_map/self_backward/pallas_call | solution.py:152
  303.9 2.0 fusion.2
  305.9 2.0 convolution_add_fusion.1
  307.8 0.8 slice_reduce_fusion
  308.7 1.9 fusion.14
  312.4 149.5 %reduce_grads.1 = (bf16[16,192,768]{2,1,0:T(8,128)(2,1)}, f32[40,768]{1,0:T(8,128)}) custom-call(bf16[128,768]{1,0:T(8,128)(2,1)} %get-tuple-element.73.refs_0_, bf16[128,768]{1,0:T(8,128)(2,1)} %get-tuple-element.54.refs_2_.refs_1_, bf16[128,768]{1,0:T(8,128)(2,1)} %get-tuple-element.74.refs_2_, bf16[640,768]{1,0:T(8,128)(2,1)} %bitcast.90, ...), custom_call_target="tpu_custom_call" | custom-call | tf_op jit(solution)/shard_map/reduce_grads/pallas_call | solution.py:1390
  461.9 3.5 convert_element_type.18
  465.4 2.2 slice_bitcast_fusion.3
  467.6 1.7 pad_maximum_fusion
  469.3 1.6 slice.150
  472.9 0.9 fusion.23
  474.4 0.9 copy.63
  (69 shorter events, 15.4 us)
Async XLA Ops:
  23.2 258.8 %copy-start.9 = (s32[2]{0:T(128)}, s32[2]{0:T(128)S(1)}, u32[]{:S(2)}) copy-start(s32[2]{0:T(128)S(1)} %get-tuple-element.91.own) | copy-start | bytes 28
  28.5 4.1 copy-start.3
  303.9 4.7 copy-start
  303.9 4.8 %copy-start.5 = (bf16[128,768]{1,0:T(8,128)(2,1)S(1)}, bf16[128,768]{1,0:T(8,128)(2,1)}, u32[]{:S(2)}) copy-start(bf16[128,768]{1,0:T(8,128)(2,1)} %get-tuple-element.71.refs_7_) | copy-start | bytes 589828
  305.8 4.8 %copy-start.7 = (f32[16,2048]{1,0:T(8,128)S(1)}, f32[16,2048]{1,0:T(8,128)}, u32[]{:S(2)}) copy-start(f32[16,2048]{1,0:T(8,128)} %get-tuple-element.84) | copy-start | bytes 393220
  305.9 4.8 %copy-start.8 = (s32[2048]{0:T(1024)S(1)}, s32[2048]{0:T(1024)}, u32[]{:S(2)}) copy-start(s32[2048]{0:T(1024)} %pad.19) | copy-start | bytes 24580
  461.9 7.4 %slice-start = ((s8[4718592]{0:T(1024)(128)(4,1)}), s8[4194304]{0:T(1024)(128)(4,1)S(1)}, s32[]{:S(2)}) async-start(s8[4718592]{0:T(1024)(128)(4,1)} %bitcast.85), calls=%async_computation | async-start | bytes 8388608
  465.4 3.9 slice-start.1
  469.3 1.6 copy-start.6
  469.3 3.5 copy-start.2
  469.3 4.4 copy-start.4
  469.3 5.1 %copy-start.1 = (bf16[640,768]{1,0:T(8,128)(2,1)S(1)}, bf16[640,768]{1,0:T(8,128)(2,1)}, u32[]{:S(2)}) copy-start(bf16[640,768]{1,0:T(8,128)(2,1)} %get-tuple-element.72) | copy-start | bytes 2949124

commit v5 on v4

--- a/solution.py
+++ b/solution.py
@@ -24,6 +24,7 @@
 F32 = jnp.float32
 BF16 = jnp.bfloat16
 VMEM_LIMIT = 60 * 2**20
+TAIL_VMEM = 63 * 2**20
 
 def nn(a, b):
     return lax.dot_general(a, b, (((1,), (0,)), ((), ())), preferred_element_type=F32)
@@ -48,118 +49,12 @@
         x = jnp.where(row & bit != 0, pltpu.roll(x, (sign * bit) % x.shape[1], 1), x)
     return x
 
-def piece_bias(tables, h, piece, length):
-    start = pl.multiple_of(length - (piece + piece % 2) * PIECE, LANES)
-    return tables[piece % 2, h, :, pl.ds(start, length)].astype(F32)
-
-def bias_rows(tables, h, own, count, length):
-    return jnp.concatenate([piece_bias(tables, h, own[i], length) for i in range(count)], 0)
-
-def bias_at(tables, h, own, count, length):
-    parts = []
-    for i in range(count):
-        parts.append(tables[own[i, 1], h, :, pl.ds(own[i, 2] * LANES, length)].astype(F32))
-    return jnp.concatenate(parts, 0)
-
-
-def add_diagonals(acc, block, piece):
-    rows, length = block.shape
-    wide = jnp.concatenate([block, jnp.zeros((rows, LANES), F32)], axis=1)
-    total = pltpu.roll(wide[0:8], LANES, 1)
-    for g in range(1, rows // 8):
-        total += pltpu.roll(wide[8 * g:8 * g + 8], LANES - 8 * g, 1)
-    start = pl.multiple_of(length - (piece - piece % 2) * PIECE - LANES, LANES)
-    where = (piece % 2, slice(None), pl.ds(start, length + LANES))
-    acc[where] += total
-
 def full_spec():
     return pl.BlockSpec(memory_space=pltpu.VMEM)
 def smem_spec():
     return pl.BlockSpec(memory_space=pltpu.SMEM)
 def sds(shape, dtype):
     return jax.ShapeDtypeStruct(shape, dtype)
-
-def self_backward_kernel(order, own, q_nat, k_nat, v_nat, do_slot, do_own, stat_slot, stat_own, delta_own, table, back_table,
-                         dq, dk, dv, diag, inv, q_own, k_own, v_own, do_nat, stat_nat, stat_t, acc):
-    length = q_nat.shape[0]
-    rows = do_own.shape[0]
-    full = 2 * length
-    slots, mine = length // PIECE, rows // PIECE
-    per = BLOCK // PIECE
-    for s in range(slots):
-        inv[order[s]] = s
-    def move(i, c):
-        src = pl.ds(pl.multiple_of(inv[i] * PIECE, PIECE), PIECE)
-        dst = pl.ds(pl.multiple_of(i * PIECE, PIECE), PIECE)
-        do_nat[dst, :] = do_slot[src, :]
-        stat_nat[dst, :] = stat_slot[src, :]
-        return c
-    lax.fori_loop(0, slots, move, 0)
-    for i in range(length // LANES):
-        stat_t[:, i * LANES:(i + 1) * LANES] = stat_nat[i * LANES:(i + 1) * LANES, :].T
-    for i in range(mine):
-        src = pl.ds(pl.multiple_of(own[i] * PIECE, PIECE), PIECE)
-        dst = slice(i * PIECE, (i + 1) * PIECE)
-        q_own[dst, :] = q_nat[src, :]
-        k_own[dst, :] = k_nat[src, :]
-        v_own[dst, :] = v_nat[src, :]
-    lane = lax.broadcasted_iota(jnp.int32, (rows, length), 1)
-    limit = jnp.concatenate([jnp.full((PIECE, 1), (own[i] // per + 1) * BLOCK, jnp.int32) for i in range(mine)], 0)
-    first = jnp.concatenate([jnp.full((PIECE, 1), (own[i] // per) * BLOCK, jnp.int32) for i in range(mine)], 0)
-    visible, seen = lane < limit, lane >= first
-    stat_lane = lax.broadcasted_iota(jnp.int32, (rows, LANES), 1)
-
-    def column(h):
-        return jnp.sum(jnp.where(stat_lane == h, stat_own[...], 0.0), axis=1, keepdims=True)
-
-    diag[...] = jnp.zeros_like(diag)
-    def pair(p, c):
-        sl = lanes_of(p)
-        q, k, v, do = q_own[:, sl], k_nat[:, sl], v_nat[:, sl], do_own[:, sl]
-        kq, vq, qa, da = k_own[:, sl], v_own[:, sl], q_nat[:, sl], do_nat[:, sl]
-        dqp = jnp.zeros((rows, LANES), F32)
-        dkp = jnp.zeros((rows, LANES), F32)
-        dvp = jnp.zeros((rows, LANES), F32)
-        for half in range(2):
-            h = 2 * p + half
-            bias = bias_rows(table, h, own, mine, length)
-            km, vm = half_mask(k, half), half_mask(v, half)
-            s = jnp.where(visible, nt(q, km) + bias, NEGATIVE)
-            e = jnp.exp(s - column(h))
-            ds = e * (nt(do, vm) - column(16 + h))
-            dqp += nn(ds.astype(BF16), km)
-            acc[...] = jnp.zeros_like(acc)
-            for i in range(mine):
-                add_diagonals(acc, ds[i * PIECE:(i + 1) * PIECE, :], own[i])
-            joined = shear(acc[0] + pltpu.roll(acc[1], full - PIECE, 1), -1)
-            diag[pl.ds(h, 1), :] = jnp.sum(pltpu.roll(joined, full - 1, 1), axis=0, keepdims=True)
-            bias = bias_rows(back_table, h, own, mine, length)
-            s = jnp.where(seen, nt(half_mask(kq, half), qa) + bias, NEGATIVE)
-            e = jnp.exp(s - stat_t[pl.ds(h, 1), :])
-            dvp += nn(e.astype(BF16), half_mask(da, half))
-            ds = e * (nt(half_mask(vq, half), da) - stat_t[pl.ds(16 + h, 1), :])
-            dkp += nn(ds.astype(BF16), half_mask(qa, half))
-        dq[:, sl] = dqp.astype(BF16)
-        dk[:, sl] = dkp.astype(BF16)
-        dv[:, sl] = dvp.astype(BF16)
-        return c
-    lax.fori_loop(0, PAIRS, pair, 0)
-
-def self_backward(order, own, q_nat, k_nat, v_nat, do_slot, do_own, stat_slot, stat_own, table, back_table):
-    length, rows = q_nat.shape[0], do_own.shape[0]
-    def kern(order, own, q_nat, k_nat, v_nat, do_slot, do_own, stat_slot, stat_own, table, back_table, *rest):
-        self_backward_kernel(order, own, q_nat, k_nat, v_nat, do_slot, do_own, stat_slot, stat_own, None, table, back_table, *rest)
-    return pl.pallas_call(
-        kern,
-        name="self_backward",
-        out_shape=[sds((rows, D), BF16)] * 3 + [sds((16, 2 * length), F32)],
-        in_specs=[smem_spec()] * 2 + [full_spec()] * 9,
-        out_specs=[full_spec()] * 4,
-        scratch_shapes=[pltpu.SMEM((length // PIECE,), jnp.int32)] + [pltpu.VMEM((rows, D), BF16)] * 3
-        + [pltpu.VMEM((length, D), BF16), pltpu.VMEM((length, LANES), F32), pltpu.VMEM((LANES, length), F32), pltpu.VMEM((2, 8, 2 * length), F32)],
-        compiler_params=pltpu.CompilerParams(vmem_limit_bytes=VMEM_LIMIT),
-    )(order, own, q_nat, k_nat, v_nat, do_slot, do_own, stat_slot, stat_own, table, back_table)
-
 
 def norm_scale(values, gain_vector):
     return (
@@ -769,19 +664,32 @@
         remote(slot, slot, sem, 3 * i + 2, at.core).wait_recv()
 
 
-def fill_tables(table, out):
+def own_bias(table, lines, own, out):
     full = table.shape[1]
+    rows, length = out.shape[1], out.shape[2]
 
     def head(h, c):
         base = shear(pltpu.roll(jnp.broadcast_to(table[pl.ds(h, 1), :], (8, full)), 1, 1), 1)
-        for parity in range(2):
-            for i in range(PIECE // 16):
-                shifts = [(8 * g - 64 * parity) % full for g in (2 * i, 2 * i + 1)]
-                both = [pltpu.roll(base, s, 1) if s else base for s in shifts]
-                out[parity, h, 16 * i : 16 * i + 16, :] = jnp.concatenate(both, 0).astype(BF16)
+        lines[0] = base
+        lines[1] = pltpu.roll(base, PIECE, 1)
+        for i in range(rows // PIECE):
+            window = lines[own[i, 1], :, pl.ds(own[i, 2] * LANES, length + LANES)]
+            for g in range(0, PIECE // 8, 2):
+                both = [pltpu.roll(window, 8 * k, 1) if k else window for k in (g, g + 1)]
+                both = jnp.concatenate(both, 0)[:, LANES:]
+                out[h, i * PIECE + 8 * g : i * PIECE + 8 * g + 16, :] = both.astype(BF16)
         return c
 
     lax.fori_loop(0, HEADS, head, 0)
+
+
+def diagonal_sums(block):
+    rows, length = block.shape
+    wide = jnp.concatenate([block, jnp.zeros((rows, LANES), F32)], axis=1)
+    total = pltpu.roll(wide[0:8], LANES, 1)
+    for g in range(1, rows // 8):
+        total += pltpu.roll(wide[8 * g : 8 * g + 8], LANES - 8 * g, 1)
+    return jnp.sum(shear(total, -1), axis=0, keepdims=True)
 
 
 N_FRONT = 7
@@ -792,7 +700,7 @@
     inv, own, tok, pack, buckets, buckets_back = refs[:6]
     shards_in = refs[6 : 6 + N_FRONT]
     (w_self, w_rest, gains, ahead, behind, q_nat, k_nat, v_nat, a1, o1, h1, a2, q2, lse) = refs[6 + N_FRONT : 20 + N_FRONT]
-    (tok_all, pack_all, table, q_own, *sem) = refs[20 + N_FRONT :]
+    (tok_all, pack_all, table, lines, q_own, *sem) = refs[20 + N_FRONT :]
     weights = [w_self.at[i] for i in range(3)] + [w_rest.at[i] for i in range(N_FRONT - 3)]
     sem_t, sem_w, sem_p = sem[0:2], sem[2:4], sem[4:6]
     wire = Wire(peers)
@@ -818,7 +726,7 @@
     for line, out in ((buckets, ahead), (buckets_back, behind)):
         hot = jnp.where(line[...] == bucket, 1.0, 0.0).astype(BF16)
         table[...] = tn(bias, hot)[0:16, :]
-        fill_tables(table, out)
+        own_bias(table, lines, own, out)
     for step in range(1, depth):
         wire.relay(tok_all, sem_t, step)
     for i in range(3):
@@ -857,7 +765,7 @@
         total = jnp.zeros((rows, LANES), F32)
         for half in range(2):
             h = 2 * p + half
-            s = jnp.where(visible, nt(q, half_mask(k, half)) + bias_at(ahead, h, own, mine, length), NEGATIVE)
+            s = jnp.where(visible, nt(q, half_mask(k, half)) + ahead[h].astype(F32), NEGATIVE)
             m = jnp.max(s, axis=1, keepdims=True)
             e = jnp.exp(s - m)
             l = jnp.sum(e, axis=1, keepdims=True)
@@ -891,7 +799,7 @@
         functools.partial(front_kernel, peers),
         name="front",
         out_shape=[sds((3, D, D), BF16), sds((N_FRONT - 3, D, D), BF16), sds((8, D), F32)]
-        + [sds((2, HEADS, PIECE, 2 * length), BF16)] * 2
+        + [sds((HEADS, rows, length), BF16)] * 2
         + [sds((length, D), BF16)] * 3
         + [block(BF16), block(BF16), block(F32), block(BF16), block(BF16), sds((rows, LANES), F32)],
         in_specs=[smem_spec()] * 2 + [full_spec()] * (4 + N_FRONT),
@@ -900,6 +808,7 @@
             pltpu.VMEM((length, D), BF16),
             pltpu.VMEM((WAYS,) + pack.shape, BF16),
             pltpu.VMEM((16, 2 * length), F32),
+            pltpu.VMEM((2, 8, 2 * length), F32),
             pltpu.VMEM((rows, D), BF16),
         ]
         + sems(2 * depth) + sems(3 * N_FRONT) + sems(WAYS),
@@ -980,12 +889,12 @@
 
 def middle_kernel(peers, *refs):
     (q2, h1, o1, lse1, w_rest, gains, mem, mask_row, mask_col, grad, co_shard, in_shard, w_out) = refs[:13]
-    (o2_out, branch2_out, dq2_out, dk2_out, dv2_out, branch1_out, dh1_out, do1_out, do1_all, stat1_all, g_in, g_out, layer_out, gmem_out, small) = refs[13:28]
+    (o2_out, branch2_out, dq2_out, dk2_out, dv2_out, branch1_out, dh1_out, do1_out, stat1_out, g_in, g_out, layer_out, gmem_out, small) = refs[13:27]
     (q_all, k2, v2, part, part_lse, from_b, from_b_lse, joined, joined_lse, from_z, from_z_lse,
      w_co, w_in, g_all, a3_all, dact, act, dpre, da3_send, da3_in, out_send, out_in,
-     do_all, stat_all, stat_own, dk_acc, dv_acc, dqp, dq_b, dq_j, dq_z, *sem) = refs[28:]
+     do_all, stat_all, stat_own, dk_acc, dv_acc, dqp, dq_b, dq_j, dq_z, *sem) = refs[27:]
     sem = [sem[2 * i : 2 * i + 2] for i in range(len(sem) // 2)]
-    (s_q, s_w, s_in, s_g, s_y, s_yl, s_z, s_zl, s_a3, s_da3, s_out, s_do, s_st, s_dy, s_dz, s_do1, s_st1) = sem
+    (s_q, s_w, s_in, s_g, s_y, s_yl, s_z, s_zl, s_a3, s_da3, s_out, s_do, s_st, s_dy, s_dz) = sem
     wire = Wire(peers)
     at, depth = wire.at, wire.depth
     rows = q2.shape[0]
@@ -1185,24 +1094,14 @@
     do1 = nt(branch1, w_rest[0]).astype(BF16)
     do1_out[...] = do1
     stat_own[1] = jnp.concatenate([lse1[...].T[:STAT], per_head_sums(do1.astype(F32) * o1[...].astype(F32), heads)], 0)
-    wire.slot(do1_all, at.c)[...] = do1
-    stat1_all[at.c] = stat_own[1]
-    wire.spread(do1_out, do1_all, s_do1)
-    wire.spread(stat_own.at[1], stat1_all, s_st1)
+    stat1_out[...] = stat_own[1]
     gmem_out[...] = (nt(dk2_out[...], w_rest[2]) + nt(dv2_out[...], w_rest[3])).astype(BF16)
-    both = [(do1_all, s_do1), (stat1_all, s_st1)]
-    for step in range(1, depth):
-        for buf, s in both:
-            wire.relay(buf, s, step)
-    for a in range(depth):
-        for buf, s in both:
-            wire.from_beside(buf, s, a)
     wire.drain()
 
 
 def middle(peers, q2, h1, o1, lse1, w_rest, gains, mem, mask_row, mask_col, grad, co_shard, in_shard, w_out):
     rows, slots = q2.shape[0], mem.shape[0]
-    length, depth = peers * rows, peers // 2
+    depth = peers // 2
     units = w_out.shape[0]
     row = lambda dtype: sds((rows, D), dtype)
     store = lambda n, dtype=BF16: pltpu.VMEM((n, rows, D), dtype)
@@ -1220,8 +1119,7 @@
             row(BF16),
             row(F32),
             row(BF16),
-            sds((length, D), BF16),
-            sds((peers, 2 * STAT, rows), F32),
+            sds((2 * STAT, rows), F32),
             sds((D, units), BF16),
             sds((units, D), BF16),
             row(BF16),
@@ -1229,7 +1127,7 @@
             sds((8, D), F32),
         ],
         in_specs=[full_spec()] * 13,
-        out_specs=[full_spec()] * 15,
+        out_specs=[full_spec()] * 14,
         scratch_shapes=[
             store(peers), pltpu.VMEM((slots, D), BF16), pltpu.VMEM((slots, D), BF16),
             store(peers), stat(peers), store(depth), stat(depth), store(depth), stat(depth), store(depth), stat(depth),
@@ -1243,180 +1141,254 @@
         + sems(depth) * 4
         + sems(WAYS) * 3
         + sems(2 * depth) * 2
-        + sems(depth) * 2
-        + sems(2 * depth) * 2,
+        + sems(depth) * 2,
         compiler_params=pltpu.CompilerParams(collective_id=2, has_side_effects=True, vmem_limit_bytes=VMEM_LIMIT),
     )(q2, h1, o1, lse1, w_rest, gains, mem, mask_row, mask_col, grad, co_shard, in_shard, w_out)
 
 
-def reduce_kernel(peers, left_index, *refs):
-    n_left = len(set(left_index))
-    n_mats = len(left_index)
-    lefts, rights = refs[:n_left], refs[n_left : n_left + n_mats]
-    g_in, g_out, small, out, small_out = refs[n_left + n_mats : n_left + n_mats + 5]
-    (prod, own, sa, ra, sb, rb, sc, rc, sd, rd, tiny, tiny_in, *sem) = refs[n_left + n_mats + 5 :]
-    sem_a, sem_b, sem_c, sem_d, sem_e, sem_f, sem_g, sem_t = [sem[2 * i : 2 * i + 2] for i in range(8)]
-    at = Place(peers)
-    depth = at.depth
-    quarter, wide = out.shape[1], out.shape[2]
-    half, part = wide // 2, quarter // depth
-    total = out.shape[0]
-    sent = []
-
-    def go(copy):
-        copy.start()
-        sent.append(copy)
-        return copy
-
-    columns = lambda b: pl.ds(pl.multiple_of(b * half, LANES), half)
+def tail_kernel(peers, *refs):
+    (inv, own, do1, stat1, q_nat, k_nat, v_nat, bias, bias_back, tok, w_self, gains, dh1, bucket_rows,
+     a1, o1, branch1, a2, dq2, mem, dk2, dv2, o2, branch2, g_in, g_out, small_mid) = refs[:27]
+    out, small_out, grad_tokens = refs[27:30]
+    (prod, ra, sb, rb, sc, rc, sd, rd, tiny, tiny_in, do_all, do_nat, stat_all, stat_rows, stat_t, q_own, k_own, v_own,
+     dq1, dk1, dv1, diagonals, s_w, *sem) = refs[30:]
+    sem = [sem[2 * i : 2 * i + 2] for i in range(len(sem) // 2)]
+    s_do, s_st, sem_a, sem_b, sem_c, sem_d, sem_e, sem_f, sem_g, sem_t = sem
+    wire = Wire(peers)
+    at, depth, go = wire.at, wire.depth, wire.go
+    rows, length = do1.shape[0], q_nat.shape[0]
+    mine, pieces = rows // PIECE, length // PIECE
+    total, quarter, wide = out.shape
+    half_width, part = wide // 2, quarter // depth
+    pairs = [(o2, branch2), (mem, dk2), (mem, dv2), (a2, dq2), (o1, branch1), (a1, dq1), (a1, dk1), (a1, dv1)]
+    n_mats = len(pairs)
+    columns = lambda b: pl.ds(pl.multiple_of(b * half_width, LANES), half_width)
     shard_rows = lambda f: pl.ds(pl.multiple_of(f * quarter, quarter), quarter)
     part_rows = lambda a: pl.ds(pl.multiple_of(a * part, part), part)
-    mine, theirs = columns(at.b), columns(1 - at.b)
-
-    greet(
-        [at.core, at.across, at.beside]
-        + [at.column(at.ahead(d)) for d in range(1, depth)]
-        + [(at.c, (1 - at.x) * 2 + 1 - at.k)]
-    )
+    own_half, other_half = columns(at.b), columns(1 - at.b)
 
     def stage_a(i):
-        prod[...] = tn(lefts[left_index[i]][...], rights[i][...])
+        left, right = pairs[i]
+        prod[i] = tn(left[...], right[...]).astype(BF16)
         for x in range(2):
-            own[i, x] = prod[shard_rows(x * 2 + at.k), :]
-            sa[i, x] = prod[shard_rows(x * 2 + 1 - at.k), :].astype(BF16)
-        go(remote(sa.at[i], ra.at[i], sem_a, i, at.core))
+            go(remote(prod.at[i, shard_rows(x * 2 + 1 - at.k)], ra.at[i, x], sem_a, 2 * i + x, at.core))
 
     def stage_b(i):
-        remote(sa.at[i], ra.at[i], sem_a, i, at.core).wait_recv()
-        sb[i] = (own[i, 1 - at.x] + ra[i, 1 - at.x].astype(F32)).astype(BF16)
+        for x in range(2):
+            remote(ra.at[i, x], ra.at[i, x], sem_a, 2 * i + x, at.core).wait_recv()
+        x = 1 - at.x
+        sb[i] = (prod[i, shard_rows(x * 2 + at.k), :].astype(F32) + ra[i, x].astype(F32)).astype(BF16)
         go(remote(sb.at[i], rb.at[i], sem_b, i, at.across))
+
+    def source(j):
+        if j < n_mats + WAYS:
+            return sc.at[j]
+        q = j - n_mats - WAYS
+        return g_out.at[q * quarter : (q + 1) * quarter]
 
     def stage_c(j):
         if j < n_mats:
             remote(sb.at[j], rb.at[j], sem_b, j, at.across).wait_recv()
-            value = own[j, at.x] + ra[j, at.x].astype(F32) + rb[j].astype(F32)
+            value = prod[j, shard_rows(at.f), :].astype(F32) + ra[j, at.x].astype(F32) + rb[j].astype(F32)
             sc[j] = value.astype(BF16)
-        go(remote(sc.at[j, :, theirs], rc.at[j], sem_c, j, at.beside))
+        go(remote(source(j).at[:, other_half], rc.at[j], sem_c, j, at.beside))
 
     def stage_d(j):
-        remote(sc.at[j, :, mine], rc.at[j], sem_c, j, at.beside).wait_recv()
-        value = sc[j, :, mine].astype(F32) + rc[j].astype(F32)
+        remote(rc.at[j], rc.at[j], sem_c, j, at.beside).wait_recv()
+        value = source(j)[:, own_half].astype(F32) + rc[j].astype(F32)
         sd[j] = value.astype(BF16)
         for d in range(1, depth):
-            go(remote(sd.at[j, part_rows(at.ahead(d))], rd.at[j, part_rows(at.a)], sem_d, j * depth + d, at.column(at.ahead(d))))
+            spot = rd.at[j, part_rows(at.a)]
+            go(remote(sd.at[j, part_rows(at.ahead(d))], spot, sem_d, j * depth + d, at.column(at.ahead(d))))
 
     def stage_e(j):
         value = sd[j, part_rows(at.a), :].astype(F32)
         for d in range(1, depth):
-            slot = rd.at[j, part_rows(at.behind(d))]
-            remote(slot, slot, sem_d, j * depth + d, at.column(at.behind(d))).wait_recv()
-            value += slot[...].astype(F32)
-        spot = out.at[j, part_rows(at.a), mine]
+            spot = rd.at[j, part_rows(at.behind(d))]
+            remote(spot, spot, sem_d, j * depth + d, at.column(at.behind(d))).wait_recv()
+            value += spot[...].astype(F32)
+        spot = out.at[j, part_rows(at.a), own_half]
         spot[...] = value.astype(BF16)
         for d in range(1, depth):
             go(remote(spot, spot, sem_e, j * depth + d, at.column(at.ahead(d))))
 
     def stage_f(j):
         for d in range(1, depth):
-            spot = out.at[j, part_rows(at.behind(d)), mine]
+            spot = out.at[j, part_rows(at.behind(d)), own_half]
             remote(spot, spot, sem_e, j * depth + d, at.column(at.behind(d))).wait_recv()
-        go(remote(out.at[j, :, mine], out.at[j, :, mine], sem_f, j, at.beside))
+        go(remote(out.at[j, :, own_half], out.at[j, :, own_half], sem_f, j, at.beside))
 
     def stage_g(j):
-        remote(out.at[j, :, theirs], out.at[j, :, theirs], sem_f, j, at.beside).wait_recv()
-
-    order = list(range(n_mats + WAYS, n_mats + 2 * WAYS)) + list(range(n_mats)) + list(range(n_mats, n_mats + WAYS))
-    for q in range(WAYS):
-        sc[n_mats + WAYS + q] = g_out[q * quarter : (q + 1) * quarter, :]
-    tiny[0] = small[...]
+        spot = out.at[j, :, other_half]
+        remote(spot, spot, sem_f, j, at.beside).wait_recv()
+
+    def send_g_in():
+        sc[n_mats + at.f] = g_in[shard_rows(at.f), :]
+        for d in range(1, WAYS):
+            f = lax.rem(at.f + d, WAYS)
+            go(remote(g_in.at[shard_rows(f)], sc.at[n_mats + at.f], sem_g, d, at.group(d)))
+
+    def have_g_in():
+        for d in range(1, WAYS):
+            spot = sc.at[n_mats + lax.rem(at.f + WAYS - d, WAYS)]
+            remote(spot, spot, sem_g, d, at.group(WAYS - d)).wait_recv()
+
     hops = [at.core, at.across, at.beside]
-    for t in range(total + 4):
-        if 4 <= t:
-            stage_g(order[t - 4])
-        if 3 <= t < total + 3:
-            stage_f(order[t - 3])
-        if 2 <= t < total + 2:
-            stage_e(order[t - 2])
-        if 1 <= t < total + 1:
-            stage_d(order[t - 1])
-        if t == total - WAYS:
-            for d in range(1, WAYS):
-                slot = sc.at[n_mats + lax.rem(at.f + WAYS - d, WAYS)]
-                remote(slot, slot, sem_g, d, at.group(WAYS - d)).wait_recv()
-        if t < total:
-            stage_c(order[t])
-        if 1 <= t <= n_mats:
-            stage_b(t - 1)
-        if t < n_mats:
-            stage_a(t)
-        if t == n_mats:
-            sc[n_mats + at.f] = g_in[shard_rows(at.f), :]
-            for d in range(1, WAYS):
-                f = lax.rem(at.f + d, WAYS)
-                go(remote(g_in.at[shard_rows(f)], sc.at[n_mats + at.f], sem_g, d, at.group(d)))
-        if t < 4:
-            if t:
-                remote(tiny.at[t - 1], tiny_in.at[t - 1], sem_t, t - 1, hops[t - 1]).wait_recv()
-                tiny[t] = tiny[t - 1] + tiny_in[t - 1]
-            if t < 3:
-                go(remote(tiny.at[t], tiny_in.at[t], sem_t, t, hops[t]))
-            else:
-                for d in range(1, depth):
-                    go(remote(tiny.at[3], tiny_in.at[2 + d], sem_t, 2 + d, at.column(at.ahead(d))))
-        if t == 4:
-            value = tiny[3]
+
+    def small_hop(t):
+        if t:
+            remote(tiny_in.at[t - 1], tiny_in.at[t - 1], sem_t, t - 1, hops[t - 1]).wait_recv()
+            tiny[t] = tiny[t - 1] + tiny_in[t - 1]
+        if t < 3:
+            go(remote(tiny.at[t], tiny_in.at[t], sem_t, t, hops[t]))
+        else:
             for d in range(1, depth):
-                remote(tiny.at[3], tiny_in.at[2 + d], sem_t, 2 + d, at.column(at.behind(d))).wait_recv()
-                value += tiny_in[2 + d]
-            small_out[...] = value
-    for copy in sent:
-        copy.wait_send()
-
-
-def reduce_grads(peers, pairs, g_in, g_out, small):
-    lefts, left_index = [], []
-    for left, _ in pairs:
-        for i, seen in enumerate(lefts):
-            if seen is left:
-                break
-        else:
-            lefts.append(left)
-            i = len(lefts) - 1
-        left_index.append(i)
-    rights = [right for _, right in pairs]
-    n, total = len(pairs), len(pairs) + 2 * WAYS
-    width = g_in.shape[1]
-    quarter, half, depth = width // WAYS, width // 2, peers // 2
+                go(remote(tiny.at[3], tiny_in.at[2 + d], sem_t, 2 + d, at.column(at.ahead(d))))
+
+    def small_end():
+        value = tiny[3]
+        for d in range(1, depth):
+            remote(tiny_in.at[2 + d], tiny_in.at[2 + d], sem_t, 2 + d, at.column(at.behind(d))).wait_recv()
+            value += tiny_in[2 + d]
+        small_out[...] = value
+
+    gathered = [(do_all, s_do), (stat_all, s_st)]
+
+    def relay(step):
+        for buf, s in gathered:
+            wire.relay(buf, s, step)
+
+    def prepare():
+        for a in range(depth):
+            for buf, s in gathered:
+                wire.from_beside(buf, s, a)
+        for c in range(peers):
+            spread = jnp.concatenate([stat_all[c], jnp.zeros((LANES - 2 * STAT, rows), F32)], 0)
+            stat_rows[c * rows : (c + 1) * rows, :] = spread.T
+        for i in range(pieces):
+            do_nat[i * PIECE : (i + 1) * PIECE, :] = do_all[pl.ds(inv[i] * PIECE, PIECE), :]
+        per = LANES // PIECE
+        for t in range(length // LANES):
+            lines = [stat_rows[pl.ds(inv[t * per + i] * PIECE, PIECE), :] for i in range(per)]
+            stat_t[:, t * LANES : (t + 1) * LANES] = jnp.concatenate(lines, 0).T
+        for i in range(mine):
+            dst = slice(i * PIECE, (i + 1) * PIECE)
+            src = pl.ds(own[i, 0] * PIECE, PIECE)
+            q_own[dst, :] = q_nat[src, :]
+            k_own[dst, :] = k_nat[src, :]
+            v_own[dst, :] = v_nat[src, :]
+
+    def own_column(i):
+        return jnp.concatenate([jnp.full((PIECE, 1), own[j, i], jnp.int32) for j in range(mine)], 0)
+
+    def attend_back(low, high):
+        lane = lax.broadcasted_iota(jnp.int32, (rows, length), 1)
+        visible, seen = lane < own_column(3), lane >= own_column(4)
+        stat_lane = lax.broadcasted_iota(jnp.int32, (rows, LANES), 1)
+        stat_own = jnp.concatenate([stat1[...], jnp.zeros((LANES - 2 * STAT, rows), F32)], 0).T
+
+        def column(h):
+            return jnp.sum(jnp.where(stat_lane == h, stat_own, 0.0), axis=1, keepdims=True)
+
+        def pair(p, c):
+            sl = lanes_of(p)
+            q, k, v, do = q_own[:, sl], k_nat[:, sl], v_nat[:, sl], do1[:, sl]
+            kq, vq, qa, da = k_own[:, sl], v_own[:, sl], q_nat[:, sl], do_nat[:, sl]
+            dq = dk = dv = jnp.zeros((rows, LANES), F32)
+            for half in range(2):
+                h = 2 * p + half
+                km, vm = half_mask(k, half), half_mask(v, half)
+                s = jnp.where(visible, nt(q, km) + bias[h].astype(F32), NEGATIVE)
+                e = jnp.exp(s - column(h))
+                ds = e * (nt(do, vm) - column(STAT + h))
+                dq += nn(ds.astype(BF16), km)
+                for i in range(mine):
+                    diagonals[i, pl.ds(h, 1), :] = diagonal_sums(ds[i * PIECE : (i + 1) * PIECE, :])
+                s = jnp.where(seen, nt(half_mask(kq, half), qa) + bias_back[h].astype(F32), NEGATIVE)
+                e = jnp.exp(s - stat_t[pl.ds(h, 1), :])
+                dv += nn(e.astype(BF16), half_mask(da, half))
+                ds = e * (nt(half_mask(vq, half), da) - stat_t[pl.ds(STAT + h, 1), :])
+                dk += nn(ds.astype(BF16), half_mask(qa, half))
+            dq1[:, sl] = dq.astype(BF16)
+            dk1[:, sl] = dk.astype(BF16)
+            dv1[:, sl] = dv.astype(BF16)
+            return c
+
+        lax.fori_loop(low, high, pair, 0)
+
+    def finish_tokens():
+        weights_here.wait()
+        da1 = nt(dq1[...], prod[5]) + nt(dk1[...], prod[6]) + nt(dv1[...], prod[7])
+        dx, dgain = norm_back_rows(tok[...].astype(F32), gains[0:1, :], da1)
+        grad_tokens[...] = (dh1[...] + dx).astype(BF16)
+        sums = jnp.zeros((STAT, BUCKETS), F32)
+        number = lax.broadcasted_iota(jnp.int32, (BUCKETS, length + LANES), 0)
+        for i in range(mine):
+            line = bucket_rows[pl.ds(own[i, 1], 1), pl.ds(own[i, 2] * LANES, length + LANES)]
+            hot = jnp.where(line == number, 1.0, 0.0).astype(BF16)
+            high, low = split(diagonals[i])
+            sums += nt(high, hot) + nt(low, hot)
+        tiny[0] = jnp.zeros(tiny.shape[1:], F32)
+        tiny[0, 0:1, :] = dgain
+        tiny[0, 1:3, :] = small_mid[0:2, :]
+        tiny[0, 8 : 8 + STAT, 0:BUCKETS] = sums
+
+    weights_here = pltpu.make_async_copy(w_self, prod.at[5:8], s_w)
+    weights_here.start()
+    greet(wire.partners())
+    wire.spread(do1, do_all, s_do)
+    wire.spread(stat1, stat_all, s_st)
+    wire.slot(do_all, at.c)[...] = do1[...]
+    stat_all[at.c] = stat1[...]
+    diagonals[...] = jnp.zeros_like(diagonals)
+    order = [12, 13, 14, 15, 0, 1, 2, 3, 4, 8, 9, 10, 11, 5, 6, 7]
+    lag = 1.5
+    events = []
+    for tick, j in enumerate(order):
+        if j < n_mats:
+            events += [(tick - 2, 1, lambda j=j: stage_a(j)), (tick - 1, 2, lambda j=j: stage_b(j))]
+        for k, stage in enumerate((stage_c, stage_d, stage_e, stage_f, stage_g)):
+            events.append((tick + k * lag, 3 + k, lambda j=j, stage=stage: stage(j)))
+    events += [(2.5, 0, send_g_in), (8.5, 0, have_g_in)]
+    events += [(0.5, 0, lambda: relay(1)), (1.5, 0, lambda: relay(2)), (1.6, 0, lambda: relay(3)), (3.5, 0, prepare)]
+    events += [(4.5 + i, 0, lambda i=i: attend_back(2 * i, 2 * i + 2)) for i in range(PAIRS // 2)]
+    events += [(8.6, 0, finish_tokens)]
+    events += [(9.5 + t, 0, lambda t=t: small_hop(t)) for t in range(4)] + [(14.5, 0, small_end)]
+    for _, _, event in sorted(events, key=lambda e: (e[0], -e[1])):
+        event()
+    wire.drain()
+
+
+def tail(peers, inv, own, do1, stat1, q_nat, k_nat, v_nat, bias, bias_back, tok, w_self, gains, dh1, bucket_rows, *rest):
+    rows, length = do1.shape[0], q_nat.shape[0]
+    n, depth = 8, peers // 2
+    total = n + 2 * WAYS
+    quarter, half = D // WAYS, D // 2
+    shard = lambda k, width=D: pltpu.VMEM((k, quarter, width), BF16)
+    row = lambda: pltpu.VMEM((rows, D), BF16)
+    tiny = lambda k: pltpu.VMEM((k, 8 + STAT, D), F32)
+    operands = (do1, stat1, q_nat, k_nat, v_nat, bias, bias_back, tok, w_self, gains, dh1, bucket_rows) + rest
     return pl.pallas_call(
-        functools.partial(reduce_kernel, peers, left_index),
-        name="reduce_grads",
-        out_shape=[sds((total, quarter, width), BF16), sds(small.shape, F32)],
-        in_specs=[full_spec()] * (len(lefts) + n + 3),
-        out_specs=[full_spec()] * 2,
+        functools.partial(tail_kernel, peers),
+        name="tail",
+        out_shape=[sds((total, quarter, D), BF16), sds((8 + STAT, D), F32), sds((rows, D), BF16)],
+        in_specs=[smem_spec()] * 2
+        + [pl.BlockSpec(memory_space=pl.ANY) if x is w_self else full_spec() for x in operands],
+        out_specs=[full_spec()] * 3,
         scratch_shapes=[
-            pltpu.VMEM((width, width), F32),
-            pltpu.VMEM((n, 2, quarter, width), F32),
-            pltpu.VMEM((n, 2, quarter, width), BF16),
-            pltpu.VMEM((n, 2, quarter, width), BF16),
-            pltpu.VMEM((n, quarter, width), BF16),
-            pltpu.VMEM((n, quarter, width), BF16),
-            pltpu.VMEM((total, quarter, width), BF16),
-            pltpu.VMEM((total, quarter, half), BF16),
-            pltpu.VMEM((total, quarter, half), BF16),
-            pltpu.VMEM((total, quarter, half), BF16),
-            pltpu.VMEM((4,) + small.shape, F32),
-            pltpu.VMEM((3 + depth,) + small.shape, F32),
+            pltpu.VMEM((n, D, D), BF16), pltpu.VMEM((n, 2, quarter, D), BF16), shard(n), shard(n),
+            shard(n + WAYS), shard(total, half), shard(total, half), shard(total, half),
+            tiny(4), tiny(3 + depth),
+            pltpu.VMEM((length, D), BF16), pltpu.VMEM((length, D), BF16),
+            pltpu.VMEM((peers, 2 * STAT, rows), F32), pltpu.VMEM((length, LANES), F32), pltpu.VMEM((LANES, length), F32),
+            row(), row(), row(), row(), row(), row(),
+            pltpu.VMEM((rows // PIECE, STAT, length + LANES), F32),
+            pltpu.SemaphoreType.DMA,
         ]
-        + sems(n) + sems(n) + sems(total) + sems(total * depth) + sems(total * depth) + sems(total) + sems(WAYS) + sems(3 + depth),
-        compiler_params=pltpu.CompilerParams(collective_id=0, has_side_effects=True, vmem_limit_bytes=VMEM_LIMIT),
-    )(*lefts, *rights, g_in, g_out, small)
-
-
-def norm_back(x, gain, dy):
-    r = lax.rsqrt(jnp.mean(x * x, axis=-1, keepdims=True) + EPSILON)
-    gdy = gain * dy
-    dx = r * gdy - x * (r * r * r) * jnp.mean(x * gdy, axis=-1, keepdims=True)
-    return dx, jnp.sum(dy * x * r, axis=0)
+        + sems(2 * depth) + sems(2 * depth)
+        + sems(2 * n) + sems(n) + sems(total) + sems(total * depth) + sems(total * depth) + sems(total) + sems(WAYS) + sems(3 + depth),
+        compiler_params=pltpu.CompilerParams(collective_id=0, has_side_effects=True, vmem_limit_bytes=TAIL_VMEM),
+    )(inv, own, *operands)
 
 
 def shards(
@@ -1451,15 +1423,16 @@
     quarter, eighth = self_query.shape[0], position_bias.shape[0]
     slots_all = jnp.arange(piece_order.shape[0], dtype=jnp.int32)
     inv = jnp.sum(jnp.where(piece_order[None, :] == slots_all[:, None], slots_all[None, :], 0), axis=1)
+    block_start = own * PIECE // BLOCK * BLOCK
     own_facts = jnp.stack(
-        [own, own % 2, (length - (own + own % 2) * PIECE) // LANES, (own * PIECE // BLOCK + 1) * BLOCK], axis=1
+        [own, own % 2, (length - (own - own % 2) * PIECE) // LANES - 1, block_start + BLOCK, block_start], axis=1
     )
     pack = jnp.zeros((N_GAINS + BUCKETS, D), BF16)
     pack = lax.dynamic_update_slice(pack, jnp.stack([self_gain, cross_gain, hidden_gain]), (0, f * quarter))
     pack = lax.dynamic_update_slice(pack, position_bias, (N_GAINS + f * eighth, 0))
     buckets = jnp.pad(bucket_table, (0, 1), constant_values=-1)[None]
     buckets_back = jnp.pad(bucket_table[::-1], (0, 1), constant_values=-1)[None]
-    hot = (buckets == jnp.arange(BUCKETS, dtype=jnp.int32)[:, None]).astype(F32)
+    bucket_rows = jnp.concatenate([jnp.roll(buckets, 1, 1), jnp.roll(buckets, 1 + PIECE, 1)], 0)
     w_self, w_rest, gains, ahead, behind, q1_nat, k1_nat, v1_nat, a1, o1, h1, a2, q2, lse1 = front(
         peers,
         inv,
@@ -1470,8 +1443,8 @@
         buckets_back,
         [self_query, self_attention_key, self_value, self_output, cross_query, cross_key, cross_value],
     )
-    slot = index * slots + jnp.arange(slots, dtype=jnp.int32)
-    hidden = jnp.where(slot % PLEN < jnp.take(passage_lengths[0], slot // PLEN), 0.0, NEGATIVE)
+    taken = jnp.arange(PLEN, dtype=jnp.int32)[None, :] < passage_lengths[0][:, None]
+    hidden = jnp.where(lax.dynamic_slice_in_dim(taken.reshape(-1), index * slots, slots), 0.0, NEGATIVE)
     (
         o2,
         branch2,
@@ -1481,8 +1454,7 @@
         branch1,
         dh1,
         do1,
-        do1_all,
-        stat1_all,
+        stat1,
         g_in,
         g_out,
         layer_output,
@@ -1504,37 +1476,41 @@
         hidden_in,
         hidden_out,
     )
-    stat1_all = jnp.pad(jnp.transpose(stat1_all, (0, 2, 1)).reshape(length, 2 * STAT), ((0, 0), (0, LANES - 2 * STAT)))
-    stat1 = lax.dynamic_slice_in_dim(stat1_all, index * rows, rows)
-    dq1, dk1, dv1, diag = self_backward(
-        piece_order, own, q1_nat, k1_nat, v1_nat, do1_all, do1, stat1_all, stat1, ahead, behind
-    )
-    g_bias = jnp.einsum(
-        "hr,lr->lh", diag[:HEADS], hot, precision=lax.Precision.HIGHEST, preferred_element_type=F32
-    )
-    da1 = nt(dq1, w_self[0]) + nt(dk1, w_self[1]) + nt(dv1, w_self[2])
-    tok_wide = tok.astype(F32)
-    dx, gg1 = norm_back(tok_wide, gains[0], da1)
-    grad_tokens = (dh1 + dx).astype(BF16)
-    small = jnp.concatenate(
-        [gg1[None], small_mid[:2], jnp.pad(g_bias, ((0, 0), (0, D - HEADS)))], 0
-    )
-    small = jnp.pad(small, ((0, -small.shape[0] % 8), (0, 0)))
-    pairs = [
-        (a1, dq1),
-        (a1, dk1),
-        (a1, dv1),
-        (o1, branch1),
-        (a2, dq2),
-        (mem, dk2),
-        (mem, dv2),
-        (o2, branch2),
-    ]
-    total, small = reduce_grads(peers, pairs, g_in, g_out, small)
+    total, small, grad_tokens = tail(
+        peers,
+        inv,
+        own_facts,
+        do1,
+        stat1,
+        q1_nat,
+        k1_nat,
+        v1_nat,
+        ahead,
+        behind,
+        tok,
+        w_self,
+        gains,
+        dh1,
+        bucket_rows,
+        a1,
+        o1,
+        branch1,
+        a2,
+        dq2,
+        mem,
+        dk2,
+        dv2,
+        o2,
+        branch2,
+        g_in,
+        g_out,
+        small_mid,
+    )
     total = total.astype(F32)
     gain = lambda i: lax.dynamic_slice_in_dim(small[i], f * quarter, quarter)
-    bias_out = lax.dynamic_slice_in_dim(small[3:], f * eighth, eighth)[:, :HEADS]
-    count = len(pairs)
+    bias_out = lax.dynamic_slice_in_dim(small[8:, :BUCKETS].T, f * eighth, eighth)[:, :HEADS]
+    places = [5, 6, 7, 4, 3, 1, 2, 0]
+    count = len(places)
     return (
         layer_output[None],
         grad_tokens[None],
@@ -1543,7 +1519,7 @@
         gain(1),
         gain(2),
         bias_out,
-        *[total[i] for i in range(count)],
+        *[total[i] for i in places],
         jnp.concatenate([total[count + i] for i in range(WAYS)], 1),
         total[count + WAYS :].reshape(-1, D),
     )

time: 483 us -> 412 us (0.85)
  Pallas kernels: 418 us -> 375 us
  other arithmetic: 28.6 us -> 8.83 us
  matrix products: 6.09 us -> 0 us
    pallas_call x1, Pallas kernels: 182 us -> 147 us  [middle(): pl.pallas_call(functools.partial(middle_kernel, peers), name='middle', ou...]
    gather x15 -> x0, other arithmetic: 18 us -> none  [shards(): jnp.take(passage_lengths[0], slot // PLEN)]
    pallas_call x2 -> x1, Pallas kernels: 169 us -> 162 us  [tail(): pl.pallas_call(functools.partial(tail_kernel, peers), name='tail', out_sh...]
    dot_general x4 -> x0, matrix products: 6.09 us -> none  [the longest x3 5.84 us: nt(): lax.dot_general(a, b, (((1,), (1,)), ((), ())), preferred_element_type=F32)]
where the time goes in v5:
time: 412 us; the launch traced here: 404 us
  Pallas kernels  375 us (91%)
  local copies, waits for them, and re-layouts  19.7 us (5%)
  other arithmetic  8.83 us (2%)
    pallas_call x1, Pallas kernels, tail(): pl.pallas_call(functools.partial(tail_kernel, peers), name='tail', out_sh...  162 us
    pallas_call x1, Pallas kernels, middle(): pl.pallas_call(functools.partial(middle_kernel, peers), name='middle', ou...  147 us
    pallas_call x1, Pallas kernels, front(): pl.pallas_call(functools.partial(front_kernel, peers), name='front', out_...  65.7 us

profile of v5, /device:TPU:0, one launch (start us, length us, event | category | flops | bytes accessed | tf_op | source)
XLA Modules:
  0.0 404.3 jit_solution(5553094972675907863)
XLA Ops:
  0.7 0.7 add_bitcast_fusion
  1.9 0.7 stack.35.refs_1_
  2.5 0.7 stack.36
  3.2 0.7 stack.37
  3.9 0.7 stack.38
  5.0 1.6 dynamic_update_slice.7.refs_3_
  6.6 1.3 pad.7
  7.9 1.3 select_reduce_fusion.refs_0_
  9.2 0.8 reverse
  10.7 65.7 %front.1 = (bf16[3,768,768]{2,1,0:T(8,128)(2,1)}, bf16[4,768,768]{2,1,0:T(8,128)(2,1)}, f32[8,768]{1,0:T(8,128)}, bf16[12,128,1024]{2,1,0:T(8,128)(2,1)}, bf16[1...) custom-call(s32[16]{0:T(128)} %select_reduce_fusion.refs_0_, ...), custom_call_target="tpu_custom_call" | custom-call | tf_op jit(solution)/shard_map/front/pallas_call | solution.py:798
  76.6 0.9 broadcast_in_dim.60.refs_8_
  78.0 147.1 %middle.1 = (bf16[128,768]{1,0:T(8,128)(2,1)}, bf16[128,768]{1,0:T(8,128)(2,1)}, bf16[128,768]{1,0:T(8,128)(2,1)}, bf16[640,768]{1,0:T(8,128)(2,1)}, bf16[640,76...) custom-call(bf16[128,768]{1,0:T(8,128)(2,1)} %get-tuple-element.48.r, ...), custom_call_target="tpu_custom_call" | custom-call | tf_op jit(solution)/shard_map/middle/pallas_call | solution.py:1110
  225.7 0.7 pad_add_fusion.1
  227.2 161.7 %tail.1 = (bf16[16,192,768]{2,1,0:T(8,128)(2,1)}, f32[24,768]{1,0:T(8,128)}, bf16[128,768]{1,0:T(8,128)(2,1)}) custom-call(s32[16]{0:T(128)} %select_reduce_fusion.refs_0_, s32[2,5]{1,0:T(2,128)} %stack.35.refs_1_, bf16[128,768]{1,0:T(8,128)(2,1)} %get-tuple-element.55.refs_2_, f32[32,128]{1,0:T(8,128)} %get-tuple-element.56.refs_3_, ...), custom_call_target="tpu_custom_call" | custom-call | tf_op jit(solution)/shard_map/tail/pallas_call | solution.py:1371
  389.0 3.5 convert_element_type.3
  392.5 2.2 slice_bitcast_fusion.3
  394.7 1.7 pad_maximum_fusion
  396.4 1.6 slice.109
  398.0 0.9 fusion.3
  399.5 0.7 slice.77
  400.3 0.7 copy.56
  401.6 0.7 copy.62
  402.3 0.7 copy.63
  403.0 0.9 copy.64
  (39 shorter events, 5.2 us)
Async XLA Ops:
  0.7 75.7 %copy-start.5 = (s32[1,20]{1,0:T(1,128)S(1)}, s32[1,20]{1,0:T(1,128)}, u32[]{:S(2)}) copy-start(s32[1,20]{1,0:T(1,128)} %param.24) | copy-start | bytes 244
  6.6 4.1 %copy-start.1 = (bf16[48,768]{1,0:T(8,128)(2,1)}, bf16[48,768]{1,0:T(8,128)(2,1)S(1)}, u32[]{:S(2)}) copy-start(bf16[48,768]{1,0:T(8,128)(2,1)S(1)} %dynamic_update_slice.7.refs_3_) | copy-start | bytes 221188
  78.0 147.1 %copy-start.4 = (s32[2048]{0:T(1024)S(1)}, s32[2048]{0:T(1024)}, u32[]{:S(2)}) copy-start(s32[2048]{0:T(1024)} %pad.7) | copy-start | bytes 24580
  389.0 7.4 %slice-start = ((s8[4718592]{0:T(1024)(128)(4,1)}), s8[4194304]{0:T(1024)(128)(4,1)S(1)}, s32[]{:S(2)}) async-start(s8[4718592]{0:T(1024)(128)(4,1)} %bitcast.50), calls=%async_computation | async-start | bytes 8388608
  392.5 3.9 slice-start.1
  396.4 5.2 %copy-start.2 = (bf16[128,768]{1,0:T(8,128)(2,1)S(1)}, bf16[128,768]{1,0:T(8,128)(2,1)}, u32[]{:S(2)}) copy-start(bf16[128,768]{1,0:T(8,128)(2,1)} %get-tuple-element.54) | copy-start | bytes 589828
  396.4 5.9 %copy-start.3 = (bf16[128,768]{1,0:T(8,128)(2,1)S(1)}, bf16[128,768]{1,0:T(8,128)(2,1)}, u32[]{:S(2)}) copy-start(bf16[128,768]{1,0:T(8,128)(2,1)} %get-tuple-element.75) | copy-start | bytes 589828
  396.4 6.6 %copy-start = (bf16[640,768]{1,0:T(8,128)(2,1)S(1)}, bf16[640,768]{1,0:T(8,128)(2,1)}, u32[]{:S(2)}) copy-start(bf16[640,768]{1,0:T(8,128)(2,1)} %get-tuple-element.76) | copy-start | bytes 2949124

commit v6 on v5

--- a/solution.py
+++ b/solution.py
@@ -51,6 +51,10 @@
 
 def full_spec():
     return pl.BlockSpec(memory_space=pltpu.VMEM)
+def any_spec():
+    return pl.BlockSpec(memory_space=pl.ANY)
+
+
 def smem_spec():
     return pl.BlockSpec(memory_space=pltpu.SMEM)
 def sds(shape, dtype):
@@ -584,6 +588,21 @@
     )
 
 
+def apart(src, dst, sems, send_index, recv_index, target):
+    return pltpu.make_async_remote_copy(
+        src_ref=src,
+        dst_ref=dst,
+        send_sem=sems[0].at[send_index],
+        recv_sem=sems[1].at[recv_index],
+        device_id=target,
+        device_id_type=MESH,
+    )
+
+
+def line_sems(depth, chunks):
+    return sems((2 * depth + 2) * chunks)
+
+
 def sems(count):
     return [pltpu.SemaphoreType.DMA((count,)), pltpu.SemaphoreType.DMA((count,))]
 
@@ -596,11 +615,18 @@
 
     def go(self, copy):
         copy.start()
-        self.sent.append(copy)
+        self.sent.append((None, copy.wait_send))
+
+    def go_if(self, condition, make):
+        pl.when(condition)(lambda: make().start())
+        self.sent.append((condition, lambda: make().wait_send()))
 
     def drain(self):
-        for copy in self.sent:
-            copy.wait_send()
+        for condition, wait in self.sent:
+            if condition is None:
+                wait()
+            else:
+                pl.when(condition)(wait)
 
     def partners(self):
         at = self.at
@@ -616,28 +642,81 @@
         mirrored = jnp.where(step - 1 < last - a, step - 1, step)
         return jnp.where(2 * a < last, low, last - mirrored)
 
+    def piece(self, buf, c, chunk, chunks):
+        if len(buf.shape) == 3:
+            size = buf.shape[1] // chunks
+            return buf.at[c, chunk * size : (chunk + 1) * size]
+        rows = buf.shape[0] // (2 * self.depth)
+        size = rows // chunks
+        return buf.at[pl.ds(pl.multiple_of(c * rows + chunk * size, size), size)]
+
     def slot(self, buf, c):
-        if len(buf.shape) == 3:
-            return buf.at[c]
-        rows = buf.shape[0] // (2 * self.depth)
-        return buf.at[pl.ds(pl.multiple_of(c * rows, rows), rows)]
-
-    def spread(self, src, buf, sem):
+        return self.piece(buf, c, 0, 1)
+
+    def pass_on(self, src, dst, sem, up, beside, own, chunk, chunks, origin):
+        at, a = self.at, self.at.a
+        line = origin * chunks + chunk
+        side = (self.depth + origin) * chunks + chunk
+        for step in (1, -1):
+            if own or (step == 1) == up:
+                first = (2 * self.depth + (step == 1)) * chunks + chunk if own else line
+                self.go_if(
+                    a + 1 < self.depth if step == 1 else a > 0,
+                    lambda step=step, first=first: apart(src, dst, sem, first, line, at.column(a + step)),
+                )
+        if beside:
+            self.go(apart(src, dst, sem, side, side, at.beside))
+
+    def spread(self, src, buf, sem, chunks):
         at = self.at
-        slot = self.slot(buf, at.c)
-        self.go(remote(src, slot, sem, at.a, at.beside))
-        for step in range(1, self.depth):
-            self.go(remote(src, slot, sem, self.depth + at.a, at.column(self.near(step))))
-
-    def relay(self, buf, sem, step):
-        a = self.near(step)
-        slot = self.slot(buf, a * 2 + self.at.b)
-        remote(slot, slot, sem, self.depth + a, self.at.beside).wait_recv()
-        self.go(remote(slot, slot, sem, a, self.at.beside))
-
-    def from_beside(self, buf, sem, a):
-        slot = self.slot(buf, a * 2 + 1 - self.at.b)
-        remote(slot, slot, sem, a, self.at.beside).wait_recv()
+        size = src.shape[0] // chunks
+        for chunk in range(chunks):
+            part = src.at[chunk * size : (chunk + 1) * size]
+            self.pass_on(part, self.piece(buf, at.c, chunk, chunks), sem, True, True, True, chunk, chunks, at.a)
+
+    def relay(self, gathered, step):
+        at, depth = self.at, self.depth
+        for buf, sem, chunks in gathered:
+            for chunk in range(chunks):
+                for up in (True, False):
+                    origin = at.a - step if up else at.a + step
+                    inside = origin >= 0 if up else origin < depth
+                    onward = at.a + 1 < depth if up else at.a > 0
+                    line = origin * chunks + chunk
+                    side = (depth + origin) * chunks + chunk
+                    spot = lambda: self.piece(buf, origin * 2 + at.b, chunk, chunks)
+                    target = at.column(at.a + 1 if up else at.a - 1)
+
+                    def forward(_):
+                        return apart(spot(), spot(), sem, line, line, target)
+
+                    def sideways(_):
+                        return apart(spot(), spot(), sem, side, side, at.beside)
+
+                    @pl.when(inside)
+                    def _():
+                        apart(spot(), spot(), sem, line, line, at.beside).wait_recv()
+                        sideways(0).start()
+                        pl.when(onward)(lambda: forward(0).start())
+
+                    self.sent.append((inside, self.later(buf, sem, side, origin, chunk, chunks, at.beside)))
+                    self.sent.append(
+                        (jnp.logical_and(inside, onward), self.later(buf, sem, line, origin, chunk, chunks, target))
+                    )
+
+    def later(self, buf, sem, index, origin, chunk, chunks, target):
+        def wait():
+            spot = self.piece(buf, origin * 2 + self.at.b, chunk, chunks)
+            apart(spot, spot, sem, index, index, target).wait_send()
+
+        return wait
+
+    def from_beside(self, gathered, a):
+        for buf, sem, chunks in gathered:
+            for chunk in range(chunks):
+                spot = self.piece(buf, a * 2 + 1 - self.at.b, chunk, chunks)
+                index = (self.depth + a) * chunks + chunk
+                apart(spot, spot, sem, index, index, self.at.beside).wait_recv()
 
     def shard(self, full, f):
         quarter = full.shape[0] // WAYS
@@ -664,6 +743,55 @@
         remote(slot, slot, sem, 3 * i + 2, at.core).wait_recv()
 
 
+def two_heads(x):
+    return jnp.concatenate([half_mask(x, 0), half_mask(x, 1)], 0)
+
+
+def ones_beside(x):
+    ones = jnp.ones_like(x)
+    return jnp.concatenate([two_heads(x), two_heads(ones)], 1)
+
+
+def softmax_pair(scores, v, stats, p):
+    weights, tops = [], []
+    for s in scores:
+        m = jnp.max(s, axis=1, keepdims=True)
+        weights.append(jnp.exp(s - m).astype(BF16))
+        tops.append(m)
+    both = nn(jnp.concatenate(weights, 1), ones_beside(v))
+    sums = both[:, LANES:]
+    logs = jnp.log(sums)
+    turned = pltpu.roll(logs, HEAD_DIM, 1)
+    lane = lax.broadcasted_iota(jnp.int32, logs.shape, 1)
+    inside = lane < HEAD_DIM
+    stats = jnp.where(lane == 2 * p, tops[0] + jnp.where(inside, logs, turned), stats)
+    stats = jnp.where(lane == 2 * p + 1, tops[1] + jnp.where(inside, turned, logs), stats)
+    return both[:, :LANES] / sums, stats
+
+
+def fill_inverse(order, inv):
+    count = order.shape[0]
+    for p in range(count):
+        slot = jnp.int32(0)
+        for s in range(count):
+            slot = jnp.where(order[s] == p, s, slot)
+        inv[p] = slot
+
+
+def own_facts(order, c, count, length):
+    per = (BLOCK // PIECE).bit_length() - 1
+    facts = []
+    for i in range(count):
+        n = order[c * count + i]
+        start = lax.shift_right_logical(n, per) * BLOCK
+        facts.append((n, n & 1, length // LANES - 1 - lax.shift_right_logical(n, 1), start + BLOCK, start))
+    return facts
+
+
+def own_column(facts, i):
+    return jnp.concatenate([jnp.full((PIECE, 1), fact[i], jnp.int32) for fact in facts], 0)
+
+
 def own_bias(table, lines, own, out):
     full = table.shape[1]
     rows, length = out.shape[1], out.shape[2]
@@ -673,7 +801,7 @@
         lines[0] = base
         lines[1] = pltpu.roll(base, PIECE, 1)
         for i in range(rows // PIECE):
-            window = lines[own[i, 1], :, pl.ds(own[i, 2] * LANES, length + LANES)]
+            window = lines[own[i][1], :, pl.ds(own[i][2] * LANES, length + LANES)]
             for g in range(0, PIECE // 8, 2):
                 both = [pltpu.roll(window, 8 * k, 1) if k else window for k in (g, g + 1)]
                 both = jnp.concatenate(both, 0)[:, LANES:]
@@ -692,15 +820,16 @@
     return jnp.sum(shear(total, -1), axis=0, keepdims=True)
 
 
-N_FRONT = 7
+N_FRONT = 5
+CHUNKS = 2
 N_GAINS = 16
 
 
 def front_kernel(peers, *refs):
-    inv, own, tok, pack, buckets, buckets_back = refs[:6]
-    shards_in = refs[6 : 6 + N_FRONT]
-    (w_self, w_rest, gains, ahead, behind, q_nat, k_nat, v_nat, a1, o1, h1, a2, q2, lse) = refs[6 + N_FRONT : 20 + N_FRONT]
-    (tok_all, pack_all, table, lines, q_own, *sem) = refs[20 + N_FRONT :]
+    order, tok, gain1, gain2, gain3, bias_shard, buckets = refs[:7]
+    shards_in = refs[7 : 7 + N_FRONT]
+    (w_self_out, w_rest_out, gains, ahead_out, behind_out, q_out, k_out, v_out, a1, o1, h1, a2, q2, lse) = refs[7 + N_FRONT : 21 + N_FRONT]
+    (tok_all, pack, pack_all, table, lines, q_own, w_self, w_rest, ahead, behind, q_nat, k_nat, v_nat, s_keep, inv, *sem) = refs[21 + N_FRONT :]
     weights = [w_self.at[i] for i in range(3)] + [w_rest.at[i] for i in range(N_FRONT - 3)]
     sem_t, sem_w, sem_p = sem[0:2], sem[2:4], sem[4:6]
     wire = Wire(peers)
@@ -708,10 +837,27 @@
     rows = tok.shape[0]
     length = peers * rows
     mine, per = rows // PIECE, BLOCK // PIECE
+    kept = []
+
+    def keep(i, src, dst):
+        copy = pltpu.make_async_copy(src, dst, s_keep.at[i])
+        copy.start()
+        kept.append(copy)
+
+    quarter = gain1.shape[1]
+    spot = lax.broadcasted_iota(jnp.int32, (quarter, D), 0) + at.f * quarter
+    place = jnp.where(lax.broadcasted_iota(jnp.int32, (quarter, D), 1) == spot, 1.0, 0.0).astype(BF16)
+    pack[...] = jnp.zeros_like(pack)
+    for i, gain in enumerate((gain1, gain2, gain3)):
+        pack[i : i + 1, :] = nn(gain[...], place)
+    eighth, heads = bias_shard.shape
+    spot = lax.broadcasted_iota(jnp.int32, (BUCKETS, eighth), 1) + at.f * eighth
+    place = jnp.where(lax.broadcasted_iota(jnp.int32, (BUCKETS, eighth), 0) == spot, 1.0, 0.0).astype(BF16)
+    pack[N_GAINS:, 0:heads] = nn(place, bias_shard[...])
     greet(wire.partners())
     for d in range(1, WAYS):
         wire.go(remote(pack, pack_all.at[at.f], sem_p, d, at.group(d)))
-    wire.spread(tok, tok_all, sem_t)
+    wire.spread(tok, tok_all, sem_t, CHUNKS)
     for i in range(3):
         wire.weight_start(shards_in[i], weights[i], sem_w, i)
     wire.slot(tok_all, at.c)[...] = tok[...]
@@ -719,16 +865,27 @@
     for d in range(1, WAYS):
         slot = pack_all.at[lax.rem(at.f + WAYS - d, WAYS)]
         remote(slot, slot, sem_p, d, at.group(WAYS - d)).wait_recv()
-    everything = pack_all[0].astype(F32) + pack_all[1].astype(F32) + pack_all[2].astype(F32) + pack_all[3].astype(F32)
+    everything = pack_all[0] + pack_all[1] + pack_all[2] + pack_all[3]
+    fill_inverse(order, inv)
+    own = own_facts(order, at.c, mine, length)
     gains[...] = everything[0:8, :]
     bias = everything[N_GAINS:, 0:LANES].astype(BF16)
     bucket = lax.broadcasted_iota(jnp.int32, (bias.shape[0], 2 * length), 0)
-    for line, out in ((buckets, ahead), (buckets_back, behind)):
-        hot = jnp.where(line[...] == bucket, 1.0, 0.0).astype(BF16)
-        table[...] = tn(bias, hot)[0:16, :]
-        own_bias(table, lines, own, out)
+    hot = jnp.where(buckets[...] == bucket, 1.0, 0.0).astype(BF16)
+    table[0] = tn(bias, hot)[0:16, :]
+    shifted = pltpu.roll(table[0], 1, 1).astype(BF16)
+    row = lax.broadcasted_iota(jnp.int32, (LANES, LANES), 0)
+    mirror = jnp.where(row + lax.broadcasted_iota(jnp.int32, (LANES, LANES), 1) == LANES - 1, 1.0, 0.0).astype(BF16)
+    tiles = 2 * length // LANES
+    for t in range(tiles):
+        u = tiles - 1 - t
+        table[1, :, t * LANES : (t + 1) * LANES] = nn(shifted[:, u * LANES : (u + 1) * LANES], mirror)
+
+    gathered = [(tok_all, sem_t, CHUNKS)]
     for step in range(1, depth):
-        wire.relay(tok_all, sem_t, step)
+        wire.relay(gathered, step)
+    own_bias(table.at[0], lines, own, ahead)
+    keep(3, ahead, ahead_out)
     for i in range(3):
         wire.weight_relay(weights[i], sem_w, i)
     for i in range(3, N_FRONT):
@@ -737,8 +894,9 @@
     a1[...] = normed(tok[...].astype(F32), first).astype(BF16)
     for i in range(3):
         wire.weight_ready(weights[i], sem_w, i)
-    for step in range(depth):
-        wire.from_beside(tok_all, sem_t, step)
+    keep(0, w_self, w_self_out)
+    for a in range(depth):
+        wire.from_beside(gathered, a)
 
     def tile(t, c):
         parts = []
@@ -752,32 +910,27 @@
 
     lax.fori_loop(0, length // BLOCK, tile, 0)
     for i in range(mine):
-        q_own[i * PIECE : (i + 1) * PIECE, :] = q_nat[pl.ds(own[i, 0] * PIECE, PIECE), :]
+        q_own[i * PIECE : (i + 1) * PIECE, :] = q_nat[pl.ds(own[i][0] * PIECE, PIECE), :]
+    for i, (src, dst) in enumerate(((q_nat, q_out), (k_nat, k_out), (v_nat, v_out))):
+        keep(5 + i, src, dst)
     wire.weight_relay(weights[3], sem_w, 3)
     lane = lax.broadcasted_iota(jnp.int32, (rows, length), 1)
-    limit = jnp.concatenate([jnp.full((PIECE, 1), own[i, 3], jnp.int32) for i in range(mine)], 0)
-    visible = lane < limit
-    stat_lane = lax.broadcasted_iota(jnp.int32, (rows, LANES), 1)
+    visible = lane < own_column(own, 3)
 
     def pair(p, stats):
         sl = lanes_of(p)
-        q, k, v = q_own[:, sl], k_nat[:, sl], v_nat[:, sl]
-        total = jnp.zeros((rows, LANES), F32)
+        s = nt(q_own[:, sl], two_heads(k_nat[:, sl]))
+        scores = []
         for half in range(2):
-            h = 2 * p + half
-            s = jnp.where(visible, nt(q, half_mask(k, half)) + ahead[h].astype(F32), NEGATIVE)
-            m = jnp.max(s, axis=1, keepdims=True)
-            e = jnp.exp(s - m)
-            l = jnp.sum(e, axis=1, keepdims=True)
-            total += nn(e.astype(BF16), half_mask(v, half)) / l
-            stats = jnp.where(stat_lane == h, m + jnp.log(l), stats)
-        o1[:, sl] = total.astype(BF16)
+            biased = s[:, half * length : (half + 1) * length] + ahead[2 * p + half].astype(F32)
+            scores.append(jnp.where(visible, biased, NEGATIVE))
+        value, stats = softmax_pair(scores, v_nat[:, sl], stats, p)
+        o1[:, sl] = value.astype(BF16)
         return stats
 
-    stats = lax.fori_loop(0, PAIRS // 2, pair, jnp.zeros((rows, LANES), F32))
+    stats = lax.fori_loop(0, PAIRS // 2, pair, jnp.zeros((rows, LANES), F32), unroll=True)
     wire.weight_relay(weights[4], sem_w, 4)
-    lse[...] = lax.fori_loop(PAIRS // 2, PAIRS, pair, stats)
-    wire.weight_relay(weights[5], sem_w, 5)
+    lse[...] = lax.fori_loop(PAIRS // 2, PAIRS, pair, stats, unroll=True)
     wire.weight_ready(weights[3], sem_w, 3)
     h = tok[...].astype(F32) + nn(o1[...], weights[3][...])
     h1[...] = h
@@ -785,13 +938,15 @@
     a2[...] = a
     wire.weight_ready(weights[4], sem_w, 4)
     q2[...] = nn(a, weights[4][...]).astype(BF16)
-    wire.weight_relay(weights[6], sem_w, 6)
-    for i in (5, 6):
-        wire.weight_ready(weights[i], sem_w, i)
+    keep(1, w_rest, w_rest_out)
+    own_bias(table.at[1], lines, own, behind)
+    keep(4, behind, behind_out)
+    for copy in kept:
+        copy.wait()
     wire.drain()
 
 
-def front(peers, inv, own, tok, pack, buckets, buckets_back, weight_shards):
+def front(peers, order, tok, gain_shards, bias_shard, buckets, weight_shards):
     rows = tok.shape[0]
     length, depth = peers * rows, peers // 2
     block = lambda dtype: sds((rows, D), dtype)
@@ -802,18 +957,24 @@
         + [sds((HEADS, rows, length), BF16)] * 2
         + [sds((length, D), BF16)] * 3
         + [block(BF16), block(BF16), block(F32), block(BF16), block(BF16), sds((rows, LANES), F32)],
-        in_specs=[smem_spec()] * 2 + [full_spec()] * (4 + N_FRONT),
-        out_specs=[full_spec()] * 14,
+        in_specs=[smem_spec()] + [full_spec()] * (6 + N_FRONT),
+        out_specs=[any_spec() if i in (0, 1, 3, 4, 5, 6, 7) else full_spec() for i in range(14)],
         scratch_shapes=[
             pltpu.VMEM((length, D), BF16),
-            pltpu.VMEM((WAYS,) + pack.shape, BF16),
-            pltpu.VMEM((16, 2 * length), F32),
+            pltpu.VMEM((N_GAINS + BUCKETS, D), F32),
+            pltpu.VMEM((WAYS, N_GAINS + BUCKETS, D), F32),
+            pltpu.VMEM((2, 16, 2 * length), F32),
             pltpu.VMEM((2, 8, 2 * length), F32),
             pltpu.VMEM((rows, D), BF16),
+            pltpu.VMEM((3, D, D), BF16),
+            pltpu.VMEM((N_FRONT - 3, D, D), BF16),
         ]
-        + sems(2 * depth) + sems(3 * N_FRONT) + sems(WAYS),
+        + [pltpu.VMEM((HEADS, rows, length), BF16)] * 2
+        + [pltpu.VMEM((length, D), BF16)] * 3
+        + [pltpu.SemaphoreType.DMA((8,)), pltpu.SMEM(order.shape, jnp.int32)]
+        + line_sems(depth, CHUNKS) + sems(3 * N_FRONT) + sems(WAYS),
         compiler_params=pltpu.CompilerParams(collective_id=1, has_side_effects=True, vmem_limit_bytes=VMEM_LIMIT),
-    )(inv, own, tok, pack, buckets, buckets_back, *weight_shards)
+    )(order, tok, *gain_shards, bias_shard, buckets, *weight_shards)
 
 
 STAT = 16
@@ -853,46 +1014,38 @@
     return dx, jnp.sum(dy * x * r, axis=0, keepdims=True)
 
 
-def round_trip(wire, gathered, filler, compute, ship, fold):
+def round_trip(wire, gathered, fillers, compute, ship, fold):
     at = wire.at
     b = at.b
     first, second, third = [wire.near(step) for step in (1, 2, 3)]
-
-    def relay(step):
-        for buf, sem in gathered:
-            wire.relay(buf, sem, step)
-
-    def ready(a):
-        for buf, sem in gathered:
-            wire.from_beside(buf, sem, a)
-
-    filler()
-    relay(1)
-    ready(at.a)
+    for step in range(1, wire.depth):
+        fillers[step - 1]()
+        wire.relay(gathered, step)
+    for filler in fillers[wire.depth - 1 :]:
+        filler()
+    wire.from_beside(gathered, at.a)
     compute(at.c, at.a * 2 + 1 - b)
     ship(at.a)
-    relay(2)
-    relay(3)
-    compute(first * 2 + b, second * 2 + b)
-    ready(third)
-    ready(second)
-    compute(third * 2 + 1 - b, second * 2 + 1 - b)
+    wire.from_beside(gathered, third)
+    compute(third * 2 + 1 - b, third * 2 + b)
     ship(third)
+    wire.from_beside(gathered, second)
+    compute(second * 2 + 1 - b, second * 2 + b)
     ship(second)
-    ready(first)
-    compute(third * 2 + b, first * 2 + 1 - b)
+    fold(third)
+    wire.from_beside(gathered, first)
+    compute(first * 2 + 1 - b, first * 2 + b)
     ship(first)
-    fold(third)
     fold(second)
     fold(first)
 
 
 def middle_kernel(peers, *refs):
-    (q2, h1, o1, lse1, w_rest, gains, mem, mask_row, mask_col, grad, co_shard, in_shard, w_out) = refs[:13]
-    (o2_out, branch2_out, dq2_out, dk2_out, dv2_out, branch1_out, dh1_out, do1_out, stat1_out, g_in, g_out, layer_out, gmem_out, small) = refs[13:27]
+    (lengths, q2, h1, o1, lse1, w_rest, gains, mem, grad, ck_shard, cv_shard, co_shard, in_shard, w_out) = refs[:14]
+    (o2_out, branch2_out, dq2_out, dk2_out, dv2_out, branch1_out, dh1_out, do1_out, stat1_out, g_in, g_out, layer_out, gmem_out, small) = refs[14:28]
     (q_all, k2, v2, part, part_lse, from_b, from_b_lse, joined, joined_lse, from_z, from_z_lse,
-     w_co, w_in, g_all, a3_all, dact, act, dpre, da3_send, da3_in, out_send, out_in,
-     do_all, stat_all, stat_own, dk_acc, dv_acc, dqp, dq_b, dq_j, dq_z, *sem) = refs[27:]
+     w_ck, w_cv, w_co, w_in, g_all, a3_all, dact, act, dpre, da3_send, da3_in, out_send, out_in,
+     do_all, stat_all, stat_own, dk_acc, dv_acc, dqp, dq_b, dq_j, dq_z, mask, *sem) = refs[28:]
     sem = [sem[2 * i : 2 * i + 2] for i in range(len(sem) // 2)]
     (s_q, s_w, s_in, s_g, s_y, s_yl, s_z, s_zl, s_a3, s_da3, s_out, s_do, s_st, s_dy, s_dz) = sem
     wire = Wire(peers)
@@ -903,40 +1056,60 @@
     units = w_out.shape[0]
     block = lambda f: pl.ds(pl.multiple_of(f * rows, rows), rows)
     greet(wire.partners())
-    wire.spread(q2, q_all, s_q)
+    wire.spread(q2, q_all, s_q, CHUNKS)
+    wire.weight_start(ck_shard, w_ck, s_w, 1)
+    wire.weight_start(cv_shard, w_cv, s_w, 2)
     q_all[at.c] = q2[...]
-    wire.weight_start(co_shard, w_co, s_w, 0)
-    for d in range(1, WAYS):
-        f = lax.rem(at.f + d, WAYS)
-        wire.go(remote(grad, g_all.at[block(at.f)], s_g, d, at.group(d)))
-        wire.go(remote(in_shard.at[:, pl.ds(pl.multiple_of(f * units, LANES), units)], wire.shard(w_in, at.f), s_in, d, at.group(d)))
     g_all[block(at.f), :] = grad[...]
     wire.shard(w_in, at.f)[...] = in_shard[:, pl.ds(pl.multiple_of(at.f * units, LANES), units)]
 
+    slots, passages = mem.shape[0], lengths.shape[1]
+    log = PLEN.bit_length() - 1
+
+    def hidden(shape, axis):
+        slot = lax.broadcasted_iota(jnp.int32, shape, axis) + at.c * slots
+        first = at.c * slots // PLEN
+        taken = jnp.zeros(shape, jnp.int32)
+        for i in range(slots // PLEN + 2):
+            size = lengths[0, jnp.minimum(first + i, passages - 1)]
+            taken = jnp.where(lax.shift_right_logical(slot, log) == first + i, size, taken)
+        return jnp.where((slot & (PLEN - 1)) < taken, 0.0, NEGATIVE)
+
+    def fill_mask():
+        mask[...] = hidden(mask.shape, 0)
+
+    def next_weights():
+        wire.weight_relay(w_ck, s_w, 1)
+        wire.weight_start(co_shard, w_co, s_w, 0)
+
     def project_memory():
-        k2[...] = nn(mem[...], w_rest[2]).astype(BF16)
-        v2[...] = nn(mem[...], w_rest[3]).astype(BF16)
-
-    stat_lane = lax.broadcasted_iota(jnp.int32, (2 * rows, LANES), 1)
+        wire.weight_relay(w_cv, s_w, 2)
+        feed_forward_operands()
+        wire.weight_ready(w_ck, s_w, 1)
+        k2[...] = nn(mem[...], w_ck[...]).astype(BF16)
+        wire.weight_ready(w_cv, s_w, 2)
+        v2[...] = nn(mem[...], w_cv[...]).astype(BF16)
+
+    def feed_forward_operands():
+        for d in range(1, WAYS):
+            f = lax.rem(at.f + d, WAYS)
+            part = in_shard.at[:, pl.ds(pl.multiple_of(f * units, LANES), units)]
+            wire.go(remote(grad, g_all.at[block(at.f)], s_g, d, at.group(d)))
+            wire.go(remote(part, wire.shard(w_in, at.f), s_in, d, at.group(d)))
+
+    mask_row = hidden((1, slots), 1)
 
     def attend(c1, c2):
         def pair(p, stats):
             sl = lanes_of(p)
             q = jnp.concatenate([q_all[c1, :, sl], q_all[c2, :, sl]], 0)
-            k, v = k2[:, sl], v2[:, sl]
-            total = jnp.zeros((2 * rows, LANES), F32)
-            for half in range(2):
-                s = nt(q, half_mask(k, half)) + mask_row[...]
-                m = jnp.max(s, axis=1, keepdims=True)
-                e = jnp.exp(s - m)
-                l = jnp.sum(e, axis=1, keepdims=True)
-                total += nn(e.astype(BF16), half_mask(v, half)) / l
-                stats = jnp.where(stat_lane == 2 * p + half, m + jnp.log(l), stats)
-            part[c1, :, sl] = total[:rows].astype(BF16)
-            part[c2, :, sl] = total[rows:].astype(BF16)
+            s = nt(q, two_heads(k2[:, sl]))
+            value, stats = softmax_pair([s[:, :slots] + mask_row, s[:, slots:] + mask_row], v2[:, sl], stats, p)
+            part[c1, :, sl] = value[:rows].astype(BF16)
+            part[c2, :, sl] = value[rows:].astype(BF16)
             return stats
 
-        stats = lax.fori_loop(0, PAIRS, pair, jnp.zeros((2 * rows, LANES), F32))
+        stats = lax.fori_loop(0, PAIRS, pair, jnp.zeros((2 * rows, LANES), F32), unroll=True)
         part_lse[c1] = stats[:rows].T[:STAT]
         part_lse[c2] = stats[rows:].T[:STAT]
 
@@ -958,7 +1131,7 @@
         wire.go(remote(joined.at[a], from_z.at[at.a], s_z, at.a, at.column(a)))
         wire.go(remote(joined_lse.at[a], from_z_lse.at[at.a], s_zl, at.a, at.column(a)))
 
-    round_trip(wire, [(q_all, s_q)], project_memory, attend, ship_part, fold_part)
+    round_trip(wire, [(q_all, s_q, CHUNKS)], [fill_mask, lambda: None, next_weights, project_memory], attend, ship_part, fold_part)
     wire.weight_relay(w_co, s_w, 0)
     value, stat = blend_column(at.a)
     parts, stats = [value], [stat]
@@ -1028,41 +1201,43 @@
     do_all[at.c] = do2
     stat_own[0] = jnp.concatenate([lse2, per_head_sums(do2.astype(F32) * out2, heads)], 0)
     stat_all[at.c] = stat_own[0]
-    wire.spread(do_all.at[at.c], do_all, s_do)
-    wire.spread(stat_own.at[0], stat_all, s_st)
-
-    def feed_forward_grads():
+    wire.spread(do_all.at[at.c], do_all, s_do, CHUNKS)
+    wire.spread(stat_own.at[0], stat_all, s_st, 1)
+
+    def finish_output():
         layer_out[...] = (h2 + collect(out_send, out_in, s_out)).astype(BF16)
-        g_out[...] = tn(act[...], g_all[...]).astype(BF16)
-        g_in[...] = tn(a3_all[...], dpre[...]).astype(BF16)
         dk_acc[...] = jnp.zeros_like(dk_acc)
         dv_acc[...] = jnp.zeros_like(dv_acc)
+
+    def out_grads():
+        g_out[...] = tn(act[...], g_all[...]).astype(BF16)
+
+    def in_grads():
+        g_in[...] = tn(a3_all[...], dpre[...]).astype(BF16)
 
     def attend_back(c1, c2):
         def pair(p, carry):
             sl = lanes_of(p)
             q = jnp.concatenate([q_all[c1, :, sl], q_all[c2, :, sl]], 0)
             do = jnp.concatenate([do_all[c1, :, sl], do_all[c2, :, sl]], 0)
-            k, v = k2[:, sl], v2[:, sl]
-            dkp, dvp = dk_acc[:, sl], dv_acc[:, sl]
-            dq = jnp.zeros((2 * rows, LANES), F32)
+            kk = two_heads(k2[:, sl])
+            s = nt(kk, q)
+            d = nt(two_heads(v2[:, sl]), do)
+            line = lambda i: jnp.concatenate([stat_all[c1, pl.ds(i, 1), :], stat_all[c2, pl.ds(i, 1), :]], 1)
+            weights, slopes = [], []
             for half in range(2):
-                line = lambda i: jnp.concatenate([stat_all[c1, pl.ds(i, 1), :], stat_all[c2, pl.ds(i, 1), :]], 1)
-                h = 2 * p + half
-                km = half_mask(k, half)
-                s = nt(km, q) + mask_col[...]
-                e = jnp.exp(s - line(h))
-                dvp = dvp + nn(e.astype(BF16), half_mask(do, half))
-                ds = (e * (nt(half_mask(v, half), do) - line(STAT + h))).astype(BF16)
-                dkp = dkp + nn(ds, half_mask(q, half))
-                dq = dq + tn(ds, km)
-            dk_acc[:, sl] = dkp
-            dv_acc[:, sl] = dvp
+                h, hs = 2 * p + half, slice(half * slots, (half + 1) * slots)
+                e = jnp.exp(s[hs] + mask[...] - line(h))
+                weights.append(e.astype(BF16))
+                slopes.append((e * (d[hs] - line(STAT + h))).astype(BF16))
+            dv_acc[:, sl] += nn(jnp.concatenate(weights, 1), two_heads(do))
+            dk_acc[:, sl] += nn(jnp.concatenate(slopes, 1), two_heads(q))
+            dq = tn(kk, jnp.concatenate(slopes, 0)).T
             dqp[c1, :, sl] = dq[:rows].astype(BF16)
             dqp[c2, :, sl] = dq[rows:].astype(BF16)
             return carry
 
-        lax.fori_loop(0, PAIRS, pair, 0)
+        lax.fori_loop(0, PAIRS, pair, 0, unroll=True)
 
     def ship_dq(a):
         wire.go(remote(dqp.at[a * 2 + 1 - at.b], dq_b.at[a], s_dy, a, at.beside))
@@ -1075,7 +1250,7 @@
         dq_j[a] = column_dq(a).astype(BF16)
         wire.go(remote(dq_j.at[a], dq_z.at[at.a], s_dz, at.a, at.column(a)))
 
-    round_trip(wire, [(do_all, s_do), (stat_all, s_st)], feed_forward_grads, attend_back, ship_dq, fold_dq)
+    round_trip(wire, [(do_all, s_do, CHUNKS), (stat_all, s_st, 1)], [finish_output, out_grads, in_grads], attend_back, ship_dq, fold_dq)
     dk2_out[...] = dk_acc[...].astype(BF16)
     dv2_out[...] = dv_acc[...].astype(BF16)
     value = column_dq(at.a)
@@ -1095,11 +1270,11 @@
     do1_out[...] = do1
     stat_own[1] = jnp.concatenate([lse1[...].T[:STAT], per_head_sums(do1.astype(F32) * o1[...].astype(F32), heads)], 0)
     stat1_out[...] = stat_own[1]
-    gmem_out[...] = (nt(dk2_out[...], w_rest[2]) + nt(dv2_out[...], w_rest[3])).astype(BF16)
+    gmem_out[...] = (nt(dk2_out[...], w_ck[...]) + nt(dv2_out[...], w_cv[...])).astype(BF16)
     wire.drain()
 
 
-def middle(peers, q2, h1, o1, lse1, w_rest, gains, mem, mask_row, mask_col, grad, co_shard, in_shard, w_out):
+def middle(peers, lengths, q2, h1, o1, lse1, w_rest, gains, mem, grad, ck_shard, cv_shard, co_shard, in_shard, w_out):
     rows, slots = q2.shape[0], mem.shape[0]
     depth = peers // 2
     units = w_out.shape[0]
@@ -1126,37 +1301,38 @@
             sds((slots, D), BF16),
             sds((8, D), F32),
         ],
-        in_specs=[full_spec()] * 13,
+        in_specs=[smem_spec()] + [full_spec()] * 13,
         out_specs=[full_spec()] * 14,
         scratch_shapes=[
             store(peers), pltpu.VMEM((slots, D), BF16), pltpu.VMEM((slots, D), BF16),
             store(peers), stat(peers), store(depth), stat(depth), store(depth), stat(depth), store(depth), stat(depth),
-            pltpu.VMEM((D, D), BF16), pltpu.VMEM((D, units), BF16),
+            pltpu.VMEM((D, D), BF16), pltpu.VMEM((D, D), BF16), pltpu.VMEM((D, D), BF16), pltpu.VMEM((D, units), BF16),
             group(D), group(D), group(units, F32), group(units), group(units), group(D), group(D), group(D), group(D),
             store(peers), stat(peers, 2 * STAT), stat(2, 2 * STAT),
             pltpu.VMEM((slots, D), F32), pltpu.VMEM((slots, D), F32),
             store(peers), store(depth), store(depth), store(depth),
+            pltpu.VMEM((slots, 2 * rows), F32),
         ]
-        + sems(2 * depth) + sems(3) + sems(WAYS) + sems(WAYS)
+        + line_sems(depth, CHUNKS) + sems(9) + sems(WAYS) + sems(WAYS)
         + sems(depth) * 4
         + sems(WAYS) * 3
-        + sems(2 * depth) * 2
+        + line_sems(depth, CHUNKS) + line_sems(depth, 1)
         + sems(depth) * 2,
         compiler_params=pltpu.CompilerParams(collective_id=2, has_side_effects=True, vmem_limit_bytes=VMEM_LIMIT),
-    )(q2, h1, o1, lse1, w_rest, gains, mem, mask_row, mask_col, grad, co_shard, in_shard, w_out)
+    )(lengths, q2, h1, o1, lse1, w_rest, gains, mem, grad, ck_shard, cv_shard, co_shard, in_shard, w_out)
 
 
 def tail_kernel(peers, *refs):
-    (inv, own, do1, stat1, q_nat, k_nat, v_nat, bias, bias_back, tok, w_self, gains, dh1, bucket_rows,
-     a1, o1, branch1, a2, dq2, mem, dk2, dv2, o2, branch2, g_in, g_out, small_mid) = refs[:27]
-    out, small_out, grad_tokens = refs[27:30]
+    (order, do1, stat1, q_far, k_far, v_far, bias_far, bias_back_far, tok, w_self, gains, dh1, buckets,
+     a1, o1, branch1, a2, dq2, mem, dk2, dv2, o2, branch2, g_in, g_out, small_mid) = refs[:26]
+    out, small_out, grad_tokens = refs[26:29]
     (prod, ra, sb, rb, sc, rc, sd, rd, tiny, tiny_in, do_all, do_nat, stat_all, stat_rows, stat_t, q_own, k_own, v_own,
-     dq1, dk1, dv1, diagonals, s_w, *sem) = refs[30:]
+     dq1, dk1, dv1, diagonals, q_nat, k_nat, v_nat, bias, bias_back, bucket_rows, inv, s_w, s_far, *sem) = refs[29:]
     sem = [sem[2 * i : 2 * i + 2] for i in range(len(sem) // 2)]
     s_do, s_st, sem_a, sem_b, sem_c, sem_d, sem_e, sem_f, sem_g, sem_t = sem
     wire = Wire(peers)
     at, depth, go = wire.at, wire.depth, wire.go
-    rows, length = do1.shape[0], q_nat.shape[0]
+    rows, length = do1.shape[0], q_far.shape[0]
     mine, pieces = rows // PIECE, length // PIECE
     total, quarter, wide = out.shape
     half_width, part = wide // 2, quarter // depth
@@ -1252,16 +1428,16 @@
             value += tiny_in[2 + d]
         small_out[...] = value
 
-    gathered = [(do_all, s_do), (stat_all, s_st)]
+    gathered = [(do_all, s_do, CHUNKS), (stat_all, s_st, 1)]
 
     def relay(step):
-        for buf, s in gathered:
-            wire.relay(buf, s, step)
+        wire.relay(gathered, step)
 
     def prepare():
+        for copy in coming:
+            copy.wait()
         for a in range(depth):
-            for buf, s in gathered:
-                wire.from_beside(buf, s, a)
+            wire.from_beside(gathered, a)
         for c in range(peers):
             spread = jnp.concatenate([stat_all[c], jnp.zeros((LANES - 2 * STAT, rows), F32)], 0)
             stat_rows[c * rows : (c + 1) * rows, :] = spread.T
@@ -1273,17 +1449,14 @@
             stat_t[:, t * LANES : (t + 1) * LANES] = jnp.concatenate(lines, 0).T
         for i in range(mine):
             dst = slice(i * PIECE, (i + 1) * PIECE)
-            src = pl.ds(own[i, 0] * PIECE, PIECE)
+            src = pl.ds(own[i][0] * PIECE, PIECE)
             q_own[dst, :] = q_nat[src, :]
             k_own[dst, :] = k_nat[src, :]
             v_own[dst, :] = v_nat[src, :]
 
-    def own_column(i):
-        return jnp.concatenate([jnp.full((PIECE, 1), own[j, i], jnp.int32) for j in range(mine)], 0)
-
     def attend_back(low, high):
         lane = lax.broadcasted_iota(jnp.int32, (rows, length), 1)
-        visible, seen = lane < own_column(3), lane >= own_column(4)
+        visible, seen = lane < own_column(own, 3), lane >= own_column(own, 4)
         stat_lane = lax.broadcasted_iota(jnp.int32, (rows, LANES), 1)
         stat_own = jnp.concatenate([stat1[...], jnp.zeros((LANES - 2 * STAT, rows), F32)], 0).T
 
@@ -1324,7 +1497,7 @@
         sums = jnp.zeros((STAT, BUCKETS), F32)
         number = lax.broadcasted_iota(jnp.int32, (BUCKETS, length + LANES), 0)
         for i in range(mine):
-            line = bucket_rows[pl.ds(own[i, 1], 1), pl.ds(own[i, 2] * LANES, length + LANES)]
+            line = bucket_rows[pl.ds(own[i][1], 1), pl.ds(own[i][2] * LANES, length + LANES)]
             hot = jnp.where(line == number, 1.0, 0.0).astype(BF16)
             high, low = split(diagonals[i])
             sums += nt(high, hot) + nt(low, hot)
@@ -1335,16 +1508,26 @@
 
     weights_here = pltpu.make_async_copy(w_self, prod.at[5:8], s_w)
     weights_here.start()
+    coming = []
+    for i, (src, dst) in enumerate(
+        ((q_far, q_nat), (k_far, k_nat), (v_far, v_nat), (bias_far, bias), (bias_back_far, bias_back))
+    ):
+        coming.append(pltpu.make_async_copy(src, dst, s_far.at[i]))
+        coming[-1].start()
+    own = own_facts(order, at.c, mine, length)
     greet(wire.partners())
-    wire.spread(do1, do_all, s_do)
-    wire.spread(stat1, stat_all, s_st)
+    wire.spread(do1, do_all, s_do, CHUNKS)
+    wire.spread(stat1, stat_all, s_st, 1)
     wire.slot(do_all, at.c)[...] = do1[...]
     stat_all[at.c] = stat1[...]
+    fill_inverse(order, inv)
     diagonals[...] = jnp.zeros_like(diagonals)
-    order = [12, 13, 14, 15, 0, 1, 2, 3, 4, 8, 9, 10, 11, 5, 6, 7]
+    bucket_rows[0:1, :] = pltpu.roll(buckets[...], 1, 1)
+    bucket_rows[1:2, :] = pltpu.roll(buckets[...], 1 + PIECE, 1)
+    turns = [12, 13, 14, 15, 0, 1, 2, 3, 4, 8, 9, 10, 11, 5, 6, 7]
     lag = 1.5
     events = []
-    for tick, j in enumerate(order):
+    for tick, j in enumerate(turns):
         if j < n_mats:
             events += [(tick - 2, 1, lambda j=j: stage_a(j)), (tick - 1, 2, lambda j=j: stage_b(j))]
         for k, stage in enumerate((stage_c, stage_d, stage_e, stage_f, stage_g)):
@@ -1359,7 +1542,7 @@
     wire.drain()
 
 
-def tail(peers, inv, own, do1, stat1, q_nat, k_nat, v_nat, bias, bias_back, tok, w_self, gains, dh1, bucket_rows, *rest):
+def tail(peers, order, do1, stat1, q_nat, k_nat, v_nat, bias, bias_back, tok, w_self, gains, dh1, buckets, *rest):
     rows, length = do1.shape[0], q_nat.shape[0]
     n, depth = 8, peers // 2
     total = n + 2 * WAYS
@@ -1367,13 +1550,13 @@
     shard = lambda k, width=D: pltpu.VMEM((k, quarter, width), BF16)
     row = lambda: pltpu.VMEM((rows, D), BF16)
     tiny = lambda k: pltpu.VMEM((k, 8 + STAT, D), F32)
-    operands = (do1, stat1, q_nat, k_nat, v_nat, bias, bias_back, tok, w_self, gains, dh1, bucket_rows) + rest
+    operands = (do1, stat1, q_nat, k_nat, v_nat, bias, bias_back, tok, w_self, gains, dh1, buckets) + rest
     return pl.pallas_call(
         functools.partial(tail_kernel, peers),
         name="tail",
         out_shape=[sds((total, quarter, D), BF16), sds((8 + STAT, D), F32), sds((rows, D), BF16)],
-        in_specs=[smem_spec()] * 2
-        + [pl.BlockSpec(memory_space=pl.ANY) if x is w_self else full_spec() for x in operands],
+        in_specs=[smem_spec()]
+        + [any_spec() if i in (2, 3, 4, 5, 6, 8) else full_spec() for i in range(len(operands))],
         out_specs=[full_spec()] * 3,
         scratch_shapes=[
             pltpu.VMEM((n, D, D), BF16), pltpu.VMEM((n, 2, quarter, D), BF16), shard(n), shard(n),
@@ -1383,12 +1566,51 @@
             pltpu.VMEM((peers, 2 * STAT, rows), F32), pltpu.VMEM((length, LANES), F32), pltpu.VMEM((LANES, length), F32),
             row(), row(), row(), row(), row(), row(),
             pltpu.VMEM((rows // PIECE, STAT, length + LANES), F32),
-            pltpu.SemaphoreType.DMA,
         ]
-        + sems(2 * depth) + sems(2 * depth)
+        + [pltpu.VMEM((length, D), BF16)] * 3
+        + [pltpu.VMEM((HEADS, rows, length), BF16)] * 2
+        + [pltpu.VMEM((2, 2 * length), jnp.int32), pltpu.SMEM(order.shape, jnp.int32)]
+        + [pltpu.SemaphoreType.DMA, pltpu.SemaphoreType.DMA((5,))]
+        + line_sems(depth, CHUNKS) + line_sems(depth, 1)
         + sems(2 * n) + sems(n) + sems(total) + sems(total * depth) + sems(total * depth) + sems(total) + sems(WAYS) + sems(3 + depth),
         compiler_params=pltpu.CompilerParams(collective_id=0, has_side_effects=True, vmem_limit_bytes=TAIL_VMEM),
-    )(inv, own, *operands)
+    )(order, *operands)
+
+
+def widen_kernel(src, *refs):
+    outs, sem = refs[:-2], refs[-1]
+    wide = refs[-2]
+    copies = []
+    count = src.shape[0]
+    quarter, width = src.shape[1], src.shape[2]
+    for j in range(count):
+        wide[j] = src[j].astype(F32)
+        if j < count - 2 * WAYS:
+            dst = outs[j]
+        elif j < count - WAYS:
+            i = j - (count - 2 * WAYS)
+            dst = outs[-2].at[:, i * width : (i + 1) * width]
+        else:
+            i = j - (count - WAYS)
+            dst = outs[-1].at[i * quarter : (i + 1) * quarter]
+        copies.append(pltpu.make_async_copy(wide.at[j], dst, sem.at[j]))
+        copies[-1].start()
+    for copy in copies:
+        copy.wait()
+
+
+def widen(total):
+    count, quarter, width = total.shape
+    each = [sds((quarter, width), F32)] * (count - 2 * WAYS)
+    return pl.pallas_call(
+        widen_kernel,
+        name="widen",
+        out_shape=each + [sds((quarter, WAYS * width), F32), sds((WAYS * quarter, width), F32)],
+        in_specs=[full_spec()],
+        out_specs=[any_spec()] * (len(each) + 2),
+        scratch_shapes=[pltpu.VMEM(total.shape, F32), pltpu.SemaphoreType.DMA((count,))],
+        compiler_params=pltpu.CompilerParams(vmem_limit_bytes=VMEM_LIMIT),
+    )(total)
 
 
 def shards(
@@ -1417,34 +1639,18 @@
     rows, slots = tok.shape[0], mem.shape[0]
     length = (bucket_table.shape[0] + 1) // 2
     peers = length // rows
-    index = lax.axis_index("ctx")
-    own = lax.dynamic_slice_in_dim(piece_order, index * (rows // PIECE), rows // PIECE)
     f = lax.axis_index("fsdp")
     quarter, eighth = self_query.shape[0], position_bias.shape[0]
-    slots_all = jnp.arange(piece_order.shape[0], dtype=jnp.int32)
-    inv = jnp.sum(jnp.where(piece_order[None, :] == slots_all[:, None], slots_all[None, :], 0), axis=1)
-    block_start = own * PIECE // BLOCK * BLOCK
-    own_facts = jnp.stack(
-        [own, own % 2, (length - (own - own % 2) * PIECE) // LANES - 1, block_start + BLOCK, block_start], axis=1
-    )
-    pack = jnp.zeros((N_GAINS + BUCKETS, D), BF16)
-    pack = lax.dynamic_update_slice(pack, jnp.stack([self_gain, cross_gain, hidden_gain]), (0, f * quarter))
-    pack = lax.dynamic_update_slice(pack, position_bias, (N_GAINS + f * eighth, 0))
     buckets = jnp.pad(bucket_table, (0, 1), constant_values=-1)[None]
-    buckets_back = jnp.pad(bucket_table[::-1], (0, 1), constant_values=-1)[None]
-    bucket_rows = jnp.concatenate([jnp.roll(buckets, 1, 1), jnp.roll(buckets, 1 + PIECE, 1)], 0)
     w_self, w_rest, gains, ahead, behind, q1_nat, k1_nat, v1_nat, a1, o1, h1, a2, q2, lse1 = front(
         peers,
-        inv,
-        own_facts,
+        piece_order,
         tok,
-        pack,
+        [self_gain[None], cross_gain[None], hidden_gain[None]],
+        position_bias,
         buckets,
-        buckets_back,
-        [self_query, self_attention_key, self_value, self_output, cross_query, cross_key, cross_value],
-    )
-    taken = jnp.arange(PLEN, dtype=jnp.int32)[None, :] < passage_lengths[0][:, None]
-    hidden = jnp.where(lax.dynamic_slice_in_dim(taken.reshape(-1), index * slots, slots), 0.0, NEGATIVE)
+        [self_query, self_attention_key, self_value, self_output, cross_query],
+    )
     (
         o2,
         branch2,
@@ -1462,6 +1668,7 @@
         small_mid,
     ) = middle(
         peers,
+        passage_lengths,
         q2,
         h1,
         o1,
@@ -1469,17 +1676,16 @@
         w_rest,
         gains,
         mem,
-        hidden[None, :],
-        hidden[:, None],
         grad,
+        cross_key,
+        cross_value,
         cross_output,
         hidden_in,
         hidden_out,
     )
     total, small, grad_tokens = tail(
         peers,
-        inv,
-        own_facts,
+        piece_order,
         do1,
         stat1,
         q1_nat,
@@ -1491,7 +1697,7 @@
         w_self,
         gains,
         dh1,
-        bucket_rows,
+        buckets,
         a1,
         o1,
         branch1,
@@ -1506,11 +1712,9 @@
         g_out,
         small_mid,
     )
-    total = total.astype(F32)
+    *each, sum_in, sum_out = widen(total)
     gain = lambda i: lax.dynamic_slice_in_dim(small[i], f * quarter, quarter)
     bias_out = lax.dynamic_slice_in_dim(small[8:, :BUCKETS].T, f * eighth, eighth)[:, :HEADS]
-    places = [5, 6, 7, 4, 3, 1, 2, 0]
-    count = len(places)
     return (
         layer_output[None],
         grad_tokens[None],
@@ -1519,9 +1723,9 @@
         gain(1),
         gain(2),
         bias_out,
-        *[total[i] for i in places],
-        jnp.concatenate([total[count + i] for i in range(WAYS)], 1),
-        total[count + WAYS :].reshape(-1, D),
+        *[each[i] for i in (5, 6, 7, 4, 3, 1, 2, 0)],
+        sum_in,
+        sum_out,
     )
 
 

time: 412 us -> 373 us (0.905)
  Pallas kernels: 375 us -> 357 us
  local copies, waits for them, and re-layouts: 19.7 us -> 10.8 us
  other arithmetic: 8.83 us -> 0 us
    pallas_call x1, Pallas kernels: 147 us -> 133 us  [middle(): pl.pallas_call(functools.partial(middle_kernel, peers), name='middle', ou...]
    pallas_call x0 -> x1, Pallas kernels: none -> 6.23 us  [widen(): pl.pallas_call(widen_kernel, name='widen', out_shape=each + [sds((quarter...]
    pallas_call x1, Pallas kernels: 65.7 us -> 59.9 us  [front(): pl.pallas_call(functools.partial(front_kernel, peers), name='front', out_...]
    pallas_call x1, Pallas kernels: 162 us -> 158 us  [tail(): pl.pallas_call(functools.partial(tail_kernel, peers), name='tail', out_sh...]
where the time goes in v6:
time: 373 us; the launch traced here: 369 us
  Pallas kernels  357 us (96%)
  local copies, waits for them, and re-layouts  10.8 us (3%)
    pallas_call x1, Pallas kernels, tail(): pl.pallas_call(functools.partial(tail_kernel, peers), name='tail', out_sh...  158 us
    pallas_call x1, Pallas kernels, middle(): pl.pallas_call(functools.partial(middle_kernel, peers), name='middle', ou...  133 us
    pallas_call x1, Pallas kernels, front(): pl.pallas_call(functools.partial(front_kernel, peers), name='front', out_...  59.9 us

profile of v6, /device:TPU:0, one launch (start us, length us, event | category | flops | bytes accessed | tf_op | source)
XLA Modules:
  0.0 368.6 jit_solution(652500812852783554)
XLA Ops:
  0.7 1.3 pad.4
  2.0 1.2 broadcast_in_dim.21.refs_2_
  3.2 1.2 broadcast_in_dim.22.refs_3_
  4.4 1.2 broadcast_in_dim.23.refs_4_
  5.6 59.9 %front.1 = (bf16[3,768,768]{2,1,0:T(8,128)(2,1)}, bf16[2,768,768]{2,1,0:T(8,128)(2,1)}, f32[8,768]{1,0:T(8,128)}, bf16[12,128,1024]{2,1,0:T(8,128)(2,1)}, bf16[1...) custom-call(s32[16]{0:T(128)} %refs_0_.5, ...), custom_call_target="tpu_custom_call" | custom-call | tf_op jit(solution)/shard_map/front/pallas_call | solution.py:953
  65.5 132.9 %middle.1 = (bf16[128,768]{1,0:T(8,128)(2,1)}, bf16[128,768]{1,0:T(8,128)(2,1)}, bf16[128,768]{1,0:T(8,128)(2,1)}, bf16[640,768]{1,0:T(8,128)(2,1)}, bf16[640,76...) custom-call(s32[1,20]{1,0:T(1,128)} %refs_0_.4, ...), custom_call_target="tpu_custom_call" | custom-call | tf_op jit(solution)/shard_map/middle/pallas_call | solution.py:1285
  198.4 157.5 %tail.1 = (bf16[16,192,768]{2,1,0:T(8,128)(2,1)}, f32[24,768]{1,0:T(8,128)}, bf16[128,768]{1,0:T(8,128)(2,1)}) custom-call(s32[16]{0:T(128)} %refs_0_.5, bf16[128,768]{1,0:T(8,128)(2,1)} %get-tuple-element.65.refs_1_, f32[32,128]{1,0:T(8,128)} %get-tuple-element.66.refs_2_, bf16[1024,768]{1,0:T(8,128)(2,1)} %get-tuple-element.67.refs_3_, ...), custom_call_target="tpu_custom_call" | custom-call | tf_op jit(solution)/shard_map/tail/pallas_call | solution.py:1554
  355.9 0.0 copy-start.1
  355.9 0.0 copy-start.2
  356.0 0.0 copy-start
  356.0 6.2 %widen.1 = (f32[192,768]{1,0:T(8,128)}, f32[192,768]{1,0:T(8,128)}, f32[192,768]{1,0:T(8,128)}, f32[192,768]{1,0:T(8,128)}, f32[192,768]{1,0:T(8,128)}, /*index=...) custom-call(bf16[16,192,768]{2,1,0:T(8,128)(2,1)} %get-tuple-element.88.src), custom_call_target="tpu_custom_call" | custom-call | tf_op jit(solution)/shard_map/widen/pallas_call | solution.py:1605
  362.2 0.9 fusion
  363.1 0.6 constant_dynamic-slice_fusion
  363.7 0.7 slice.18
  364.4 0.1 dynamic-slice_bitcast_fusion
  364.5 0.7 copy.37
  365.1 0.6 constant_dynamic-slice_fusion.2
  365.8 0.0 copy-done.1
  365.8 0.7 copy.41
  366.5 0.0 copy-done.2
  366.5 0.7 copy.42
  367.1 0.0 copy-done
  367.1 0.9 copy.43
Async XLA Ops:
  355.9 9.9 %copy-start.1 = (bf16[128,768]{1,0:T(8,128)(2,1)S(1)}, bf16[128,768]{1,0:T(8,128)(2,1)}, u32[]{:S(2)}) copy-start(bf16[128,768]{1,0:T(8,128)(2,1)} %get-tuple-element.64) | copy-start | bytes 589828
  355.9 10.5 %copy-start.2 = (bf16[128,768]{1,0:T(8,128)(2,1)S(1)}, bf16[128,768]{1,0:T(8,128)(2,1)}, u32[]{:S(2)}) copy-start(bf16[128,768]{1,0:T(8,128)(2,1)} %get-tuple-element.85) | copy-start | bytes 589828
  356.0 11.2 %copy-start = (bf16[640,768]{1,0:T(8,128)(2,1)S(1)}, bf16[640,768]{1,0:T(8,128)(2,1)}, u32[]{:S(2)}) copy-start(bf16[640,768]{1,0:T(8,128)(2,1)} %get-tuple-element.86) | copy-start | bytes 2949124

commit v7 on v6

--- a/solution.py
+++ b/solution.py
@@ -743,6 +743,55 @@
         remote(slot, slot, sem, 3 * i + 2, at.core).wait_recv()
 
 
+class Summed:
+    def __init__(self, wire, source, out, rc, sd, rd, sem_c, sem_d, sem_e, sem_f):
+        self.wire, self.source, self.out, self.rc, self.sd, self.rd = wire, source, out, rc, sd, rd
+        self.sem_c, self.sem_d, self.sem_e, self.sem_f = sem_c, sem_d, sem_e, sem_f
+        at = wire.at
+        half, part = out.shape[2] // 2, out.shape[1] // wire.depth
+        columns = lambda b: pl.ds(pl.multiple_of(b * half, LANES), half)
+        self.mine, self.theirs = columns(at.b), columns(1 - at.b)
+        self.rows = lambda a: pl.ds(pl.multiple_of(a * part, part), part)
+
+    def stage_c(self, j):
+        at = self.wire.at
+        self.wire.go(remote(self.source(j).at[:, self.theirs], self.rc.at[j], self.sem_c, j, at.beside))
+
+    def stage_d(self, j):
+        at, depth = self.wire.at, self.wire.depth
+        remote(self.rc.at[j], self.rc.at[j], self.sem_c, j, at.beside).wait_recv()
+        value = self.source(j)[:, self.mine].astype(F32) + self.rc[j].astype(F32)
+        self.sd[j] = value.astype(BF16)
+        for d in range(1, depth):
+            spot = self.rd.at[j, self.rows(at.a)]
+            target = at.ahead(d)
+            self.wire.go(remote(self.sd.at[j, self.rows(target)], spot, self.sem_d, j * depth + d, at.column(target)))
+
+    def stage_e(self, j):
+        at, depth = self.wire.at, self.wire.depth
+        value = self.sd[j, self.rows(at.a), :].astype(F32)
+        for d in range(1, depth):
+            spot = self.rd.at[j, self.rows(at.behind(d))]
+            remote(spot, spot, self.sem_d, j * depth + d, at.column(at.behind(d))).wait_recv()
+            value += spot[...].astype(F32)
+        spot = self.out.at[j, self.rows(at.a), self.mine]
+        spot[...] = value.astype(BF16)
+        for d in range(1, depth):
+            self.wire.go(remote(spot, spot, self.sem_e, j * depth + d, at.column(at.ahead(d))))
+
+    def stage_f(self, j):
+        at, depth = self.wire.at, self.wire.depth
+        for d in range(1, depth):
+            spot = self.out.at[j, self.rows(at.behind(d)), self.mine]
+            remote(spot, spot, self.sem_e, j * depth + d, at.column(at.behind(d))).wait_recv()
+        spot = self.out.at[j, :, self.mine]
+        self.wire.go(remote(spot, spot, self.sem_f, j, at.beside))
+
+    def stage_g(self, j):
+        spot = self.out.at[j, :, self.theirs]
+        remote(spot, spot, self.sem_f, j, self.wire.at.beside).wait_recv()
+
+
 def two_heads(x):
     return jnp.concatenate([half_mask(x, 0), half_mask(x, 1)], 0)
 
@@ -792,7 +841,7 @@
     return jnp.concatenate([jnp.full((PIECE, 1), fact[i], jnp.int32) for fact in facts], 0)
 
 
-def own_bias(table, lines, own, out):
+def own_bias(table, lines, own, out, low, high):
     full = table.shape[1]
     rows, length = out.shape[1], out.shape[2]
 
@@ -808,7 +857,7 @@
                 out[h, i * PIECE + 8 * g : i * PIECE + 8 * g + 16, :] = both.astype(BF16)
         return c
 
-    lax.fori_loop(0, HEADS, head, 0)
+    lax.fori_loop(low, high, head, 0)
 
 
 def diagonal_sums(block):
@@ -828,10 +877,10 @@
 def front_kernel(peers, *refs):
     order, tok, gain1, gain2, gain3, bias_shard, buckets = refs[:7]
     shards_in = refs[7 : 7 + N_FRONT]
-    (w_self_out, w_rest_out, gains, ahead_out, behind_out, q_out, k_out, v_out, a1, o1, h1, a2, q2, lse) = refs[7 + N_FRONT : 21 + N_FRONT]
-    (tok_all, pack, pack_all, table, lines, q_own, w_self, w_rest, ahead, behind, q_nat, k_nat, v_nat, s_keep, inv, *sem) = refs[21 + N_FRONT :]
+    (w_self_out, w_rest_out, gains, ahead_out, table_out, q_out, k_out, v_out, a1, o1, h1, a2, q2, lse) = refs[7 + N_FRONT : 21 + N_FRONT]
+    (tok_all, pack, pack_all, marks, marks_all, table, lines, q_own, w_self, w_rest, ahead, q_nat, k_nat, v_nat, s_keep, inv, *sem) = refs[21 + N_FRONT :]
     weights = [w_self.at[i] for i in range(3)] + [w_rest.at[i] for i in range(N_FRONT - 3)]
-    sem_t, sem_w, sem_p = sem[0:2], sem[2:4], sem[4:6]
+    sem_t, sem_w, sem_p, sem_m = sem[0:2], sem[2:4], sem[4:6], sem[6:8]
     wire = Wire(peers)
     at, depth = wire.at, wire.depth
     rows = tok.shape[0]
@@ -849,27 +898,32 @@
     place = jnp.where(lax.broadcasted_iota(jnp.int32, (quarter, D), 1) == spot, 1.0, 0.0).astype(BF16)
     pack[...] = jnp.zeros_like(pack)
     for i, gain in enumerate((gain1, gain2, gain3)):
-        pack[i : i + 1, :] = nn(gain[...], place)
+        pack[i : i + 1, :] = nn(gain[...], place).astype(BF16)
     eighth, heads = bias_shard.shape
     spot = lax.broadcasted_iota(jnp.int32, (BUCKETS, eighth), 1) + at.f * eighth
     place = jnp.where(lax.broadcasted_iota(jnp.int32, (BUCKETS, eighth), 0) == spot, 1.0, 0.0).astype(BF16)
-    pack[N_GAINS:, 0:heads] = nn(place, bias_shard[...])
+    marks[...] = jnp.zeros_like(marks)
+    marks[:, 0:heads] = nn(place, bias_shard[...]).astype(BF16)
     greet(wire.partners())
     for d in range(1, WAYS):
         wire.go(remote(pack, pack_all.at[at.f], sem_p, d, at.group(d)))
+        wire.go(remote(marks, marks_all.at[at.f], sem_m, d, at.group(d)))
     wire.spread(tok, tok_all, sem_t, CHUNKS)
     for i in range(3):
         wire.weight_start(shards_in[i], weights[i], sem_w, i)
     wire.slot(tok_all, at.c)[...] = tok[...]
     pack_all[at.f] = pack[...]
+    marks_all[at.f] = marks[...]
     for d in range(1, WAYS):
         slot = pack_all.at[lax.rem(at.f + WAYS - d, WAYS)]
         remote(slot, slot, sem_p, d, at.group(WAYS - d)).wait_recv()
-    everything = pack_all[0] + pack_all[1] + pack_all[2] + pack_all[3]
+        slot = marks_all.at[lax.rem(at.f + WAYS - d, WAYS)]
+        remote(slot, slot, sem_m, d, at.group(WAYS - d)).wait_recv()
+    whole = lambda x: x[0].astype(F32) + x[1].astype(F32) + x[2].astype(F32) + x[3].astype(F32)
     fill_inverse(order, inv)
     own = own_facts(order, at.c, mine, length)
-    gains[...] = everything[0:8, :]
-    bias = everything[N_GAINS:, 0:LANES].astype(BF16)
+    gains[...] = whole(pack_all)[0:8, :]
+    bias = whole(marks_all).astype(BF16)
     bucket = lax.broadcasted_iota(jnp.int32, (bias.shape[0], 2 * length), 0)
     hot = jnp.where(buckets[...] == bucket, 1.0, 0.0).astype(BF16)
     table[0] = tn(bias, hot)[0:16, :]
@@ -879,12 +933,13 @@
     tiles = 2 * length // LANES
     for t in range(tiles):
         u = tiles - 1 - t
-        table[1, :, t * LANES : (t + 1) * LANES] = nn(shifted[:, u * LANES : (u + 1) * LANES], mirror)
+        table_out[:, t * LANES : (t + 1) * LANES] = nn(shifted[:, u * LANES : (u + 1) * LANES], mirror)
 
     gathered = [(tok_all, sem_t, CHUNKS)]
+    share = HEADS // (depth - 1)
     for step in range(1, depth):
         wire.relay(gathered, step)
-    own_bias(table.at[0], lines, own, ahead)
+        own_bias(table.at[0], lines, own, ahead, (step - 1) * share, step * share)
     keep(3, ahead, ahead_out)
     for i in range(3):
         wire.weight_relay(weights[i], sem_w, i)
@@ -939,8 +994,6 @@
     wire.weight_ready(weights[4], sem_w, 4)
     q2[...] = nn(a, weights[4][...]).astype(BF16)
     keep(1, w_rest, w_rest_out)
-    own_bias(table.at[1], lines, own, behind)
-    keep(4, behind, behind_out)
     for copy in kept:
         copy.wait()
     wire.drain()
@@ -954,25 +1007,27 @@
         functools.partial(front_kernel, peers),
         name="front",
         out_shape=[sds((3, D, D), BF16), sds((N_FRONT - 3, D, D), BF16), sds((8, D), F32)]
-        + [sds((HEADS, rows, length), BF16)] * 2
+        + [sds((HEADS, rows, length), BF16), sds((16, 2 * length), F32)]
         + [sds((length, D), BF16)] * 3
         + [block(BF16), block(BF16), block(F32), block(BF16), block(BF16), sds((rows, LANES), F32)],
         in_specs=[smem_spec()] + [full_spec()] * (6 + N_FRONT),
-        out_specs=[any_spec() if i in (0, 1, 3, 4, 5, 6, 7) else full_spec() for i in range(14)],
+        out_specs=[any_spec() if i in (0, 1, 3, 5, 6, 7) else full_spec() for i in range(14)],
         scratch_shapes=[
             pltpu.VMEM((length, D), BF16),
-            pltpu.VMEM((N_GAINS + BUCKETS, D), F32),
-            pltpu.VMEM((WAYS, N_GAINS + BUCKETS, D), F32),
-            pltpu.VMEM((2, 16, 2 * length), F32),
+            pltpu.VMEM((N_GAINS, D), BF16),
+            pltpu.VMEM((WAYS, N_GAINS, D), BF16),
+            pltpu.VMEM((BUCKETS, LANES), BF16),
+            pltpu.VMEM((WAYS, BUCKETS, LANES), BF16),
+            pltpu.VMEM((1, 16, 2 * length), F32),
             pltpu.VMEM((2, 8, 2 * length), F32),
             pltpu.VMEM((rows, D), BF16),
             pltpu.VMEM((3, D, D), BF16),
             pltpu.VMEM((N_FRONT - 3, D, D), BF16),
         ]
-        + [pltpu.VMEM((HEADS, rows, length), BF16)] * 2
+        + [pltpu.VMEM((HEADS, rows, length), BF16)]
         + [pltpu.VMEM((length, D), BF16)] * 3
         + [pltpu.SemaphoreType.DMA((8,)), pltpu.SMEM(order.shape, jnp.int32)]
-        + line_sems(depth, CHUNKS) + sems(3 * N_FRONT) + sems(WAYS),
+        + line_sems(depth, CHUNKS) + sems(3 * N_FRONT) + sems(WAYS) + sems(WAYS),
         compiler_params=pltpu.CompilerParams(collective_id=1, has_side_effects=True, vmem_limit_bytes=VMEM_LIMIT),
     )(order, tok, *gain_shards, bias_shard, buckets, *weight_shards)
 
@@ -1014,7 +1069,7 @@
     return dx, jnp.sum(dy * x * r, axis=0, keepdims=True)
 
 
-def round_trip(wire, gathered, fillers, compute, ship, fold):
+def round_trip(wire, gathered, fillers, compute, ship, fold, after):
     at = wire.at
     b = at.b
     first, second, third = [wire.near(step) for step in (1, 2, 3)]
@@ -1026,28 +1081,32 @@
     wire.from_beside(gathered, at.a)
     compute(at.c, at.a * 2 + 1 - b)
     ship(at.a)
+    after[0]()
     wire.from_beside(gathered, third)
     compute(third * 2 + 1 - b, third * 2 + b)
     ship(third)
+    after[1]()
     wire.from_beside(gathered, second)
     compute(second * 2 + 1 - b, second * 2 + b)
     ship(second)
+    after[2]()
     fold(third)
     wire.from_beside(gathered, first)
     compute(first * 2 + 1 - b, first * 2 + b)
     ship(first)
+    after[3]()
     fold(second)
     fold(first)
 
 
 def middle_kernel(peers, *refs):
     (lengths, q2, h1, o1, lse1, w_rest, gains, mem, grad, ck_shard, cv_shard, co_shard, in_shard, w_out) = refs[:14]
-    (o2_out, branch2_out, dq2_out, dk2_out, dv2_out, branch1_out, dh1_out, do1_out, stat1_out, g_in, g_out, layer_out, gmem_out, small) = refs[14:28]
+    (o2_out, branch2_out, dq2_out, dk2_out, dv2_out, branch1_out, dh1_out, do1_out, stat1_out, in_all, out_sum, layer_out, gmem_out, small) = refs[14:28]
     (q_all, k2, v2, part, part_lse, from_b, from_b_lse, joined, joined_lse, from_z, from_z_lse,
      w_ck, w_cv, w_co, w_in, g_all, a3_all, dact, act, dpre, da3_send, da3_in, out_send, out_in,
-     do_all, stat_all, stat_own, dk_acc, dv_acc, dqp, dq_b, dq_j, dq_z, mask, *sem) = refs[28:]
+     do_all, stat_all, stat_own, dk_acc, dv_acc, dqp, dq_b, dq_j, dq_z, mask, g_in, g_out, rc, sd, rd, *sem) = refs[28:]
     sem = [sem[2 * i : 2 * i + 2] for i in range(len(sem) // 2)]
-    (s_q, s_w, s_in, s_g, s_y, s_yl, s_z, s_zl, s_a3, s_da3, s_out, s_do, s_st, s_dy, s_dz) = sem
+    (s_q, s_w, s_in, s_g, s_y, s_yl, s_z, s_zl, s_a3, s_da3, s_out, s_do, s_st, s_dy, s_dz, s_gi, *s_sum) = sem
     wire = Wire(peers)
     at, depth = wire.at, wire.depth
     rows = q2.shape[0]
@@ -1131,7 +1190,7 @@
         wire.go(remote(joined.at[a], from_z.at[at.a], s_z, at.a, at.column(a)))
         wire.go(remote(joined_lse.at[a], from_z_lse.at[at.a], s_zl, at.a, at.column(a)))
 
-    round_trip(wire, [(q_all, s_q, CHUNKS)], [fill_mask, lambda: None, next_weights, project_memory], attend, ship_part, fold_part)
+    round_trip(wire, [(q_all, s_q, CHUNKS)], [fill_mask, lambda: None, next_weights, project_memory], attend, ship_part, fold_part, [lambda: None] * 4)
     wire.weight_relay(w_co, s_w, 0)
     value, stat = blend_column(at.a)
     parts, stats = [value], [stat]
@@ -1187,9 +1246,14 @@
         return value
 
     exchange(da3_send, da3_in, s_da3)
+    sums = Summed(wire, lambda j: g_out.at[j * quarter : (j + 1) * quarter], out_sum, rc, sd, rd, *s_sum)
+    g_out[...] = tn(act[...], g_all[...]).astype(BF16)
+    for j in range(WAYS):
+        sums.stage_c(j)
     for rs in tiles:
         out_send[rs, :] = nn(act[rs, :], w_out[...]).astype(BF16)
-    exchange(out_send, out_in, s_out)
+    sums.stage_d(0)
+    sums.stage_d(1)
     da3 = collect(da3_send, da3_in, s_da3)
     dx, dgain = norm_back_rows(h2, gains[2:3, :], da3)
     small[...] = jnp.zeros_like(small)
@@ -1203,17 +1267,25 @@
     stat_all[at.c] = stat_own[0]
     wire.spread(do_all.at[at.c], do_all, s_do, CHUNKS)
     wire.spread(stat_own.at[0], stat_all, s_st, 1)
+    exchange(out_send, out_in, s_out)
+
+    def clear():
+        dk_acc[...] = jnp.zeros_like(dk_acc)
+        dv_acc[...] = jnp.zeros_like(dv_acc)
 
     def finish_output():
         layer_out[...] = (h2 + collect(out_send, out_in, s_out)).astype(BF16)
-        dk_acc[...] = jnp.zeros_like(dk_acc)
-        dv_acc[...] = jnp.zeros_like(dv_acc)
-
-    def out_grads():
-        g_out[...] = tn(act[...], g_all[...]).astype(BF16)
+
+    def stages(stage, *js):
+        return lambda: [stage(j) for j in js]
 
     def in_grads():
         g_in[...] = tn(a3_all[...], dpre[...]).astype(BF16)
+        rows_of = lambda f: pl.ds(pl.multiple_of(f * quarter, quarter), quarter)
+        in_all[at.f] = g_in[rows_of(at.f), :]
+        for d in range(1, WAYS):
+            f = lax.rem(at.f + d, WAYS)
+            wire.go(remote(g_in.at[rows_of(f)], in_all.at[at.f], s_gi, d, at.group(d)))
 
     def attend_back(c1, c2):
         def pair(p, carry):
@@ -1250,7 +1322,10 @@
         dq_j[a] = column_dq(a).astype(BF16)
         wire.go(remote(dq_j.at[a], dq_z.at[at.a], s_dz, at.a, at.column(a)))
 
-    round_trip(wire, [(do_all, s_do, CHUNKS), (stat_all, s_st, 1)], [finish_output, out_grads, in_grads], attend_back, ship_dq, fold_dq)
+    round_trip(
+        wire, [(do_all, s_do, CHUNKS), (stat_all, s_st, 1)], [clear, in_grads, lambda: None, stages(sums.stage_d, 2, 3)], attend_back, ship_dq, fold_dq,
+        [stages(sums.stage_e, 0, 1), stages(sums.stage_e, 2, 3), stages(sums.stage_f, 0, 1), stages(sums.stage_f, 2, 3)],
+    )
     dk2_out[...] = dk_acc[...].astype(BF16)
     dv2_out[...] = dv_acc[...].astype(BF16)
     value = column_dq(at.a)
@@ -1271,6 +1346,12 @@
     stat_own[1] = jnp.concatenate([lse1[...].T[:STAT], per_head_sums(do1.astype(F32) * o1[...].astype(F32), heads)], 0)
     stat1_out[...] = stat_own[1]
     gmem_out[...] = (nt(dk2_out[...], w_ck[...]) + nt(dv2_out[...], w_cv[...])).astype(BF16)
+    finish_output()
+    for d in range(1, WAYS):
+        spot = in_all.at[lax.rem(at.f + WAYS - d, WAYS)]
+        remote(spot, spot, s_gi, d, at.group(WAYS - d)).wait_recv()
+    for j in range(WAYS):
+        sums.stage_g(j)
     wire.drain()
 
 
@@ -1295,8 +1376,8 @@
             row(F32),
             row(BF16),
             sds((2 * STAT, rows), F32),
-            sds((D, units), BF16),
-            sds((units, D), BF16),
+            sds((WAYS, D // WAYS, units), BF16),
+            sds((WAYS, units // WAYS, D), BF16),
             row(BF16),
             sds((slots, D), BF16),
             sds((8, D), F32),
@@ -1312,36 +1393,36 @@
             pltpu.VMEM((slots, D), F32), pltpu.VMEM((slots, D), F32),
             store(peers), store(depth), store(depth), store(depth),
             pltpu.VMEM((slots, 2 * rows), F32),
+            pltpu.VMEM((D, units), BF16),
+            pltpu.VMEM((units, D), BF16),
         ]
+        + [pltpu.VMEM((WAYS, units // WAYS, D // 2), BF16)] * 3
         + line_sems(depth, CHUNKS) + sems(9) + sems(WAYS) + sems(WAYS)
         + sems(depth) * 4
         + sems(WAYS) * 3
         + line_sems(depth, CHUNKS) + line_sems(depth, 1)
-        + sems(depth) * 2,
+        + sems(depth) * 2
+        + sems(WAYS) + sems(WAYS) + sems(WAYS * depth) + sems(WAYS * depth) + sems(WAYS),
         compiler_params=pltpu.CompilerParams(collective_id=2, has_side_effects=True, vmem_limit_bytes=VMEM_LIMIT),
     )(lengths, q2, h1, o1, lse1, w_rest, gains, mem, grad, ck_shard, cv_shard, co_shard, in_shard, w_out)
 
 
 def tail_kernel(peers, *refs):
-    (order, do1, stat1, q_far, k_far, v_far, bias_far, bias_back_far, tok, w_self, gains, dh1, buckets,
-     a1, o1, branch1, a2, dq2, mem, dk2, dv2, o2, branch2, g_in, g_out, small_mid) = refs[:26]
-    out, small_out, grad_tokens = refs[26:29]
+    (order, do1, stat1, q_far, k_far, v_far, bias_far, table_back, tok, w_self, gains, dh1, buckets,
+     a1, o1, branch1, a2, dq2, mem, dk2, dv2, o2, branch2, in_all, small_mid) = refs[:25]
+    out, small_out, grad_tokens = refs[25:28]
     (prod, ra, sb, rb, sc, rc, sd, rd, tiny, tiny_in, do_all, do_nat, stat_all, stat_rows, stat_t, q_own, k_own, v_own,
-     dq1, dk1, dv1, diagonals, q_nat, k_nat, v_nat, bias, bias_back, bucket_rows, inv, s_w, s_far, *sem) = refs[29:]
+     dq1, dk1, dv1, diagonals, q_nat, k_nat, v_nat, bias, bias_back, lines, bucket_rows, inv, s_w, s_far, *sem) = refs[28:]
     sem = [sem[2 * i : 2 * i + 2] for i in range(len(sem) // 2)]
-    s_do, s_st, sem_a, sem_b, sem_c, sem_d, sem_e, sem_f, sem_g, sem_t = sem
+    s_do, s_st, sem_a, sem_b, sem_c, sem_d, sem_e, sem_f, sem_t = sem
     wire = Wire(peers)
     at, depth, go = wire.at, wire.depth, wire.go
     rows, length = do1.shape[0], q_far.shape[0]
     mine, pieces = rows // PIECE, length // PIECE
     total, quarter, wide = out.shape
-    half_width, part = wide // 2, quarter // depth
     pairs = [(o2, branch2), (mem, dk2), (mem, dv2), (a2, dq2), (o1, branch1), (a1, dq1), (a1, dk1), (a1, dv1)]
     n_mats = len(pairs)
-    columns = lambda b: pl.ds(pl.multiple_of(b * half_width, LANES), half_width)
     shard_rows = lambda f: pl.ds(pl.multiple_of(f * quarter, quarter), quarter)
-    part_rows = lambda a: pl.ds(pl.multiple_of(a * part, part), part)
-    own_half, other_half = columns(at.b), columns(1 - at.b)
 
     def stage_a(i):
         left, right = pairs[i]
@@ -1356,58 +1437,14 @@
         sb[i] = (prod[i, shard_rows(x * 2 + at.k), :].astype(F32) + ra[i, x].astype(F32)).astype(BF16)
         go(remote(sb.at[i], rb.at[i], sem_b, i, at.across))
 
-    def source(j):
-        if j < n_mats + WAYS:
-            return sc.at[j]
-        q = j - n_mats - WAYS
-        return g_out.at[q * quarter : (q + 1) * quarter]
+    sums = Summed(wire, lambda j: sc.at[j] if j < n_mats else in_all.at[j - n_mats], out, rc, sd, rd, sem_c, sem_d, sem_e, sem_f)
 
     def stage_c(j):
         if j < n_mats:
             remote(sb.at[j], rb.at[j], sem_b, j, at.across).wait_recv()
             value = prod[j, shard_rows(at.f), :].astype(F32) + ra[j, at.x].astype(F32) + rb[j].astype(F32)
             sc[j] = value.astype(BF16)
-        go(remote(source(j).at[:, other_half], rc.at[j], sem_c, j, at.beside))
-
-    def stage_d(j):
-        remote(rc.at[j], rc.at[j], sem_c, j, at.beside).wait_recv()
-        value = source(j)[:, own_half].astype(F32) + rc[j].astype(F32)
-        sd[j] = value.astype(BF16)
-        for d in range(1, depth):
-            spot = rd.at[j, part_rows(at.a)]
-            go(remote(sd.at[j, part_rows(at.ahead(d))], spot, sem_d, j * depth + d, at.column(at.ahead(d))))
-
-    def stage_e(j):
-        value = sd[j, part_rows(at.a), :].astype(F32)
-        for d in range(1, depth):
-            spot = rd.at[j, part_rows(at.behind(d))]
-            remote(spot, spot, sem_d, j * depth + d, at.column(at.behind(d))).wait_recv()
-            value += spot[...].astype(F32)
-        spot = out.at[j, part_rows(at.a), own_half]
-        spot[...] = value.astype(BF16)
-        for d in range(1, depth):
-            go(remote(spot, spot, sem_e, j * depth + d, at.column(at.ahead(d))))
-
-    def stage_f(j):
-        for d in range(1, depth):
-            spot = out.at[j, part_rows(at.behind(d)), own_half]
-            remote(spot, spot, sem_e, j * depth + d, at.column(at.behind(d))).wait_recv()
-        go(remote(out.at[j, :, own_half], out.at[j, :, own_half], sem_f, j, at.beside))
-
-    def stage_g(j):
-        spot = out.at[j, :, other_half]
-        remote(spot, spot, sem_f, j, at.beside).wait_recv()
-
-    def send_g_in():
-        sc[n_mats + at.f] = g_in[shard_rows(at.f), :]
-        for d in range(1, WAYS):
-            f = lax.rem(at.f + d, WAYS)
-            go(remote(g_in.at[shard_rows(f)], sc.at[n_mats + at.f], sem_g, d, at.group(d)))
-
-    def have_g_in():
-        for d in range(1, WAYS):
-            spot = sc.at[n_mats + lax.rem(at.f + WAYS - d, WAYS)]
-            remote(spot, spot, sem_g, d, at.group(WAYS - d)).wait_recv()
+        sums.stage_c(j)
 
     hops = [at.core, at.across, at.beside]
 
@@ -1510,7 +1547,7 @@
     weights_here.start()
     coming = []
     for i, (src, dst) in enumerate(
-        ((q_far, q_nat), (k_far, k_nat), (v_far, v_nat), (bias_far, bias), (bias_back_far, bias_back))
+        ((q_far, q_nat), (k_far, k_nat), (v_far, v_nat), (bias_far, bias))
     ):
         coming.append(pltpu.make_async_copy(src, dst, s_far.at[i]))
         coming[-1].start()
@@ -1524,43 +1561,46 @@
     diagonals[...] = jnp.zeros_like(diagonals)
     bucket_rows[0:1, :] = pltpu.roll(buckets[...], 1, 1)
     bucket_rows[1:2, :] = pltpu.roll(buckets[...], 1 + PIECE, 1)
-    turns = [12, 13, 14, 15, 0, 1, 2, 3, 4, 8, 9, 10, 11, 5, 6, 7]
+    turns = [8, 9, 10, 11, 0, 1, 2, 3, 4, 5, 6, 7]
     lag = 1.5
     events = []
     for tick, j in enumerate(turns):
         if j < n_mats:
             events += [(tick - 2, 1, lambda j=j: stage_a(j)), (tick - 1, 2, lambda j=j: stage_b(j))]
-        for k, stage in enumerate((stage_c, stage_d, stage_e, stage_f, stage_g)):
+        for k, stage in enumerate((stage_c, sums.stage_d, sums.stage_e, sums.stage_f, sums.stage_g)):
             events.append((tick + k * lag, 3 + k, lambda j=j, stage=stage: stage(j)))
-    events += [(2.5, 0, send_g_in), (8.5, 0, have_g_in)]
-    events += [(0.5, 0, lambda: relay(1)), (1.5, 0, lambda: relay(2)), (1.6, 0, lambda: relay(3)), (3.5, 0, prepare)]
-    events += [(4.5 + i, 0, lambda i=i: attend_back(2 * i, 2 * i + 2)) for i in range(PAIRS // 2)]
-    events += [(8.6, 0, finish_tokens)]
-    events += [(9.5 + t, 0, lambda t=t: small_hop(t)) for t in range(4)] + [(14.5, 0, small_end)]
+    share = HEADS // 3
+    for i in range(3):
+        events.append((i + 0.3, 0, lambda i=i: own_bias(table_back, lines, own, bias_back, i * share, (i + 1) * share)))
+        events.append((0.5 * i + 0.2, 0, lambda i=i: relay(i + 1)))
+    events.append((2.4, 0, prepare))
+    events += [(2.6 + 0.5 * i, 0, lambda i=i: attend_back(i, i + 1)) for i in range(PAIRS)]
+    events.append((5.7, 0, finish_tokens))
+    events += [(6.6 + t, 0, lambda t=t: small_hop(t)) for t in range(4)] + [(11.5, 0, small_end)]
     for _, _, event in sorted(events, key=lambda e: (e[0], -e[1])):
         event()
     wire.drain()
 
 
-def tail(peers, order, do1, stat1, q_nat, k_nat, v_nat, bias, bias_back, tok, w_self, gains, dh1, buckets, *rest):
+def tail(peers, order, do1, stat1, q_nat, k_nat, v_nat, bias, table_back, tok, w_self, gains, dh1, buckets, *rest):
     rows, length = do1.shape[0], q_nat.shape[0]
     n, depth = 8, peers // 2
-    total = n + 2 * WAYS
+    total = n + WAYS
     quarter, half = D // WAYS, D // 2
     shard = lambda k, width=D: pltpu.VMEM((k, quarter, width), BF16)
     row = lambda: pltpu.VMEM((rows, D), BF16)
     tiny = lambda k: pltpu.VMEM((k, 8 + STAT, D), F32)
-    operands = (do1, stat1, q_nat, k_nat, v_nat, bias, bias_back, tok, w_self, gains, dh1, buckets) + rest
+    operands = (do1, stat1, q_nat, k_nat, v_nat, bias, table_back, tok, w_self, gains, dh1, buckets) + rest
     return pl.pallas_call(
         functools.partial(tail_kernel, peers),
         name="tail",
         out_shape=[sds((total, quarter, D), BF16), sds((8 + STAT, D), F32), sds((rows, D), BF16)],
         in_specs=[smem_spec()]
-        + [any_spec() if i in (2, 3, 4, 5, 6, 8) else full_spec() for i in range(len(operands))],
+        + [any_spec() if i in (2, 3, 4, 5, 8) else full_spec() for i in range(len(operands))],
         out_specs=[full_spec()] * 3,
         scratch_shapes=[
             pltpu.VMEM((n, D, D), BF16), pltpu.VMEM((n, 2, quarter, D), BF16), shard(n), shard(n),
-            shard(n + WAYS), shard(total, half), shard(total, half), shard(total, half),
+            shard(n), shard(total, half), shard(total, half), shard(total, half),
             tiny(4), tiny(3 + depth),
             pltpu.VMEM((length, D), BF16), pltpu.VMEM((length, D), BF16),
             pltpu.VMEM((peers, 2 * STAT, rows), F32), pltpu.VMEM((length, LANES), F32), pltpu.VMEM((LANES, length), F32),
@@ -1569,22 +1609,22 @@
         ]
         + [pltpu.VMEM((length, D), BF16)] * 3
         + [pltpu.VMEM((HEADS, rows, length), BF16)] * 2
-        + [pltpu.VMEM((2, 2 * length), jnp.int32), pltpu.SMEM(order.shape, jnp.int32)]
-        + [pltpu.SemaphoreType.DMA, pltpu.SemaphoreType.DMA((5,))]
+        + [pltpu.VMEM((2, 8, 2 * length), F32), pltpu.VMEM((2, 2 * length), jnp.int32), pltpu.SMEM(order.shape, jnp.int32)]
+        + [pltpu.SemaphoreType.DMA, pltpu.SemaphoreType.DMA((4,))]
         + line_sems(depth, CHUNKS) + line_sems(depth, 1)
-        + sems(2 * n) + sems(n) + sems(total) + sems(total * depth) + sems(total * depth) + sems(total) + sems(WAYS) + sems(3 + depth),
+        + sems(2 * n) + sems(n) + sems(total) + sems(total * depth) + sems(total * depth) + sems(total) + sems(3 + depth),
         compiler_params=pltpu.CompilerParams(collective_id=0, has_side_effects=True, vmem_limit_bytes=TAIL_VMEM),
     )(order, *operands)
 
 
-def widen_kernel(src, *refs):
+def widen_kernel(first, last, *refs):
     outs, sem = refs[:-2], refs[-1]
     wide = refs[-2]
     copies = []
-    count = src.shape[0]
-    quarter, width = src.shape[1], src.shape[2]
+    count = first.shape[0] + last.shape[0]
+    quarter, width = first.shape[1], first.shape[2]
     for j in range(count):
-        wide[j] = src[j].astype(F32)
+        wide[j] = (first[j] if j < count - WAYS else last[j - (count - WAYS)]).astype(F32)
         if j < count - 2 * WAYS:
             dst = outs[j]
         elif j < count - WAYS:
@@ -1599,18 +1639,19 @@
         copy.wait()
 
 
-def widen(total):
-    count, quarter, width = total.shape
+def widen(first, last):
+    quarter, width = first.shape[1:]
+    count = first.shape[0] + last.shape[0]
     each = [sds((quarter, width), F32)] * (count - 2 * WAYS)
     return pl.pallas_call(
         widen_kernel,
         name="widen",
         out_shape=each + [sds((quarter, WAYS * width), F32), sds((WAYS * quarter, width), F32)],
-        in_specs=[full_spec()],
+        in_specs=[full_spec()] * 2,
         out_specs=[any_spec()] * (len(each) + 2),
-        scratch_shapes=[pltpu.VMEM(total.shape, F32), pltpu.SemaphoreType.DMA((count,))],
+        scratch_shapes=[pltpu.VMEM((count, quarter, width), F32), pltpu.SemaphoreType.DMA((count,))],
         compiler_params=pltpu.CompilerParams(vmem_limit_bytes=VMEM_LIMIT),
-    )(total)
+    )(first, last)
 
 
 def shards(
@@ -1642,7 +1683,7 @@
     f = lax.axis_index("fsdp")
     quarter, eighth = self_query.shape[0], position_bias.shape[0]
     buckets = jnp.pad(bucket_table, (0, 1), constant_values=-1)[None]
-    w_self, w_rest, gains, ahead, behind, q1_nat, k1_nat, v1_nat, a1, o1, h1, a2, q2, lse1 = front(
+    w_self, w_rest, gains, ahead, table_back, q1_nat, k1_nat, v1_nat, a1, o1, h1, a2, q2, lse1 = front(
         peers,
         piece_order,
         tok,
@@ -1661,8 +1702,8 @@
         dh1,
         do1,
         stat1,
-        g_in,
-        g_out,
+        in_all,
+        out_sum,
         layer_output,
         grad_memory,
         small_mid,
@@ -1692,7 +1733,7 @@
         k1_nat,
         v1_nat,
         ahead,
-        behind,
+        table_back,
         tok,
         w_self,
         gains,
@@ -1708,11 +1749,10 @@
         dv2,
         o2,
         branch2,
-        g_in,
-        g_out,
+        in_all,
         small_mid,
     )
-    *each, sum_in, sum_out = widen(total)
+    *each, sum_in, sum_out = widen(total, out_sum)
     gain = lambda i: lax.dynamic_slice_in_dim(small[i], f * quarter, quarter)
     bias_out = lax.dynamic_slice_in_dim(small[8:, :BUCKETS].T, f * eighth, eighth)[:, :HEADS]
     return (

time: 373 us -> 338 us (0.906)
  Pallas kernels: 357 us -> 324 us
    pallas_call x1, Pallas kernels: 158 us -> 132 us  [tail(): pl.pallas_call(functools.partial(tail_kernel, peers), name='tail', out_sh...]
    pallas_call x1, Pallas kernels: 59.9 us -> 47.7 us  [front(): pl.pallas_call(functools.partial(front_kernel, peers), name='front', out_...]
    pallas_call x1, Pallas kernels: 133 us -> 138 us  [middle(): pl.pallas_call(functools.partial(middle_kernel, peers), name='middle', ou...]
where the time goes in v7:
time: 338 us; the launch traced here: 336 us
  Pallas kernels  324 us (96%)
  local copies, waits for them, and re-layouts  10.8 us (3%)
    pallas_call x1, Pallas kernels, middle(): pl.pallas_call(functools.partial(middle_kernel, peers), name='middle', ou...  138 us
    pallas_call x1, Pallas kernels, tail(): pl.pallas_call(functools.partial(tail_kernel, peers), name='tail', out_sh...  132 us
    pallas_call x1, Pallas kernels, front(): pl.pallas_call(functools.partial(front_kernel, peers), name='front', out_...  47.7 us

profile of v7, /device:TPU:0, one launch (start us, length us, event | category | flops | bytes accessed | tf_op | source)
XLA Modules:
  0.0 335.6 jit_solution(13747829642549848336)
XLA Ops:
  0.7 1.3 pad.4
  2.0 1.2 broadcast_in_dim.21.refs_2_
  3.2 1.2 broadcast_in_dim.22.refs_3_
  4.4 1.2 broadcast_in_dim.23.refs_4_
  5.6 47.7 %front.1 = (bf16[3,768,768]{2,1,0:T(8,128)(2,1)}, bf16[2,768,768]{2,1,0:T(8,128)(2,1)}, f32[8,768]{1,0:T(8,128)}, bf16[12,128,1024]{2,1,0:T(8,128)(2,1)}, f32[16...) custom-call(s32[16]{0:T(128)} %refs_0_.5, ...), custom_call_target="tpu_custom_call" | custom-call | tf_op jit(solution)/shard_map/front/pallas_call | solution.py:1006
  53.3 138.0 %middle.1 = (bf16[128,768]{1,0:T(8,128)(2,1)}, bf16[128,768]{1,0:T(8,128)(2,1)}, bf16[128,768]{1,0:T(8,128)(2,1)}, bf16[640,768]{1,0:T(8,128)(2,1)}, bf16[640,76...) custom-call(s32[1,20]{1,0:T(1,128)} %refs_0_.4, ...), custom_call_target="tpu_custom_call" | custom-call | tf_op jit(solution)/shard_map/middle/pallas_call | solution.py:1366
  191.3 131.9 %tail.1 = (bf16[12,192,768]{2,1,0:T(8,128)(2,1)}, f32[24,768]{1,0:T(8,128)}, bf16[128,768]{1,0:T(8,128)(2,1)}) custom-call(s32[16]{0:T(128)} %refs_0_.5, bf16[128,768]{1,0:T(8,128)(2,1)} %get-tuple-element.65.refs_1_, f32[32,128]{1,0:T(8,128)} %get-tuple-element.66.refs_2_, bf16[1024,768]{1,0:T(8,128)(2,1)} %get-tuple-element.67.refs_3_, ...), custom_call_target="tpu_custom_call" | custom-call | tf_op jit(solution)/shard_map/tail/pallas_call | solution.py:1594
  323.2 0.0 copy-start.1
  323.2 0.0 copy-start.2
  323.2 0.0 copy-start
  323.2 6.2 %widen.1 = (f32[192,768]{1,0:T(8,128)}, f32[192,768]{1,0:T(8,128)}, f32[192,768]{1,0:T(8,128)}, f32[192,768]{1,0:T(8,128)}, f32[192,768]{1,0:T(8,128)}, /*index=...) custom-call(bf16[12,192,768]{2,1,0:T(8,128)(2,1)} %get-tuple-element.87.f, ...), custom_call_target="tpu_custom_call" | custom-call | tf_op jit(solution)/shard_map/widen/pallas_call | solution.py:1646
  329.5 0.9 fusion
  330.3 0.6 constant_dynamic-slice_fusion
  331.0 0.7 slice.18
  331.7 0.1 dynamic-slice_bitcast_fusion
  331.7 0.7 copy.37
  332.4 0.6 constant_dynamic-slice_fusion.2
  333.1 0.0 copy-done.1
  333.1 0.7 copy.41
  333.7 0.0 copy-done.2
  333.7 0.7 copy.42
  334.4 0.0 copy-done
  334.4 0.9 copy.43
Async XLA Ops:
  323.2 9.9 %copy-start.1 = (bf16[128,768]{1,0:T(8,128)(2,1)S(1)}, bf16[128,768]{1,0:T(8,128)(2,1)}, u32[]{:S(2)}) copy-start(bf16[128,768]{1,0:T(8,128)(2,1)} %get-tuple-element.64) | copy-start | bytes 589828
  323.2 10.5 %copy-start.2 = (bf16[128,768]{1,0:T(8,128)(2,1)S(1)}, bf16[128,768]{1,0:T(8,128)(2,1)}, u32[]{:S(2)}) copy-start(bf16[128,768]{1,0:T(8,128)(2,1)} %get-tuple-element.84) | copy-start | bytes 589828
  323.2 11.2 %copy-start = (bf16[640,768]{1,0:T(8,128)(2,1)S(1)}, bf16[640,768]{1,0:T(8,128)(2,1)}, u32[]{:S(2)}) copy-start(bf16[640,768]{1,0:T(8,128)(2,1)} %get-tuple-element.85) | copy-start | bytes 2949124

commit v8 on v7

--- a/solution.py
+++ b/solution.py
@@ -875,10 +875,10 @@
 
 
 def front_kernel(peers, *refs):
-    order, tok, gain1, gain2, gain3, bias_shard, buckets = refs[:7]
-    shards_in = refs[7 : 7 + N_FRONT]
-    (w_self_out, w_rest_out, gains, ahead_out, table_out, q_out, k_out, v_out, a1, o1, h1, a2, q2, lse) = refs[7 + N_FRONT : 21 + N_FRONT]
-    (tok_all, pack, pack_all, marks, marks_all, table, lines, q_own, w_self, w_rest, ahead, q_nat, k_nat, v_nat, s_keep, inv, *sem) = refs[21 + N_FRONT :]
+    order, tok, gain_row, bias_shard, buckets = refs[:5]
+    shards_in = refs[5 : 5 + N_FRONT]
+    (w_self_out, w_rest_out, gains, ahead_out, table_out, q_out, k_out, v_out, a1, o1, h1, a2, q2, lse) = refs[5 + N_FRONT : 19 + N_FRONT]
+    (tok_all, pack, pack_all, marks, marks_all, table, lines, q_own, w_self, w_rest, ahead, q_nat, k_nat, v_nat, s_keep, inv, *sem) = refs[19 + N_FRONT :]
     weights = [w_self.at[i] for i in range(3)] + [w_rest.at[i] for i in range(N_FRONT - 3)]
     sem_t, sem_w, sem_p, sem_m = sem[0:2], sem[2:4], sem[4:6], sem[6:8]
     wire = Wire(peers)
@@ -893,12 +893,12 @@
         copy.start()
         kept.append(copy)
 
-    quarter = gain1.shape[1]
+    quarter = gain_row.shape[1] // 3
     spot = lax.broadcasted_iota(jnp.int32, (quarter, D), 0) + at.f * quarter
     place = jnp.where(lax.broadcasted_iota(jnp.int32, (quarter, D), 1) == spot, 1.0, 0.0).astype(BF16)
     pack[...] = jnp.zeros_like(pack)
-    for i, gain in enumerate((gain1, gain2, gain3)):
-        pack[i : i + 1, :] = nn(gain[...], place).astype(BF16)
+    for i in range(3):
+        pack[i : i + 1, :] = nn(gain_row[:, i * quarter : (i + 1) * quarter], place).astype(BF16)
     eighth, heads = bias_shard.shape
     spot = lax.broadcasted_iota(jnp.int32, (BUCKETS, eighth), 1) + at.f * eighth
     place = jnp.where(lax.broadcasted_iota(jnp.int32, (BUCKETS, eighth), 0) == spot, 1.0, 0.0).astype(BF16)
@@ -999,7 +999,7 @@
     wire.drain()
 
 
-def front(peers, order, tok, gain_shards, bias_shard, buckets, weight_shards):
+def front(peers, order, tok, gain_row, bias_shard, buckets, weight_shards):
     rows = tok.shape[0]
     length, depth = peers * rows, peers // 2
     block = lambda dtype: sds((rows, D), dtype)
@@ -1010,7 +1010,7 @@
         + [sds((HEADS, rows, length), BF16), sds((16, 2 * length), F32)]
         + [sds((length, D), BF16)] * 3
         + [block(BF16), block(BF16), block(F32), block(BF16), block(BF16), sds((rows, LANES), F32)],
-        in_specs=[smem_spec()] + [full_spec()] * (6 + N_FRONT),
+        in_specs=[smem_spec()] + [full_spec()] * (4 + N_FRONT),
         out_specs=[any_spec() if i in (0, 1, 3, 5, 6, 7) else full_spec() for i in range(14)],
         scratch_shapes=[
             pltpu.VMEM((length, D), BF16),
@@ -1029,7 +1029,7 @@
         + [pltpu.SemaphoreType.DMA((8,)), pltpu.SMEM(order.shape, jnp.int32)]
         + line_sems(depth, CHUNKS) + sems(3 * N_FRONT) + sems(WAYS) + sems(WAYS),
         compiler_params=pltpu.CompilerParams(collective_id=1, has_side_effects=True, vmem_limit_bytes=VMEM_LIMIT),
-    )(order, tok, *gain_shards, bias_shard, buckets, *weight_shards)
+    )(order, tok, gain_row, bias_shard, buckets, *weight_shards)
 
 
 STAT = 16
@@ -1207,9 +1207,9 @@
     h2 = h1[...] + nn(o2, w_co[...])
     a3 = normed(h2, gains[2:3, :]).astype(BF16)
     a3_all[block(at.f), :] = a3
-    for d in range(1, WAYS):
-        spot = a3_all.at[block(at.f)]
-        wire.go(remote(spot, spot, s_a3, d, at.group(d)))
+    spot = a3_all.at[block(at.f)]
+    wire.go(remote(spot, spot, s_a3, 0, at.across))
+    wire.go(remote(spot, spot, s_a3, 1, at.core))
 
     def arrive(buf, sem, size):
         for d in range(1, WAYS):
@@ -1222,7 +1222,8 @@
     for rs in tiles:
         dact[rs, :] = nt(g_all[rs, :], w_out[...])
     arrive(w_in, s_in, quarter)
-    arrive(a3_all, s_a3, rows)
+    wire.weight_relay(a3_all, s_a3, 0)
+    wire.weight_ready(a3_all, s_a3, 0)
     for rs in tiles:
         pre = nn(a3_all[rs, :], w_in[...])
         square = pre * pre
@@ -1245,7 +1246,14 @@
             value += dst[block(lax.rem(at.f + WAYS - d, WAYS)), :].astype(F32)
         return value
 
-    exchange(da3_send, da3_in, s_da3)
+    from_core, to_pass, from_across, passed = [slice(rows * i, rows * (i + 1)) for i in range(WAYS)]
+    beyond = (1 - at.x) * 2
+    wire.go(remote(da3_send.at[block(beyond + 1 - at.k)], da3_in.at[to_pass], s_da3, 1, at.core))
+    wire.go(remote(da3_send.at[block(at.x * 2 + 1 - at.k)], da3_in.at[from_core], s_da3, 0, at.core))
+    remote(da3_in.at[to_pass], da3_in.at[to_pass], s_da3, 1, at.core).wait_recv()
+    pair_sum = da3_send[block(beyond + at.k), :].astype(F32) + da3_in[to_pass, :].astype(F32)
+    da3_in[passed, :] = pair_sum.astype(BF16)
+    wire.go(remote(da3_in.at[passed], da3_in.at[from_across], s_da3, 2, at.across))
     sums = Summed(wire, lambda j: g_out.at[j * quarter : (j + 1) * quarter], out_sum, rc, sd, rd, *s_sum)
     g_out[...] = tn(act[...], g_all[...]).astype(BF16)
     for j in range(WAYS):
@@ -1254,7 +1262,9 @@
         out_send[rs, :] = nn(act[rs, :], w_out[...]).astype(BF16)
     sums.stage_d(0)
     sums.stage_d(1)
-    da3 = collect(da3_send, da3_in, s_da3)
+    remote(da3_in.at[from_core], da3_in.at[from_core], s_da3, 0, at.core).wait_recv()
+    remote(da3_in.at[from_across], da3_in.at[from_across], s_da3, 2, at.across).wait_recv()
+    da3 = da3_send[block(at.f), :].astype(F32) + da3_in[from_core, :].astype(F32) + da3_in[from_across, :].astype(F32)
     dx, dgain = norm_back_rows(h2, gains[2:3, :], da3)
     small[...] = jnp.zeros_like(small)
     small[1:2, :] = dgain
@@ -1617,10 +1627,13 @@
     )(order, *operands)
 
 
-def widen_kernel(first, last, *refs):
-    outs, sem = refs[:-2], refs[-1]
-    wide = refs[-2]
-    copies = []
+def widen_kernel(first, last, small, *refs):
+    ready, outs, gains_out, bias_out = refs[:3], refs[3:16], refs[16], refs[17]
+    wide, sem, sem_ready = refs[18:]
+    copies = [pltpu.make_async_copy(ready[i], outs[i], sem_ready.at[i]) for i in range(3)]
+    for copy in copies:
+        copy.start()
+    outs = outs[3:]
     count = first.shape[0] + last.shape[0]
     quarter, width = first.shape[1], first.shape[2]
     for j in range(count):
@@ -1635,23 +1648,39 @@
             dst = outs[-1].at[i * quarter : (i + 1) * quarter]
         copies.append(pltpu.make_async_copy(wide.at[j], dst, sem.at[j]))
         copies[-1].start()
+    f = lax.axis_index("fsdp")
+    turned = pltpu.roll(small[0:8, :], lax.rem(WAYS - f, WAYS) * quarter, 1)
+    gains_out[...] = turned[:, :quarter]
+    eighth = bias_out.shape[0]
+    sums = jnp.concatenate([small[8:, 0:LANES], jnp.zeros((LANES - STAT, LANES), F32)], 0)
+    flipped = sums.T
+    part = flipped[0:eighth, :]
+    for i in range(1, WAYS):
+        part = jnp.where(f == i, flipped[i * eighth : (i + 1) * eighth, :], part)
+    bias_out[...] = part[:, :HEADS]
     for copy in copies:
         copy.wait()
 
 
-def widen(first, last):
+def widen(first, last, small, ready):
     quarter, width = first.shape[1:]
     count = first.shape[0] + last.shape[0]
     each = [sds((quarter, width), F32)] * (count - 2 * WAYS)
+    big = [sds(x.shape, x.dtype) for x in ready] + each
+    big += [sds((quarter, WAYS * width), F32), sds((WAYS * quarter, width), F32)]
     return pl.pallas_call(
         widen_kernel,
         name="widen",
-        out_shape=each + [sds((quarter, WAYS * width), F32), sds((WAYS * quarter, width), F32)],
-        in_specs=[full_spec()] * 2,
-        out_specs=[any_spec()] * (len(each) + 2),
-        scratch_shapes=[pltpu.VMEM((count, quarter, width), F32), pltpu.SemaphoreType.DMA((count,))],
+        out_shape=big + [sds((8, quarter), F32), sds((BUCKETS // WAYS, HEADS), F32)],
+        in_specs=[full_spec()] * 6,
+        out_specs=[any_spec()] * len(big) + [full_spec()] * 2,
+        scratch_shapes=[
+            pltpu.VMEM((count, quarter, width), F32),
+            pltpu.SemaphoreType.DMA((count,)),
+            pltpu.SemaphoreType.DMA((3,)),
+        ],
         compiler_params=pltpu.CompilerParams(vmem_limit_bytes=VMEM_LIMIT),
-    )(first, last)
+    )(first, last, small, *ready)
 
 
 def shards(
@@ -1687,7 +1716,7 @@
         peers,
         piece_order,
         tok,
-        [self_gain[None], cross_gain[None], hidden_gain[None]],
+        jnp.concatenate([self_gain, cross_gain, hidden_gain])[None],
         position_bias,
         buckets,
         [self_query, self_attention_key, self_value, self_output, cross_query],
@@ -1752,18 +1781,24 @@
         in_all,
         small_mid,
     )
-    *each, sum_in, sum_out = widen(total, out_sum)
-    gain = lambda i: lax.dynamic_slice_in_dim(small[i], f * quarter, quarter)
-    bias_out = lax.dynamic_slice_in_dim(small[8:, :BUCKETS].T, f * eighth, eighth)[:, :HEADS]
+    ready = [layer_output, grad_tokens, grad_memory]
+    *ready, e0, e1, e2, e3, e4, e5, e6, e7, sum_in, sum_out, gains_out, bias_out = widen(total, out_sum, small, ready)
     return (
-        layer_output[None],
-        grad_tokens[None],
-        grad_memory[None],
-        gain(0),
-        gain(1),
-        gain(2),
+        ready[0][None],
+        ready[1][None],
+        ready[2][None],
+        gains_out[0],
+        gains_out[1],
+        gains_out[2],
         bias_out,
-        *[each[i] for i in (5, 6, 7, 4, 3, 1, 2, 0)],
+        e5,
+        e6,
+        e7,
+        e4,
+        e3,
+        e1,
+        e2,
+        e0,
         sum_in,
         sum_out,
     )

time: 338 us -> 329 us (0.973)
  local copies, waits for them, and re-layouts: 10.8 us -> 3.26 us
    pallas_call x1, Pallas kernels: 132 us -> 122 us  [tail(): pl.pallas_call(functools.partial(tail_kernel, peers), name='tail', out_sh...]
    pallas_call x1, Pallas kernels: 138 us -> 144 us  [middle(): pl.pallas_call(functools.partial(middle_kernel, peers), name='middle', ou...]
where the time goes in v8:
time: 329 us; the launch traced here: 326 us
  Pallas kernels  322 us (98%)
    pallas_call x1, Pallas kernels, middle(): pl.pallas_call(functools.partial(middle_kernel, peers), name='middle', ou...  144 us
    pallas_call x1, Pallas kernels, tail(): pl.pallas_call(functools.partial(tail_kernel, peers), name='tail', out_sh...  122 us
    pallas_call x1, Pallas kernels, front(): pl.pallas_call(functools.partial(front_kernel, peers), name='front', out_...  47.7 us
    pallas_call x1, Pallas kernels, widen(): pl.pallas_call(widen_kernel, name='widen', out_shape=big + [sds((8, quart...  7.5 us

profile of v8, /device:TPU:0, one launch (start us, length us, event | category | flops | bytes accessed | tf_op | source)
XLA Modules:
  0.0 326.5 jit_solution(432039009382505008)
XLA Ops:
  0.7 0.8 pad_maximum_fusion
  1.4 0.6 broadcast_in_dim.15.refs_2_
  2.0 1.3 pad.4
  3.3 47.7 %front.1 = (bf16[3,768,768]{2,1,0:T(8,128)(2,1)}, bf16[2,768,768]{2,1,0:T(8,128)(2,1)}, f32[8,768]{1,0:T(8,128)}, bf16[12,128,1024]{2,1,0:T(8,128)(2,1)}, f32[16...) custom-call(s32[16]{0:T(128)} %refs_0_.5, ...), custom_call_target="tpu_custom_call" | custom-call | tf_op jit(solution)/shard_map/front/pallas_call | solution.py:1006
  51.0 144.3 %middle.1 = (bf16[128,768]{1,0:T(8,128)(2,1)}, bf16[128,768]{1,0:T(8,128)(2,1)}, bf16[128,768]{1,0:T(8,128)(2,1)}, bf16[640,768]{1,0:T(8,128)(2,1)}, bf16[640,76...) custom-call(s32[1,20]{1,0:T(1,128)} %refs_0_.4, ...), custom_call_target="tpu_custom_call" | custom-call | tf_op jit(solution)/shard_map/middle/pallas_call | solution.py:1376
  195.3 122.0 %tail.1 = (bf16[12,192,768]{2,1,0:T(8,128)(2,1)}, f32[24,768]{1,0:T(8,128)}, bf16[128,768]{1,0:T(8,128)(2,1)}) custom-call(s32[16]{0:T(128)} %refs_0_.5, bf16[128,768]{1,0:T(8,128)(2,1)} %get-tuple-element.69.refs_1_, f32[32,128]{1,0:T(8,128)} %get-tuple-element.70.refs_2_, bf16[1024,768]{1,0:T(8,128)(2,1)} %get-tuple-element.71.refs_3_, ...), custom_call_target="tpu_custom_call" | custom-call | tf_op jit(solution)/shard_map/tail/pallas_call | solution.py:1604
  317.4 7.5 %widen.1 = (bf16[128,768]{1,0:T(8,128)(2,1)}, bf16[128,768]{1,0:T(8,128)(2,1)}, bf16[640,768]{1,0:T(8,128)(2,1)}, f32[192,768]{1,0:T(8,128)}, f32[192,768]{1,0:T...) custom-call(bf16[12,192,768]{2,1,0:T(8,128)(2,1)} %get-tuple-element, ...), custom_call_target="tpu_custom_call" | custom-call | tf_op jit(solution)/shard_map/widen/pallas_call | solution.py:1671
  324.9 1.4 fusion

commit v9 on v8

--- a/solution.py
+++ b/solution.py
@@ -1338,6 +1338,8 @@
     )
     dk2_out[...] = dk_acc[...].astype(BF16)
     dv2_out[...] = dv_acc[...].astype(BF16)
+    gmem_out[...] = (nt(dk2_out[...], w_ck[...]) + nt(dv2_out[...], w_cv[...])).astype(BF16)
+    finish_output()
     value = column_dq(at.a)
     for step in range(1, depth):
         a = wire.near(step)
@@ -1355,8 +1357,6 @@
     do1_out[...] = do1
     stat_own[1] = jnp.concatenate([lse1[...].T[:STAT], per_head_sums(do1.astype(F32) * o1[...].astype(F32), heads)], 0)
     stat1_out[...] = stat_own[1]
-    gmem_out[...] = (nt(dk2_out[...], w_ck[...]) + nt(dv2_out[...], w_cv[...])).astype(BF16)
-    finish_output()
     for d in range(1, WAYS):
         spot = in_all.at[lax.rem(at.f + WAYS - d, WAYS)]
         remote(spot, spot, s_gi, d, at.group(WAYS - d)).wait_recv()

time: 329 us -> 326 us (level)
  no operation moved by 1% of the time
where the time goes in v9:
time: 326 us; the launch traced here: 324 us
  Pallas kernels  319 us (98%)
    pallas_call x1, Pallas kernels, middle(): pl.pallas_call(functools.partial(middle_kernel, peers), name='middle', ou...  143 us
    pallas_call x1, Pallas kernels, tail(): pl.pallas_call(functools.partial(tail_kernel, peers), name='tail', out_sh...  121 us
    pallas_call x1, Pallas kernels, front(): pl.pallas_call(functools.partial(front_kernel, peers), name='front', out_...  47.7 us
    pallas_call x1, Pallas kernels, widen(): pl.pallas_call(widen_kernel, name='widen', out_shape=big + [sds((8, quart...  7.5 us

profile of v9, /device:TPU:0, one launch (start us, length us, event | category | flops | bytes accessed | tf_op | source)
XLA Modules:
  0.0 323.9 jit_solution(6478197385749831404)
XLA Ops:
  0.7 0.8 pad_maximum_fusion
  1.4 0.6 broadcast_in_dim.15.refs_2_
  2.0 1.3 pad.4
  3.3 47.7 %front.1 = (bf16[3,768,768]{2,1,0:T(8,128)(2,1)}, bf16[2,768,768]{2,1,0:T(8,128)(2,1)}, f32[8,768]{1,0:T(8,128)}, bf16[12,128,1024]{2,1,0:T(8,128)(2,1)}, f32[16...) custom-call(s32[16]{0:T(128)} %refs_0_.5, ...), custom_call_target="tpu_custom_call" | custom-call | tf_op jit(solution)/shard_map/front/pallas_call | solution.py:1006
  51.0 142.6 %middle.1 = (bf16[128,768]{1,0:T(8,128)(2,1)}, bf16[128,768]{1,0:T(8,128)(2,1)}, bf16[128,768]{1,0:T(8,128)(2,1)}, bf16[640,768]{1,0:T(8,128)(2,1)}, bf16[640,76...) custom-call(s32[1,20]{1,0:T(1,128)} %refs_0_.4, ...), custom_call_target="tpu_custom_call" | custom-call | tf_op jit(solution)/shard_map/middle/pallas_call | solution.py:1376
  193.6 121.2 %tail.1 = (bf16[12,192,768]{2,1,0:T(8,128)(2,1)}, f32[24,768]{1,0:T(8,128)}, bf16[128,768]{1,0:T(8,128)(2,1)}) custom-call(s32[16]{0:T(128)} %refs_0_.5, bf16[128,768]{1,0:T(8,128)(2,1)} %get-tuple-element.69.refs_1_, f32[32,128]{1,0:T(8,128)} %get-tuple-element.70.refs_2_, bf16[1024,768]{1,0:T(8,128)(2,1)} %get-tuple-element.71.refs_3_, ...), custom_call_target="tpu_custom_call" | custom-call | tf_op jit(solution)/shard_map/tail/pallas_call | solution.py:1604
  314.8 7.5 %widen.1 = (bf16[128,768]{1,0:T(8,128)(2,1)}, bf16[128,768]{1,0:T(8,128)(2,1)}, bf16[640,768]{1,0:T(8,128)(2,1)}, f32[192,768]{1,0:T(8,128)}, f32[192,768]{1,0:T...) custom-call(bf16[12,192,768]{2,1,0:T(8,128)(2,1)} %get-tuple-element, ...), custom_call_target="tpu_custom_call" | custom-call | tf_op jit(solution)/shard_map/widen/pallas_call | solution.py:1671
  322.3 1.4 fusion
